TPU v7x, 512 devices: a whole 4x4x16 slice. The times are simulated.
512 devices in a mesh: pool: 2 (over core), seq: 64 (over y, z), tp: 4 (over x).
Axes of the slice: x: 4, y: 4, z: 16, core: 2. Of those that a mesh axis runs over, the one named last changes fastest.
Arguments:
- tokens: bfloat16 [2048, 2560], P('seq'), may hold values from -6 to 6
- query_proj: bfloat16 [2048, 2048], P('seq', ('pool', 'tp')), may hold values from -36 to 36
- key_proj: bfloat16 [2048, 2048], P('seq', ('pool', 'tp')), may hold values from -6 to 6
- value_proj: bfloat16 [2048, 2048], P('seq', ('pool', 'tp')), may hold values from -12 to 12
- w_out: bfloat16 [2048, 2560], P(('pool', 'tp')), may hold values from -0.125 to 0.125
- modulation: float32 [4, 2560], replicated, may hold values from -3 to 3
- expert_ids: int32 [2048, 2], P('seq'), may hold values from 0 to 7, all different within a row; in each aligned block of 32 rows (0 to 31, 32 to 63, ...) at most 14 rows name the same one
- gate_values: float32 [2048, 2], P('seq'), may hold values from 0.1 to 0.9
- w_gate: bfloat16 [8, 2560, 6912], P(('pool', 'tp'), None, 'seq'), may hold values from -0.125 to 0.125
- w_up: bfloat16 [8, 2560, 6912], P(('pool', 'tp'), None, 'seq'), may hold values from -0.125 to 0.125
- w_down: bfloat16 [8, 6912, 2560], P(('pool', 'tp'), 'seq'), may hold values from -0.078125 to 0.078125
Outputs:
- block_out: bfloat16 [2048, 2560], P('seq', ('pool', 'tp'))
Inputs may be any that keep to these rules, and one draw needn't show every extreme that they name: `expert_ids`: among the 32 rows of one seq shard, each expert is named by at most 14 rows.
All inputs are finite; a program needn't handle non-finite values.
Results may differ from a plain program's by a relative error of at most 0.02.
Values may be sent and summed in bfloat16 or wider, within the bound.
No kernel may reach another device: no remote copies, remote signals or barrier semaphores. Data moves between devices by JAX's collectives and lax.ppermute only.
A program may use at most 128 MiB of HBM per device.

v0:
```python
import math

import jax
import jax.numpy as jnp
from jax import lax
from jax.sharding import PartitionSpec as P

HD = 128
EXPERTS = 8
CAP = 14


def route_tables(expert_ids, gate_values, capacity, expert_count):
    token_rows = expert_ids.shape[0]
    top_count = expert_ids.shape[1]
    expert_range = jnp.arange(expert_count, dtype=jnp.int32)
    onehot = (expert_ids.reshape(-1)[:, None] == expert_range[None, :]).astype(jnp.int32)
    earlier = jnp.cumsum(onehot, axis=0) - onehot
    slot_index = jnp.sum(earlier * onehot, axis=1).reshape(token_rows, top_count)
    named = expert_range[:, None, None] == expert_ids[None, :, :]
    placed = slot_index[:, :, None] == jnp.arange(capacity, dtype=jnp.int32)[None, None, :]
    picked = (named[:, :, :, None] & placed[None, :, :, :]).astype(jnp.float32)
    dispatch_all = jnp.sum(picked, axis=2)
    combine_all = jnp.sum(gate_values[None, :, :, None] * picked, axis=2)
    return (dispatch_all, combine_all)


def body(
    tokens,
    query_proj,
    key_proj,
    value_proj,
    w_out,
    modulation,
    expert_ids,
    gate_values,
    w_gate,
    w_up,
    w_down,
):
    token_rows = tokens.shape[0]
    model_width = tokens.shape[1]
    local_heads = query_proj.shape[1] // HD
    inv_root = 1.0 / math.sqrt(HD)
    query_heads = query_proj.reshape(token_rows, local_heads, HD)
    shard_rows = (
        lax.all_gather(key_proj, "seq", axis=0, tiled=True),
        lax.all_gather(value_proj, "seq", axis=0, tiled=True),
    )
    run_max = jnp.full((local_heads, token_rows), -1e30, jnp.float32)
    key_heads = shard_rows[0].reshape(-1, local_heads, HD)
    value_heads = shard_rows[1].reshape(-1, local_heads, HD)
    scores = (
        jnp.einsum("qhd,khd->hqk", query_heads, key_heads, preferred_element_type=jnp.float32)
        * inv_root
    )
    new_max = jnp.maximum(run_max, jnp.max(scores, axis=2))
    exp_weights = jnp.exp(scores - new_max[:, :, None])
    new_total = jnp.sum(exp_weights, axis=2)
    new_acc = jnp.einsum(
        "hqk,khd->hqd",
        exp_weights.astype(jnp.bfloat16),
        value_heads,
        preferred_element_type=jnp.float32,
    )
    heads_out = (
        (new_acc / new_total[:, :, None])
        .transpose(1, 0, 2)
        .reshape(token_rows, local_heads * HD)
        .astype(jnp.bfloat16)
    )
    partial_value = jnp.dot(heads_out, w_out, preferred_element_type=jnp.float32)
    group_size = lax.axis_size(("pool", "tp"))
    group_index = lax.axis_index(("pool", "tp"))
    share_cols = model_width // group_size
    modul_share = lax.dynamic_slice_in_dim(modulation, group_index * share_cols, share_cols, 1)
    attention = lax.psum(partial_value.astype(jnp.bfloat16), ("pool", "tp")).astype(jnp.float32)
    resid = tokens.astype(jnp.float32) + modulation[0] * attention
    row_mean = jnp.mean(resid, axis=1, keepdims=True)
    row_square = jnp.mean(resid * resid, axis=1, keepdims=True)
    inv_dev = lax.rsqrt(row_square - row_mean * row_mean + 1e-06)
    normed = ((resid - row_mean) * inv_dev * (1.0 + modulation[2]) + modulation[1]).astype(
        jnp.bfloat16
    )
    resid_share = lax.dynamic_slice_in_dim(resid, group_index * share_cols, share_cols, 1)
    dispatch_all, combine_all = route_tables(expert_ids, gate_values, CAP, EXPERTS)
    dispatch_mine = lax.dynamic_index_in_dim(dispatch_all, group_index, 0, keepdims=False)
    slot_buffer = jnp.einsum(
        "tc,td->cd", dispatch_mine.astype(jnp.bfloat16), normed, preferred_element_type=jnp.float32
    ).astype(jnp.bfloat16)
    gate_part = w_gate[0]
    up_part = w_up[0]
    down_part = w_down[0]
    shard_rows = lax.all_gather(slot_buffer, "seq", axis=0, tiled=True)
    gated = jnp.dot(shard_rows, gate_part, preferred_element_type=jnp.float32)
    upward = jnp.dot(shard_rows, up_part, preferred_element_type=jnp.float32)
    hidden = (jax.nn.silu(gated) * upward).astype(jnp.bfloat16)
    partial_out = jnp.dot(hidden, down_part, preferred_element_type=jnp.float32)
    seq_count = lax.axis_size("seq")
    returned = lax.all_to_all(
        partial_out.reshape(seq_count, CAP, model_width).astype(jnp.bfloat16),
        "seq",
        split_axis=0,
        concat_axis=0,
        tiled=True,
    ).astype(jnp.float32)
    slot_sums = jnp.sum(returned, axis=0)
    combine_mine = lax.dynamic_index_in_dim(combine_all, group_index, 0, keepdims=False)
    mixture_full = jnp.dot(
        combine_mine, slot_sums, precision=lax.Precision.HIGHEST, preferred_element_type=jnp.float32
    )
    mixture = lax.psum_scatter(
        mixture_full.astype(jnp.bfloat16), ("pool", "tp"), scatter_dimension=1, tiled=True
    ).astype(jnp.float32)
    return (resid_share + modul_share[3] * mixture).astype(jnp.bfloat16)


def solution(mesh):
    in_specs = (
        P("seq", None),
        P("seq", ("pool", "tp")),
        P("seq", ("pool", "tp")),
        P("seq", ("pool", "tp")),
        P(("pool", "tp"), None),
        P(),
        P("seq", None),
        P("seq", None),
        P(("pool", "tp"), None, "seq"),
        P(("pool", "tp"), None, "seq"),
        P(("pool", "tp"), "seq", None),
    )
    out_specs = P("seq", ("pool", "tp"))
    return jax.shard_map(body, mesh=mesh, in_specs=in_specs, out_specs=out_specs, check_vma=False)
```

profile of v0, /device:TPU:1, one launch (start us, length us, event | category | flops | bytes accessed | tf_op | source)
XLA Modules:
  0.0 818.7 jit_solution(15389397423890732041)
XLA Ops:
  6.5 0.7 all-gather.5.cloned.1.call-update
  7.3 0.0 all-gather.7.cloned.1.call-start
  7.3 0.7 all-gather.7.cloned.1.call-update
  8.0 0.0 all-reduce.2.cloned.1.call-start
  8.1 0.8 copy.66
  8.8 0.1 eq.54
  8.9 0.1 fusion.20
  9.0 0.1 reduce_window_sum.11
  9.1 0.2 select_reduce_fusion
  9.3 0.1 eq.58
  9.4 0.1 copy.67
  9.5 0.7 iota_compare_fusion.2
  10.2 0.7 fusion.18
  10.9 1.0 add_reduce_fusion
  11.9 133.2 %all-gather.5.cloned.1.call-done = bf16[2048,256]{1,0:T(8,128)(2,1)} async-done(((bf16[32,256]{1,0:T(8,128)(2,1)}), bf16[2048,256]{1,0:T(8,128)(2,1)}) %all-gather.5.cloned.1.call-update) | async-done | bytes 1048592 | tf_op jit(solution)/shard_map/all_gather | solution.py:47
  145.1 1.5 copy.60
  146.6 1.1 fusion.30
  147.7 0.2 fusion.9
  147.9 135.2 %all-gather.7.cloned.1.call-done = bf16[2048,256]{1,0:T(8,128)(2,1)} async-done(((bf16[32,256]{1,0:T(8,128)(2,1)}), bf16[2048,256]{1,0:T(8,128)(2,1)}) %all-gather.7.cloned.1.call-update) | async-done | bytes 1048592 | tf_op jit(solution)/shard_map/all_gather | solution.py:48
  283.1 1.5 copy.63
  284.6 0.5 fusion.4
  285.1 1.0 convolution_convert_fusion.2
  286.1 0.0 all-reduce.2.cloned.1.call-update
  286.1 0.0 all-gather.9.cloned.1.call-start
  286.2 79.3 %all-reduce.2.cloned.1.call-done = bf16[32,2560]{1,0:T(8,128)(2,1)} async-done(((bf16[32,2560]{1,0:T(8,128)(2,1)}), bf16[32,2560]{1,0:T(8,128)(2,1)}) %all-reduce.2.cloned.1.call-update) | async-done | bytes 163856 | tf_op jit(solution)/shard_map/psum | solution.py:77
  365.5 1.1 fusion.29
  366.6 0.9 fusion
  367.5 0.0 all-gather.9.cloned.1.call-update
  367.5 0.0 copy-start.2
  367.6 141.8 %all-gather.9.cloned.1.call-done = bf16[64,14,2560]{2,1,0:T(8,128)(2,1)} async-done(((bf16[1,14,2560]{2,1,0:T(8,128)(2,1)}), bf16[64,14,2560]{2,1,0:T(8,128)(2,1)}) %all-gather.9.cloned.1.call-update) | async-done | bytes 4587536 | tf_op jit(solution)/shard_map/all_gather | solution.py:94
  509.3 7.4 reshape.50
  516.7 4.0 fusion.7
  520.7 1.5 fusion.1
  522.3 0.2 copy.68
  522.5 0.1 dot_general.35
  522.6 1.3 convolution_convert_fusion
  523.9 4.9 copy.70
  528.8 9.5 %all-to-all-start = ((bf16[64,14,2560]{2,1,0:T(8,128)(2,1)}), bf16[64,14,2560]{2,1,0:T(8,128)(2,1)}, u32[]{:S(2)}, u32[]{:S(2)}) async-start(bf16[64,14,2560]{2,1,0:T(8,128)(2,1)} %copy.70), calls=%async_computation | async-start | bytes 10485760 | tf_op jit(solution)/shard_map/all_to_all | solution.py:100
  538.3 0.0 reduce-scatter.4.cloned.1.call-start
  538.3 221.7 %all-to-all-done = bf16[64,14,2560]{2,1,0:T(8,128)(2,1)} async-done(((bf16[64,14,2560]{2,1,0:T(8,128)(2,1)}), bf16[64,14,2560]{2,1,0:T(8,128)(2,1)}, u32[]{:S(2)}, u32[]{:S(2)}) %all-to-all-start) | async-done | bytes 4587552 | tf_op jit(solution)/shard_map/all_to_all | solution.py:100
  760.1 3.4 convert_reduce_fusion
  763.5 0.5 convolution_convert_fusion.1
  763.9 1.1 copy.73
  765.0 0.0 reduce-scatter.4.cloned.1.call-update
  765.0 0.8 dynamic-slice_reduce_fusion
  765.8 44.7 %reduce-scatter.4.cloned.1.call-done = bf16[320,32]{1,0:T(8,128)(2,1)} async-done(((bf16[2560,32]{1,0:T(8,128)(2,1)}), bf16[320,32]{1,0:T(8,128)(2,1)}) %reduce-scatter.4.cloned.1.call-update) | async-done | bytes 20496
  810.5 1.0 copy.74
  811.5 0.7 add_convert_fusion.2
  (17 shorter events, 0.1 us)
Async XLA Ops:
  6.5 278.6 %copy-start = (bf16[256,2560]{1,0:T(8,128)(2,1)S(1)}, bf16[256,2560]{1,0:T(8,128)(2,1)}, u32[]{:S(2)}) copy-start(bf16[256,2560]{1,0:T(8,128)(2,1)} %param.15) | copy-start | bytes 3932164
  6.5 138.6 %all-gather.5.cloned.1.call-start = ((), (), s32[]{:S(2)}) async-start(), calls=%async_computation.2 | async-start | bytes 1064960 | tf_op jit(solution)/shard_map/all_gather | solution.py:47
  7.3 275.9 %all-gather.7.cloned.1.call-start = ((), (), s32[]{:S(2)}) async-start(), calls=%async_computation.3 | async-start | bytes 1064960 | tf_op jit(solution)/shard_map/all_gather | solution.py:48
  8.0 357.5 %all-reduce.2.cloned.1.call-start = ((), (), s32[]{:S(2)}) async-start(), calls=%async_computation.4 | async-start | bytes 327680 | tf_op jit(solution)/shard_map/psum | solution.py:77
  11.9 353.6 %copy-start.4 = (bf16[32,2560]{1,0:T(8,128)(2,1)S(1)}, bf16[32,2560]{1,0:T(8,128)(2,1)}, u32[]{:S(2)}) copy-start(bf16[32,2560]{1,0:T(8,128)(2,1)} %param.11) | copy-start | bytes 491524
  286.1 223.2 %all-gather.9.cloned.1.call-start = ((), (), s32[]{:S(2)}) async-start(), calls=%async_computation.5 | async-start | bytes 5324800 | tf_op jit(solution)/shard_map/all_gather | solution.py:94
  367.5 149.2 %copy-start.2 = (bf16[1,2560,108]{1,2,0:T(8,128)(2,1)S(1)}, bf16[1,2560,108]{1,2,0:T(8,128)(2,1)}, u32[]{:S(2)}) copy-start(bf16[1,2560,108]{1,2,0:T(8,128)(2,1)} %param.19) | copy-start | bytes 1658884
  516.7 4.0 copy-start.1
  516.7 4.0 copy-start.5
  520.7 1.8 copy-start.3
  528.8 231.3 %all-to-all-start = ((bf16[64,14,2560]{2,1,0:T(8,128)(2,1)}), bf16[64,14,2560]{2,1,0:T(8,128)(2,1)}, u32[]{:S(2)}, u32[]{:S(2)}) async-start(bf16[64,14,2560]{2,1,0:T(8,128)(2,1)} %copy.70), calls=%async_computation | async-start | bytes 10485760 | tf_op jit(solution)/shard_map/all_to_all | solution.py:100
  538.3 272.2 %reduce-scatter.4.cloned.1.call-start = ((), (), s32[]{:S(2)}) async-start(), calls=%async_computation.6 | async-start | bytes 737280
Sparse Core Ops, SparseCore 0:
  10.3 134.7 all-gather.4
  148.1 135.0 all-gather.6
  286.3 79.1 all-reduce.1
  368.7 140.5 all-gather.8
  765.2 45.2 reduce-scatter.3
where the time goes:
time: 819 us
  waiting for transfers between devices  757 us (92%)
  local copies, waits for them, and re-layouts  19.4 us (2%)
  between operations  13.3 us (2%)
  matrix products  10.8 us (1%)
  starting transfers between devices  9.65 us (1%)
  other arithmetic  8.21 us (1%)
    all_to_all x1, waiting for transfers between devices, body(): lax.all_to_all(partial_out.reshape(seq_count, CAP, model_width).astype(jn...  222 us
    all_gather x1, waiting for transfers between devices, body(): shard_rows = lax.all_gather(slot_buffer, 'seq', axis=0, tiled=True)  142 us
    all_gather x1, waiting for transfers between devices, body(): lax.all_gather(value_proj, 'seq', axis=0, tiled=True)  135 us
    all_gather x1, waiting for transfers between devices, body(): lax.all_gather(key_proj, 'seq', axis=0, tiled=True)  133 us
    psum x1, waiting for transfers between devices, body(): lax.psum(partial_value.astype(jnp.bfloat16), ('pool', 'tp'))  79.3 us
    unnamed x6, waiting for transfers between devices  46.1 us
  transfers between devices with their start and end apart: 6, of which 6 were waited for; matrix products, arithmetic and copies ran while one was open for 1% of the time, Pallas kernels for 0%

commit v1 on v0

v1 whole, which is shorter than its diff:
```python
import math

import jax
import jax.numpy as jnp
from jax import lax
from jax.experimental import pallas as pl
from jax.experimental.pallas import tpu as pltpu
from jax.sharding import Mesh
from jax.sharding import PartitionSpec as P

HD = 128
Y = 4
Z = 16
TP = 4
GROUP = ("pool", "tp")
F32 = jnp.float32
BF16 = jnp.bfloat16


def spread(x, axis, count):
    copies = jnp.broadcast_to(x[None], (count,) + x.shape)
    return lax.all_to_all(copies, axis, split_axis=0, concat_axis=0, tiled=True)


def exchange(x, axis):
    return lax.all_to_all(x, axis, split_axis=0, concat_axis=0, tiled=True)


def ffn_kernel(x_ref, c_ref, g0, u0, d0, g1, u1, d1, o_ref, acc_ref):
    step = pl.program_id(0)
    share = x_ref.shape[2]
    half = share // 2
    width = share * TP

    @pl.when(step == 0)
    def _():
        acc_ref[...] = jnp.zeros_like(acc_ref)

    total = acc_ref[...]
    for e, (g, u, d) in enumerate(((g0, u0, d0), (g1, u1, d1))):
        gate = jnp.zeros((x_ref.shape[1], g.shape[2]), F32)
        up = gate
        for t in range(TP):
            lo = slice(t * half, (t + 1) * half)
            hi = slice(width // 2 + t * half, width // 2 + (t + 1) * half)
            x = x_ref[t]
            gate += jnp.dot(
                x, jnp.concatenate([g[0, lo], g[0, hi]], 0), preferred_element_type=F32
            )
            up += jnp.dot(x, jnp.concatenate([u[0, lo], u[0, hi]], 0), preferred_element_type=F32)
        act = (gate / (1.0 + jnp.exp(-gate)) * up).astype(BF16)
        total += c_ref[:, e : e + 1] * jnp.dot(act, d[0], preferred_element_type=F32)
    acc_ref[...] = total

    @pl.when(step == Y - 1)
    def _():
        for t in range(TP):
            lo = acc_ref[:, t * half : (t + 1) * half]
            hi = acc_ref[:, width // 2 + t * half : width // 2 + (t + 1) * half]
            o_ref[t] = jnp.concatenate([lo, hi], 1).astype(BF16)


def ffn(x, weights, mine, other):
    tp, rows, share = x.shape
    width = tp * share
    hidden = mine[0].shape[2]
    wide = pl.BlockSpec((1, width, hidden), lambda i: (i, 0, 0))
    tall = pl.BlockSpec((1, hidden, width), lambda i: (i, 0, 0))
    return pl.pallas_call(
        ffn_kernel,
        grid=(Y,),
        out_shape=jax.ShapeDtypeStruct((tp, rows, share), BF16),
        in_specs=[
            pl.BlockSpec((tp, rows, share), lambda i: (0, 0, 0)),
            pl.BlockSpec(weights.shape, lambda i: (0, 0)),
            wide,
            wide,
            tall,
            wide,
            wide,
            tall,
        ],
        out_specs=pl.BlockSpec((tp, rows, share), lambda i: (0, 0, 0)),
        scratch_shapes=[pltpu.VMEM((rows, width), F32)],
        compiler_params=pltpu.CompilerParams(vmem_limit_bytes=48 << 20),
        cost_estimate=pl.CostEstimate(
            flops=12 * rows * width * hidden * Y,
            bytes_accessed=12 * width * hidden * Y,
            transcendentals=0,
        ),
    )(x, weights, *mine, *other)


def body(
    tokens,
    query_proj,
    key_proj,
    value_proj,
    w_out,
    modulation,
    expert_ids,
    gate_values,
    w_gate,
    w_up,
    w_down,
):
    rows, width = tokens.shape
    heads = query_proj.shape[1] // HD
    half_rows = rows // 2
    share = width // TP
    pool = lax.axis_index("pool")
    tp = lax.axis_index("tp")

    mine = [lax.all_gather(w[0], "y", axis=0) for w in (w_gate, w_up, w_down)]
    other = [lax.ppermute(w, "pool", [(0, 1), (1, 0)]) for w in mine]

    key_value = lax.all_gather(
        jnp.concatenate([key_proj, value_proj], 1), "z", axis=0, tiled=True
    )
    queries = spread(query_proj, "y", Y).reshape(Y * rows, heads * HD)
    parts = []
    stats = []
    for h in range(heads):
        cols = slice(h * HD, (h + 1) * HD)
        keys = key_value[:, cols]
        values = key_value[:, heads * HD + h * HD : heads * HD + (h + 1) * HD]
        scores = lax.dot_general(
            queries[:, cols], keys, (((1,), (1,)), ((), ())), preferred_element_type=F32
        ) * (1.0 / math.sqrt(HD))
        top = jnp.max(scores, axis=1, keepdims=True)
        weights = jnp.exp(scores - top)
        stats += [top, jnp.sum(weights, axis=1, keepdims=True)]
        parts.append(jnp.dot(weights.astype(BF16), values, preferred_element_type=F32))
    stats = jnp.concatenate(stats, 1)
    stats = jnp.pad(stats, ((0, 0), (0, HD - stats.shape[1])))
    packed = jnp.concatenate(parts + [stats], 1).reshape(Y, rows, (heads + 1) * HD)
    packed = exchange(packed, "y")
    outs = []
    for h in range(heads):
        acc = packed[:, :, h * HD : (h + 1) * HD]
        top = packed[:, :, heads * HD + 2 * h : heads * HD + 2 * h + 1]
        part_total = packed[:, :, heads * HD + 2 * h + 1 : heads * HD + 2 * h + 2]
        scale = jnp.exp(top - jnp.max(top, axis=0, keepdims=True))
        outs.append(jnp.sum(scale * acc, axis=0) / jnp.sum(scale * part_total, axis=0))
    heads_out = jnp.concatenate(outs, 1).astype(BF16)

    projected = jnp.dot(heads_out, w_out, preferred_element_type=F32).astype(BF16)
    projected = projected.reshape(2, half_rows, 2, TP, share // 2).transpose(0, 3, 1, 2, 4)
    projected = exchange(projected.reshape(2 * TP, half_rows, share), GROUP)
    attention = jnp.sum(projected.astype(F32), axis=0).astype(BF16)
    attention = spread(attention, "tp", TP)
    attention = (
        attention.reshape(TP, half_rows, 2, share // 2)
        .transpose(1, 2, 0, 3)
        .reshape(half_rows, width)
        .astype(F32)
    )
    half_tokens = lax.dynamic_slice_in_dim(tokens, pool * half_rows, half_rows, 0).astype(F32)
    resid = half_tokens + modulation[0] * attention
    row_mean = jnp.mean(resid, axis=1, keepdims=True)
    row_square = jnp.mean(resid * resid, axis=1, keepdims=True)
    inv_dev = lax.rsqrt(row_square - row_mean * row_mean + 1e-06)
    normed = ((resid - row_mean) * inv_dev * (1.0 + modulation[2]) + modulation[1]).astype(BF16)

    def my_share(a):
        a = a.reshape(a.shape[0], 2, TP, share // 2)
        return lax.dynamic_index_in_dim(a, tp, 2, keepdims=False).reshape(a.shape[0], share)

    normed_share = my_share(normed)
    resid_share = my_share(resid)
    modul_share = my_share(modulation[3:4])

    half_ids = lax.dynamic_slice_in_dim(expert_ids, pool * half_rows, half_rows, 0)
    half_gates = lax.dynamic_slice_in_dim(gate_values, pool * half_rows, half_rows, 0)
    gates_hi = lax.reduce_precision(half_gates, 8, 7)
    gates_lo = half_gates - gates_hi
    route = jnp.concatenate(
        [half_ids.astype(BF16), gates_hi.astype(BF16), gates_lo.astype(BF16)], 1
    )
    route = jnp.pad(route, ((0, 0), (0, HD - route.shape[1])))
    sent = jnp.concatenate([normed_share, route], 1)
    ring = spread(sent, "z", Z).reshape(Z * half_rows, share + HD)
    rows_in = spread(ring[:, :share], "tp", TP)
    route = ring[:, share : share + 6].astype(F32)
    gates = route[:, 2:4] + route[:, 4:6]
    mine_id = (pool * TP + tp).astype(F32)
    other_id = ((1 - pool) * TP + tp).astype(F32)
    gate_of = [
        jnp.sum(jnp.where(route[:, :2] == e, gates, 0.0), axis=1, keepdims=True)
        for e in (mine_id, other_id)
    ]
    gate_of = jnp.concatenate(gate_of, 1)

    mixed = ffn(rows_in, gate_of, mine, other)
    mixed = jnp.sum(exchange(mixed, "tp").astype(F32), axis=0).astype(BF16)
    mixed = mixed.reshape(Z, half_rows, 2, share // 2).transpose(2, 0, 1, 3)
    mixed = exchange(mixed.reshape(2 * Z, half_rows, share // 2), ("pool", "z"))
    mixture = jnp.sum(mixed.reshape(2, Z, half_rows, share // 2).astype(F32), axis=1)
    mixture = mixture.reshape(rows, share // 2)

    resid_halves = resid_share.reshape(half_rows, 2, share // 2)
    give = lax.dynamic_index_in_dim(resid_halves, 1 - pool, 1, keepdims=False)
    keep = lax.dynamic_index_in_dim(resid_halves, pool, 1, keepdims=False)
    got = lax.ppermute(give, "pool", [(0, 1), (1, 0)])
    resid_out = jnp.where(
        pool == 0, jnp.concatenate([keep, got], 0), jnp.concatenate([got, keep], 0)
    )
    modul_out = lax.dynamic_index_in_dim(
        modul_share.reshape(2, share // 2), pool, 0, keepdims=False
    )
    return (resid_out + modul_out * mixture).astype(BF16)


def solution(mesh):
    split = Mesh(
        mesh.devices.reshape(2, Y, Z, TP), ("pool", "y", "z", "tp")
    )
    seq = ("y", "z")
    in_specs = (
        P(seq, None),
        P(seq, GROUP),
        P(seq, GROUP),
        P(seq, GROUP),
        P(GROUP, None),
        P(),
        P(seq, None),
        P(seq, None),
        P(GROUP, None, seq),
        P(GROUP, None, seq),
        P(GROUP, seq, None),
    )
    return jax.shard_map(
        body, mesh=split, in_specs=in_specs, out_specs=P(seq, GROUP), check_vma=False
    )
```

time: 819 us -> 263 us (0.32)
  waiting for transfers between devices: 757 us -> 69.4 us
  blocking collectives: 0 us -> 53.9 us
  starting transfers between devices: 9.65 us -> 59.7 us
  local copies, waits for them, and re-layouts: 19.4 us -> 47.8 us
  Pallas kernels: 0 us -> 12.2 us
  matrix products: 10.8 us -> 1.26 us
    all_gather x3, waiting for transfers between devices: 410 us -> 28 us  [body(): mine = [lax.all_gather(w[0], 'y', axis=0) for w in (w_gate, w_up, w_down)]]
    all_to_all x1 -> x7, waiting for transfers between devices: 222 us -> 39.3 us  [the longest x3 34.7 us: exchange(): return lax.all_to_all(x, axis, split_axis=0, concat_axis=0, tiled=True)]
    psum x1 -> x0, waiting for transfers between devices: 79.3 us -> none  [body(): lax.psum(partial_value.astype(jnp.bfloat16), ('pool', 'tp'))]
    unnamed x6 -> x3, waiting for transfers between devices: 46.1 us -> 2.12 us
    all_to_all x1 -> x7, starting transfers between devices: 9.49 us -> 49.4 us  [the longest x3 30.7 us: exchange(): return lax.all_to_all(x, axis, split_axis=0, concat_axis=0, tiled=True)]
    all_gather x0 -> x1, blocking collectives: none -> 32.9 us  [body(): lax.all_gather(jnp.concatenate([key_proj, value_proj], 1), 'z', axis=0, t...]
    all_to_all x0 -> x1, blocking collectives: none -> 21 us  [exchange(): return lax.all_to_all(x, axis, split_axis=0, concat_axis=0, tiled=True)]
    all_gather x2 -> x5, local copies, waits for them, and re-layouts: 2.96 us -> 23 us  [body(): mine = [lax.all_gather(w[0], 'y', axis=0) for w in (w_gate, w_up, w_down)]]
  transfers between devices with their start and end apart: 6 -> 14, of which waited for: 6 -> 5; matrix products, arithmetic and copies ran while one was open for 1% -> 19% of each run, Pallas kernels for 0% -> 0%
where the time goes in v1:
time: 263 us; the launch traced here: 261 us
  waiting for transfers between devices  69.4 us (26%)
  starting transfers between devices  59.7 us (23%)
  blocking collectives  53.9 us (20%)
  local copies, waits for them, and re-layouts  47.8 us (18%)
  between operations  13.4 us (5%)
  Pallas kernels  12.2 us (5%)
  other arithmetic  3.44 us (1%)
    all_to_all x3, waiting for transfers between devices, exchange(): return lax.all_to_all(x, axis, split_axis=0, concat_axis=0, tiled=True)  34.7 us
    all_gather x1, blocking collectives, body(): lax.all_gather(jnp.concatenate([key_proj, value_proj], 1), 'z', axis=0, t...  32.9 us
    all_to_all x3, starting transfers between devices, exchange(): return lax.all_to_all(x, axis, split_axis=0, concat_axis=0, tiled=True)  30.7 us
    all_gather x3, waiting for transfers between devices, body(): mine = [lax.all_gather(w[0], 'y', axis=0) for w in (w_gate, w_up, w_down)]  28 us
    all_gather x5, local copies, waits for them, and re-layouts, body(): mine = [lax.all_gather(w[0], 'y', axis=0) for w in (w_gate, w_up, w_down)]  23 us
    all_to_all x1, blocking collectives, exchange(): return lax.all_to_all(x, axis, split_axis=0, concat_axis=0, tiled=True)  21 us
    all_to_all x4, starting transfers between devices, spread(): return lax.all_to_all(copies, axis, split_axis=0, concat_axis=0, tiled=True)  18.6 us
    ppermute x3, local copies, waits for them, and re-layouts, body(): other = [lax.ppermute(w, 'pool', [(0, 1), (1, 0)]) for w in mine]  14.3 us
  transfers between devices with their start and end apart: 14, of which 5 were waited for; matrix products, arithmetic and copies ran while one was open for 19% of the time, Pallas kernels for 0%

profile of v1, /device:TPU:1, one launch (start us, length us, event | category | flops | bytes accessed | tf_op | source)
XLA Modules:
  0.0 261.2 jit_solution(17475086921226323995)
XLA Ops:
  6.5 0.7 all-gather.4.cloned.1.call-update
  7.3 0.7 all-gather.6.cloned.1.call-update
  8.0 1.3 broadcast_in_dim.24
  9.4 5.0 %all-to-all-start = ((bf16[4,32,256]{2,1,0:T(8,128)(2,1)}), bf16[4,32,256]{2,1,0:T(8,128)(2,1)S(1)}, u32[]{:S(2)}, u32[]{:S(2)}) async-start(bf16[4,32,256]{2,1,0:T(8,128)(2,1)} %broadcast_in_dim.24), calls=%async_computation | async-start | bytes 131072 | tf_op jit(solution)/shard_map/all_to_all | solution.py:22
  14.4 0.7 all-gather.8.cloned.1.call-update
  15.1 0.7 pad_maximum_fusion.1
  15.8 32.9 %all_gather.12 = bf16[512,512]{1,0:T(8,128)(2,1)S(1)} all-gather(bf16[32,512]{1,0:T(8,128)(2,1)S(1)} %pad_maximum_fusion.1), channel_id=1, replica_groups=mesh['pool'=2,'y'=4,'z'=16,'tp'=4] {'z'}, dimensions={0}, use_global_device_ids=true | all-gather | bytes 557056 | tf_op jit(solution)/shard_map/all_gather | solution.py:117
  48.9 0.2 fusion.36
  49.2 0.2 fusion.4
  49.8 0.2 fusion.6
  50.1 0.8 copy.39
  50.9 4.2 %all-to-all-start.1 = ((f32[4,32,384]{2,1,0:T(8,128)}), f32[4,32,384]{2,1,0:T(8,128)S(1)}, u32[]{:S(2)}, u32[]{:S(2)}) async-start(f32[4,32,384]{2,1,0:T(8,128)} %bitcast.5), calls=%async_computation.1 | async-start | bytes 393216 | tf_op jit(solution)/shard_map/all_to_all | solution.py:26
  55.1 5.2 %all-to-all-done.1 = f32[4,32,384]{2,1,0:T(8,128)S(1)} async-done(((f32[4,32,384]{2,1,0:T(8,128)}), f32[4,32,384]{2,1,0:T(8,128)S(1)}, u32[]{:S(2)}, u32[]{:S(2)}) %all-to-all-start.1) | async-done | bytes 196640 | tf_op jit(solution)/shard_map/all_to_all | solution.py:26
  60.5 0.3 fusion.16
  61.0 0.3 convolution_convert_fusion
  61.7 0.8 reshape.94
  62.5 12.4 %all-to-all-start.2 = ((bf16[8,16,640]{2,1,0:T(8,128)(2,1)}), bf16[8,16,640]{2,1,0:T(8,128)(2,1)S(1)}, u32[]{:S(2)}, u32[]{:S(2)}) async-start(bf16[8,16,640]{2,1,0:T(8,128)(2,1)} %reshape.94), calls=%async_computation.2 | async-start | bytes 327680 | tf_op jit(solution)/shard_map/all_to_all | solution.py:26
  75.2 5.6 %all-to-all-done.2 = bf16[8,16,640]{2,1,0:T(8,128)(2,1)S(1)} async-done(((bf16[8,16,640]{2,1,0:T(8,128)(2,1)}), bf16[8,16,640]{2,1,0:T(8,128)(2,1)S(1)}, u32[]{:S(2)}, u32[]{:S(2)}) %all-to-all-start.2) | async-done | bytes 163872 | tf_op jit(solution)/shard_map/all_to_all | solution.py:26
  80.8 0.6 broadcast_in_dim.58
  81.5 3.3 %all-to-all-start.3 = ((bf16[4,16,640]{2,1,0:T(8,128)(2,1)}), bf16[4,16,640]{2,1,0:T(8,128)(2,1)S(1)}, u32[]{:S(2)}, u32[]{:S(2)}) async-start(bf16[4,16,640]{2,1,0:T(8,128)(2,1)} %broadcast_in_dim.58), calls=%async_computation.3 | async-start | bytes 163840 | tf_op jit(solution)/shard_map/all_to_all | solution.py:22
  84.9 4.6 %all-to-all-done.3 = bf16[4,16,640]{2,1,0:T(8,128)(2,1)S(1)} async-done(((bf16[4,16,640]{2,1,0:T(8,128)(2,1)}), bf16[4,16,640]{2,1,0:T(8,128)(2,1)S(1)}, u32[]{:S(2)}, u32[]{:S(2)}) %all-to-all-start.3) | async-done | bytes 81952 | tf_op jit(solution)/shard_map/all_to_all | solution.py:22
  90.7 0.8 broadcast_in_dim.59
  91.5 6.4 %all-to-all-start.4 = ((bf16[16,16,768]{2,1,0:T(8,128)(2,1)}), bf16[16,16,768]{2,1,0:T(8,128)(2,1)S(1)}, u32[]{:S(2)}, u32[]{:S(2)}) async-start(bf16[16,16,768]{2,1,0:T(8,128)(2,1)} %broadcast_in_dim.59), calls=%async_computation.4 | async-start | bytes 786432 | tf_op jit(solution)/shard_map/all_to_all | solution.py:22
  97.9 4.8 %copy.45 = bf16[4,2560,108]{1,0,2:T(4,128)(2,1)} copy(bf16[4,2560,108]{1,2,0:T(8,128)(2,1)} %all-gather.4.cloned.1.call-done) | data formatting | bytes 4423680 | tf_op jit(solution)/shard_map/all_gather | solution.py:114
  102.6 3.6 %collective-permute-start.1 = (bf16[4,2560,108]{1,0,2:T(4,128)(2,1)}, bf16[4,2560,108]{1,0,2:T(4,128)(2,1)}, u32[]{:S(2)}, u32[]{:S(2)}) collective-permute-start(bf16[4,2560,108]{1,0,2:T(4,128)(2,1)} %copy.45), channel_id=1, source_target_pairs={{0,256},{256,0},{1,257},{257,1},{2,258},{258,2},{3,259},{259,3},{4... | collective-permute-start | bytes 6635528 | tf_op jit(solution)/shard_map/ppermute | solution.py:115
  106.3 4.7 %copy.46 = bf16[4,2560,108]{1,0,2:T(4,128)(2,1)} copy(bf16[4,2560,108]{1,2,0:T(8,128)(2,1)} %all-gather.6.cloned.1.call-done) | data formatting | bytes 4423680 | tf_op jit(solution)/shard_map/all_gather | solution.py:114
  111.0 1.9 collective-permute-start.2
  112.9 27.9 %all-gather.8.cloned.1.call-done.d0 = bf16[4,108,2560]{2,1,0:T(8,128)(2,1)} async-done(((bf16[1,108,2560]{2,1,0:T(8,128)(2,1)}), bf16[4,108,2560]{2,1,0:T(8,128)(2,1)}) %all-gather.8.cloned.1.call-update) | async-done | bytes 2211856 | tf_op jit(solution)/shard_map/all_gather | solution.py:114
  140.9 4.7 %copy.47 = bf16[4,108,2560]{2,0,1:T(4,128)(2,1)} copy(bf16[4,108,2560]{2,1,0:T(8,128)(2,1)} %all-gather.8.cloned.1.call-done.d0) | data formatting | bytes 4423680 | tf_op jit(solution)/shard_map/all_gather | solution.py:114
  145.6 2.6 collective-permute-start.3
  148.2 1.2 broadcast_in_dim.60
  149.4 4.0 %all-to-all-start.5 = ((bf16[4,256,640]{2,1,0:T(8,128)(2,1)}), bf16[4,256,640]{2,1,0:T(8,128)(2,1)S(1)}, u32[]{:S(2)}, u32[]{:S(2)}) async-start(bf16[4,256,640]{2,1,0:T(8,128)(2,1)} %broadcast_in_dim.60), calls=%async_computation.5 | async-start | bytes 2621440 | tf_op jit(solution)/shard_map/all_to_all | solution.py:22
  153.4 0.3 select_reduce_fusion.1
  153.8 4.4 %copy.50.u0 = bf16[4,2560,108]{2,1,0:T(8,128)(2,1)} copy(bf16[4,2560,108]{1,2,0:T(8,128)(2,1)} %all-gather.6.cloned.1.call-done) | data formatting | bytes 4423680 | tf_op jit(solution)/shard_map/all_gather | solution.py:114
  158.2 4.4 %copy.49.g0 = bf16[4,2560,108]{2,1,0:T(8,128)(2,1)} copy(bf16[4,2560,108]{1,2,0:T(8,128)(2,1)} %all-gather.4.cloned.1.call-done) | data formatting | bytes 4423680 | tf_op jit(solution)/shard_map/all_gather | solution.py:114
  162.6 5.4 %copy.51.g1 = bf16[4,2560,108]{2,1,0:T(8,128)(2,1)} copy(bf16[4,2560,108]{1,0,2:T(4,128)(2,1)} %collective-permute-done.1) | data formatting | bytes 4423680 | tf_op jit(solution)/shard_map/ppermute | solution.py:115
  168.1 5.5 %copy.52.u1 = bf16[4,2560,108]{2,1,0:T(8,128)(2,1)} copy(bf16[4,2560,108]{1,0,2:T(4,128)(2,1)} %collective-permute-done.2) | data formatting | bytes 4423680 | tf_op jit(solution)/shard_map/ppermute | solution.py:115
  173.5 3.4 %copy.53.d1 = bf16[4,108,2560]{2,1,0:T(8,128)(2,1)} copy(bf16[4,108,2560]{2,0,1:T(4,128)(2,1)} %collective-permute-done.3) | data formatting | bytes 4423680 | tf_op jit(solution)/shard_map/ppermute | solution.py:115
  176.9 1.6 copy-done.1
  178.6 12.2 %shard_map.109 = bf16[4,256,640]{2,1,0:T(8,128)(2,1)S(1)} custom-call(bf16[4,256,640]{2,1,0:T(8,128)(2,1)S(1)} %all-to-all-done.5.x_ref, f32[256,2]{1,0:T(8,128)S(1)} %copy.48.c_ref, bf16[4,2560,108]{2,1,0:T(8,128)(2,1)} %copy.49.g0, bf16[4,2560,108]{2,1,0:T(8,128)(2,1)} %copy.50.u0, bf16[4,108,2560]{2,1,0:T(8,128)(2,1)S(1)} %copy-done.1, ...), custom_call_target="tpu_custom_call" | custom-call | flops 3397386240 | bytes 13271040 | tf_op jit(solution)/shard_map/pallas_call | solution.py:69
  190.8 21.0 %all_to_all.40 = bf16[4,256,640]{2,1,0:T(8,128)(2,1)S(1)} all-to-all(bf16[4,256,640]{2,1,0:T(8,128)(2,1)S(1)} %shard_map.109), channel_id=1, replica_groups=mesh['pool'=2,'y'=4,'z'=16,'tp'=4] {'tp'}, dimensions={0} | all-to-all | bytes 2621440 | tf_op jit(solution)/shard_map/all_to_all | solution.py:26
  211.8 0.3 reduce_sum.134
  212.2 0.3 reshape.100
  212.5 0.8 copy.54
  213.3 14.2 %all-to-all-start.7 = ((bf16[32,16,320]{2,1,0:T(8,128)(2,1)}), bf16[32,16,320]{2,1,0:T(8,128)(2,1)S(1)}, u32[]{:S(2)}, u32[]{:S(2)}) async-start(bf16[32,16,320]{2,1,0:T(8,128)(2,1)} %bitcast.12), calls=%async_computation.7 | async-start | bytes 786432 | tf_op jit(solution)/shard_map/all_to_all | solution.py:26
  227.9 2.1 collective-permute-start
  230.0 23.9 %all-to-all-done.7 = bf16[32,16,320]{2,1,0:T(8,128)(2,1)S(1)} async-done(((bf16[32,16,320]{2,1,0:T(8,128)(2,1)}), bf16[32,16,320]{2,1,0:T(8,128)(2,1)S(1)}, u32[]{:S(2)}, u32[]{:S(2)}) %all-to-all-start.7) | async-done | bytes 327712 | tf_op jit(solution)/shard_map/all_to_all | solution.py:26
  254.0 0.6 fusion.21
  (63 shorter events, 3.6 us)
Async XLA Ops:
  6.5 54.4 %copy-start = (bf16[256,2560]{1,0:T(8,128)(2,1)S(1)}, bf16[256,2560]{1,0:T(8,128)(2,1)}, u32[]{:S(2)}) copy-start(bf16[256,2560]{1,0:T(8,128)(2,1)} %param.15) | copy-start | bytes 3932164
  6.5 42.2 %copy-start.4 = (f32[32,2]{0,1:T(2,128)S(1)}, f32[32,2]{0,1:T(2,128)}, u32[]{:S(2)}) copy-start(f32[32,2]{0,1:T(2,128)} %param.18) | copy-start | bytes 772
  6.5 91.3 %all-gather.4.cloned.1.call-start = ((), (), s32[]{:S(2)}) async-start(), calls=%async_computation.8 | async-start | bytes 2867200 | tf_op jit(solution)/shard_map/all_gather | solution.py:114
  7.3 99.0 %all-gather.6.cloned.1.call-start = ((), (), s32[]{:S(2)}) async-start(), calls=%async_computation.9 | async-start | bytes 2867200 | tf_op jit(solution)/shard_map/all_gather | solution.py:114
  9.4 39.5 %all-to-all-start = ((bf16[4,32,256]{2,1,0:T(8,128)(2,1)}), bf16[4,32,256]{2,1,0:T(8,128)(2,1)S(1)}, u32[]{:S(2)}, u32[]{:S(2)}) async-start(bf16[4,32,256]{2,1,0:T(8,128)(2,1)} %broadcast_in_dim.24), calls=%async_computation | async-start | bytes 131072 | tf_op jit(solution)/shard_map/all_to_all | solution.py:22
  14.4 126.5 %all-gather.8.cloned.1.call-start = ((), (), s32[]{:S(2)}) async-start(), calls=%async_computation.10 | async-start | bytes 2867200 | tf_op jit(solution)/shard_map/all_gather | solution.py:114
  50.1 24.8 %copy-start.5 = (s32[32,2]{0,1:T(2,128)S(1)}, s32[32,2]{0,1:T(2,128)}, u32[]{:S(2)}) copy-start(s32[32,2]{0,1:T(2,128)} %param.17) | copy-start | bytes 772
  50.1 25.0 %copy-start.3 = (f32[4,2560]{1,0:T(4,128)S(1)}, f32[4,2560]{1,0:T(4,128)}, u32[]{:S(2)}) copy-start(f32[4,2560]{1,0:T(4,128)} %param.16) | copy-start | bytes 122884
  50.9 9.3 %all-to-all-start.1 = ((f32[4,32,384]{2,1,0:T(8,128)}), f32[4,32,384]{2,1,0:T(8,128)S(1)}, u32[]{:S(2)}, u32[]{:S(2)}) async-start(f32[4,32,384]{2,1,0:T(8,128)} %bitcast.5), calls=%async_computation.1 | async-start | bytes 393216 | tf_op jit(solution)/shard_map/all_to_all | solution.py:26
  61.0 29.0 %copy-start.2 = (bf16[32,2560]{1,0:T(8,128)(2,1)S(1)}, bf16[32,2560]{1,0:T(8,128)(2,1)}, u32[]{:S(2)}) copy-start(bf16[32,2560]{1,0:T(8,128)(2,1)} %param.11) | copy-start | bytes 491524
  62.5 18.3 %all-to-all-start.2 = ((bf16[8,16,640]{2,1,0:T(8,128)(2,1)}), bf16[8,16,640]{2,1,0:T(8,128)(2,1)S(1)}, u32[]{:S(2)}, u32[]{:S(2)}) async-start(bf16[8,16,640]{2,1,0:T(8,128)(2,1)} %reshape.94), calls=%async_computation.2 | async-start | bytes 327680 | tf_op jit(solution)/shard_map/all_to_all | solution.py:26
  81.5 8.0 %all-to-all-start.3 = ((bf16[4,16,640]{2,1,0:T(8,128)(2,1)}), bf16[4,16,640]{2,1,0:T(8,128)(2,1)S(1)}, u32[]{:S(2)}, u32[]{:S(2)}) async-start(bf16[4,16,640]{2,1,0:T(8,128)(2,1)} %broadcast_in_dim.58), calls=%async_computation.3 | async-start | bytes 163840 | tf_op jit(solution)/shard_map/all_to_all | solution.py:22
  91.5 56.7 %all-to-all-start.4 = ((bf16[16,16,768]{2,1,0:T(8,128)(2,1)}), bf16[16,16,768]{2,1,0:T(8,128)(2,1)S(1)}, u32[]{:S(2)}, u32[]{:S(2)}) async-start(bf16[16,16,768]{2,1,0:T(8,128)(2,1)} %broadcast_in_dim.59), calls=%async_computation.4 | async-start | bytes 786432 | tf_op jit(solution)/shard_map/all_to_all | solution.py:22
  102.6 60.0 %collective-permute-start.1 = (bf16[4,2560,108]{1,0,2:T(4,128)(2,1)}, bf16[4,2560,108]{1,0,2:T(4,128)(2,1)}, u32[]{:S(2)}, u32[]{:S(2)}) collective-permute-start(bf16[4,2560,108]{1,0,2:T(4,128)(2,1)} %copy.45), channel_id=1, source_target_pairs={{0,256},{256,0},{1,257},{257,1},{2,258},{258,2},{3,259},{259,3},{4... | collective-permute-start | bytes 6635528 | tf_op jit(solution)/shard_map/ppermute | solution.py:115
  111.0 57.1 %collective-permute-start.2 = (bf16[4,2560,108]{1,0,2:T(4,128)(2,1)}, bf16[4,2560,108]{1,0,2:T(4,128)(2,1)}, u32[]{:S(2)}, u32[]{:S(2)}) collective-permute-start(bf16[4,2560,108]{1,0,2:T(4,128)(2,1)} %copy.46), channel_id=1, source_target_pairs={{0,256},{256,0},{1,257},{257,1},{2,258},{258,2},{3,259},{259,3},{4... | collective-permute-start | bytes 6635528 | tf_op jit(solution)/shard_map/ppermute | solution.py:115
  145.6 28.0 %collective-permute-start.3 = (bf16[4,108,2560]{2,0,1:T(4,128)(2,1)}, bf16[4,108,2560]{2,0,1:T(4,128)(2,1)}, u32[]{:S(2)}, u32[]{:S(2)}) collective-permute-start(bf16[4,108,2560]{2,0,1:T(4,128)(2,1)} %copy.47), channel_id=1, source_target_pairs={{0,256},{256,0},{1,257},{257,1},{2,258},{258,2},{3,259},{259,3},{4... | collective-permute-start | bytes 6635528 | tf_op jit(solution)/shard_map/ppermute | solution.py:115
  149.4 27.5 %all-to-all-start.5 = ((bf16[4,256,640]{2,1,0:T(8,128)(2,1)}), bf16[4,256,640]{2,1,0:T(8,128)(2,1)S(1)}, u32[]{:S(2)}, u32[]{:S(2)}) async-start(bf16[4,256,640]{2,1,0:T(8,128)(2,1)} %broadcast_in_dim.60), calls=%async_computation.5 | async-start | bytes 2621440 | tf_op jit(solution)/shard_map/all_to_all | solution.py:22
  176.9 1.6 copy-start.1
  213.3 40.6 %all-to-all-start.7 = ((bf16[32,16,320]{2,1,0:T(8,128)(2,1)}), bf16[32,16,320]{2,1,0:T(8,128)(2,1)S(1)}, u32[]{:S(2)}, u32[]{:S(2)}) async-start(bf16[32,16,320]{2,1,0:T(8,128)(2,1)} %bitcast.12), calls=%async_computation.7 | async-start | bytes 786432 | tf_op jit(solution)/shard_map/all_to_all | solution.py:26
  227.9 26.1 %collective-permute-start = (f32[16,320]{1,0:T(8,128)S(1)}, f32[16,320]{1,0:T(8,128)S(1)}, u32[]{:S(2)}, u32[]{:S(2)}) collective-permute-start(f32[16,320]{1,0:T(8,128)S(1)} %bitcast.37), channel_id=1, source_target_pairs={{0,256},{256,0},{1,257},{257,1},{2,258},{258,2},{3,259},{259,3},{4... | collective-permute-start | bytes 61448 | tf_op jit(solution)/shard_map/ppermute | solution.py:204
Sparse Core Ops, SparseCore 0:
  9.5 45.4 all-gather.3
  57.1 41.3 all-gather.5
  100.5 40.2 all-gather.7

commit v2 on v1

v2 whole, which is shorter than its diff:
```python
import math

import jax
import jax.numpy as jnp
from jax import lax
from jax.experimental import pallas as pl
from jax.experimental.pallas import tpu as pltpu
from jax.sharding import Mesh
from jax.sharding import PartitionSpec as P

HD = 128
Y = 4
Z = 16
TP = 4
GROUP = ("pool", "tp")
F32 = jnp.float32
BF16 = jnp.bfloat16


def spread(x, axis, count):
    copies = jnp.broadcast_to(x[None], (count,) + x.shape)
    return lax.all_to_all(copies, axis, split_axis=0, concat_axis=0, tiled=True)


def exchange(x, axis):
    return lax.all_to_all(x, axis, split_axis=0, concat_axis=0, tiled=True)


def pack_weights(w_gate, w_up, w_down):
    pad = -w_down.shape[0] % 16
    return jnp.concatenate(
        [jnp.pad(w, ((0, pad), (0, 0))) for w in (w_gate.T, w_up.T, w_down)], 0
    )


def ffn_kernel(ids_ref, x_ref, mine_ref, other_ref, o_ref, acc_ref):
    step = pl.program_id(0)
    width = o_ref.shape[1]
    hidden = mine_ref.shape[1] // 3

    @pl.when(step == 0)
    def _():
        acc_ref[...] = jnp.zeros_like(acc_ref)

    x = x_ref[:, :width]
    route = x_ref[:, width:].astype(F32)
    total = acc_ref[...]
    for e, w in enumerate((mine_ref, other_ref)):
        both = lax.dot_general(
            x, w[0, : 2 * hidden], (((1,), (1,)), ((), ())), preferred_element_type=F32
        )
        gate = both[:, :hidden]
        act = (gate / (1.0 + jnp.exp(-gate)) * both[:, hidden:]).astype(BF16)
        scale = jnp.zeros((x.shape[0], 1), F32)
        for k in range(2):
            value = route[:, 2 + k : 3 + k] + route[:, 4 + k : 5 + k]
            scale += jnp.where(route[:, k : k + 1] == ids_ref[e].astype(F32), value, 0.0)
        total += scale * jnp.dot(act, w[0, 2 * hidden :], preferred_element_type=F32)
    acc_ref[...] = total

    @pl.when(step == pl.num_programs(0) - 1)
    def _():
        o_ref[...] = total.astype(BF16)


def ffn(ids, x, mine, other):
    rows = x.shape[0]
    steps, depth, width = mine.shape
    weights = pl.BlockSpec((1, depth, width), lambda i: (i, 0, 0))
    return pl.pallas_call(
        ffn_kernel,
        grid=(steps,),
        out_shape=jax.ShapeDtypeStruct((rows, width), BF16),
        in_specs=[
            pl.BlockSpec(memory_space=pltpu.SMEM),
            pl.BlockSpec(x.shape, lambda i: (0, 0)),
            weights,
            weights,
        ],
        out_specs=pl.BlockSpec((rows, width), lambda i: (0, 0)),
        scratch_shapes=[pltpu.VMEM((rows, width), F32)],
        compiler_params=pltpu.CompilerParams(vmem_limit_bytes=58 << 20),
        cost_estimate=pl.CostEstimate(
            flops=4 * rows * width * depth * steps,
            bytes_accessed=4 * width * depth * steps,
            transcendentals=0,
        ),
    )(ids, x, mine, other)


def body(
    tokens,
    query_proj,
    key_proj,
    value_proj,
    w_out,
    modulation,
    expert_ids,
    gate_values,
    w_gate,
    w_up,
    w_down,
):
    rows, width = tokens.shape
    heads = query_proj.shape[1] // HD
    own_rows = rows // (2 * TP)
    pool = lax.axis_index("pool")
    tp = lax.axis_index("tp")
    group = pool * TP + tp

    packed = pack_weights(w_gate[0], w_up[0], w_down[0])
    mine = lax.all_gather(packed, "y", axis=0)

    key_value = spread(jnp.concatenate([key_proj, value_proj], 1), "z", Z)
    key_value = key_value.reshape(Z * rows, 2 * heads * HD)
    queries = spread(query_proj, "y", Y).reshape(Y * rows, heads * HD)
    parts = []
    stats = []
    for h in range(heads):
        cols = slice(h * HD, (h + 1) * HD)
        keys = key_value[:, cols]
        values = key_value[:, heads * HD + h * HD : heads * HD + (h + 1) * HD]
        scores = lax.dot_general(
            queries[:, cols], keys, (((1,), (1,)), ((), ())), preferred_element_type=F32
        ) * (1.0 / math.sqrt(HD))
        top = jnp.max(scores, axis=1, keepdims=True)
        weights = jnp.exp(scores - top)
        stats += [top, jnp.sum(weights, axis=1, keepdims=True)]
        parts.append(jnp.dot(weights.astype(BF16), values, preferred_element_type=F32))
    stats = jnp.concatenate(stats, 1)
    stats = jnp.pad(stats, ((0, 0), (0, HD - stats.shape[1])))
    partial = jnp.concatenate(parts + [stats], 1).reshape(Y, rows, (heads + 1) * HD)
    partial = exchange(partial, "y")
    outs = []
    for h in range(heads):
        acc = partial[:, :, h * HD : (h + 1) * HD]
        top = partial[:, :, heads * HD + 2 * h : heads * HD + 2 * h + 1]
        part_total = partial[:, :, heads * HD + 2 * h + 1 : heads * HD + 2 * h + 2]
        scale = jnp.exp(top - jnp.max(top, axis=0, keepdims=True))
        outs.append(jnp.sum(scale * acc, axis=0) / jnp.sum(scale * part_total, axis=0))
    heads_out = jnp.concatenate(outs, 1).astype(BF16)

    projected = jnp.dot(heads_out, w_out, preferred_element_type=F32).astype(BF16)
    projected = exchange(projected.reshape(2 * TP, own_rows, width), GROUP)
    attention = jnp.sum(projected.astype(F32), axis=0)
    own_tokens = lax.dynamic_slice_in_dim(tokens, group * own_rows, own_rows, 0).astype(F32)
    resid = own_tokens + modulation[0] * attention
    row_mean = jnp.mean(resid, axis=1, keepdims=True)
    row_square = jnp.mean(resid * resid, axis=1, keepdims=True)
    inv_dev = lax.rsqrt(row_square - row_mean * row_mean + 1e-06)
    normed = ((resid - row_mean) * inv_dev * (1.0 + modulation[2]) + modulation[1]).astype(BF16)

    own_ids = lax.dynamic_slice_in_dim(expert_ids, group * own_rows, own_rows, 0)
    own_gates = lax.dynamic_slice_in_dim(gate_values, group * own_rows, own_rows, 0)
    gates_hi = lax.reduce_precision(own_gates, 8, 7)
    gates_lo = own_gates - gates_hi
    route = jnp.concatenate(
        [own_ids.astype(BF16), gates_hi.astype(BF16), gates_lo.astype(BF16)], 1
    )
    route = jnp.pad(route, ((0, 0), (0, HD - route.shape[1])))
    sent = jnp.concatenate([normed, route], 1)
    ring = spread(sent, "z", Z).reshape(Z * own_rows, width + HD)
    mine, ring = lax.optimization_barrier((mine, ring))
    other = lax.ppermute(mine, "pool", [(0, 1), (1, 0)])
    rows_in = spread(ring, "tp", TP).reshape(TP * Z * own_rows, width + HD)
    ids = jnp.stack([group, (1 - pool) * TP + tp]).astype(jnp.int32)
    mixed = ffn(ids, rows_in, mine, other)

    mixed = exchange(mixed.reshape(TP, Z * own_rows, width), "tp")
    mixed = jnp.sum(mixed.astype(F32), axis=0).astype(BF16)
    mixed = exchange(mixed.reshape(Z, own_rows, width), "z")
    mixture = jnp.sum(mixed.astype(F32), axis=0)
    block_out = (resid + modulation[3] * mixture).astype(BF16)
    block_out = block_out.reshape(own_rows, 2 * TP, width // (2 * TP)).transpose(1, 0, 2)
    return exchange(block_out, GROUP).reshape(rows, width // (2 * TP))


def solution(mesh):
    split = Mesh(
        mesh.devices.reshape(2, Y, Z, TP), ("pool", "y", "z", "tp")
    )
    seq = ("y", "z")
    in_specs = (
        P(seq, None),
        P(seq, GROUP),
        P(seq, GROUP),
        P(seq, GROUP),
        P(GROUP, None),
        P(),
        P(seq, None),
        P(seq, None),
        P(GROUP, None, seq),
        P(GROUP, None, seq),
        P(GROUP, seq, None),
    )
    return jax.shard_map(
        body, mesh=split, in_specs=in_specs, out_specs=P(seq, GROUP), check_vma=False
    )
```

time: 263 us -> 230 us (0.87)
  local copies, waits for them, and re-layouts: 47.8 us -> 7.32 us
  blocking collectives: 53.9 us -> 79.6 us
  starting transfers between devices: 59.7 us -> 46.8 us
  waiting for transfers between devices: 69.4 us -> 57 us
  Pallas kernels: 12.2 us -> 17.1 us
  other arithmetic: 3.44 us -> 6.07 us
    all_to_all x4 -> x3, waiting for transfers between devices: 4.61 us -> 44 us  [spread(): return lax.all_to_all(copies, axis, split_axis=0, concat_axis=0, tiled=True)]
    all_to_all x1 -> x3, blocking collectives: 21 us -> 54.8 us  [exchange(): return lax.all_to_all(x, axis, split_axis=0, concat_axis=0, tiled=True)]
    all_gather x1 -> x0, blocking collectives: 32.9 us -> none  [body(): lax.all_gather(jnp.concatenate([key_proj, value_proj], 1), 'z', axis=0, t...]
    all_gather x3 -> x1, waiting for transfers between devices: 28 us -> 0.02 us  [body(): mine = lax.all_gather(packed, 'y', axis=0)]
    all_to_all x0 -> x1, blocking collectives: none -> 24.8 us  [spread(): return lax.all_to_all(copies, axis, split_axis=0, concat_axis=0, tiled=True)]
    all_gather x5 -> x0, local copies, waits for them, and re-layouts: 23 us -> none  [body(): mine = [lax.all_gather(w[0], 'y', axis=0) for w in (w_gate, w_up, w_down)]]
    all_to_all x3 -> x2, waiting for transfers between devices: 34.7 us -> 13 us  [exchange(): return lax.all_to_all(x, axis, split_axis=0, concat_axis=0, tiled=True)]
    all_to_all x3 -> x2, starting transfers between devices: 30.7 us -> 16.3 us  [exchange(): return lax.all_to_all(x, axis, split_axis=0, concat_axis=0, tiled=True)]
  transfers between devices with their start and end apart: 14 -> 7, of which waited for: 5 -> 5; matrix products, arithmetic and copies ran while one was open for 19% -> 4% of each run, Pallas kernels for 0% -> 0%
where the time goes in v2:
time: 230 us; the launch traced here: 229 us
  blocking collectives  79.6 us (35%)
  waiting for transfers between devices  57 us (25%)
  starting transfers between devices  46.8 us (20%)
  Pallas kernels  17.1 us (7%)
  between operations  13.6 us (6%)
  local copies, waits for them, and re-layouts  7.32 us (3%)
  other arithmetic  6.07 us (3%)
    all_to_all x3, blocking collectives, exchange(): return lax.all_to_all(x, axis, split_axis=0, concat_axis=0, tiled=True)  54.8 us
    all_to_all x3, waiting for transfers between devices, spread(): return lax.all_to_all(copies, axis, split_axis=0, concat_axis=0, tiled=True)  44 us
    all_to_all x1, blocking collectives, spread(): return lax.all_to_all(copies, axis, split_axis=0, concat_axis=0, tiled=True)  24.8 us
    all_to_all x3, starting transfers between devices, spread(): return lax.all_to_all(copies, axis, split_axis=0, concat_axis=0, tiled=True)  23.5 us
    pallas_call x1, Pallas kernels, ffn(): pl.pallas_call(ffn_kernel, grid=(steps,), out_shape=jax.ShapeDtypeStruct(...  17.1 us
    all_to_all x2, starting transfers between devices, exchange(): return lax.all_to_all(x, axis, split_axis=0, concat_axis=0, tiled=True)  16.3 us
    all_to_all x2, waiting for transfers between devices, exchange(): return lax.all_to_all(x, axis, split_axis=0, concat_axis=0, tiled=True)  13 us
    ppermute x1, starting transfers between devices, body(): other = lax.ppermute(mine, 'pool', [(0, 1), (1, 0)])  6.96 us
  transfers between devices with their start and end apart: 7, of which 5 were waited for; matrix products, arithmetic and copies ran while one was open for 4% of the time, Pallas kernels for 0%

profile of v2, /device:TPU:1, one launch (start us, length us, event | category | flops | bytes accessed | tf_op | source)
XLA Modules:
  0.0 228.8 jit_solution(10373194473293505459)
XLA Ops:
  6.5 2.9 %fusion.5 = bf16[336,2560]{1,0:T(8,128)(2,1)} fusion(bf16[108,2560]{1,0:T(8,128)(2,1)} %bitcast.31, bf16[108,2560]{1,0:T(8,128)(2,1)} %bitcast.32, bf16[108,2560]{1,0:T(8,128)(2,1)} %bitcast.33), kind=kLoop, calls=%fused_computation.10 | loop fusion | flops 12042240 | bytes 3379200 | tf_op jit(solution)/shard_map/concatenate | solution.py:31
  9.4 0.7 copy-done.3
  10.1 0.6 broadcast_in_dim.17
  10.8 5.0 %all-to-all-start.1 = ((bf16[4,32,256]{2,1,0:T(8,128)(2,1)}), bf16[4,32,256]{2,1,0:T(8,128)(2,1)S(1)}, u32[]{:S(2)}, u32[]{:S(2)}) async-start(bf16[4,32,256]{2,1,0:T(8,128)(2,1)} %broadcast_in_dim.17), calls=%async_computation.1 | async-start | bytes 131072 | tf_op jit(solution)/shard_map/all_to_all | solution.py:22
  15.8 4.5 %all-to-all-done.1 = bf16[4,32,256]{2,1,0:T(8,128)(2,1)S(1)} async-done(((bf16[4,32,256]{2,1,0:T(8,128)(2,1)}), bf16[4,32,256]{2,1,0:T(8,128)(2,1)S(1)}, u32[]{:S(2)}, u32[]{:S(2)}) %all-to-all-start.1) | async-done | bytes 65568 | tf_op jit(solution)/shard_map/all_to_all | solution.py:22
  20.2 0.9 broadcast_in_dim.16
  21.1 14.9 %all-to-all-start = ((bf16[16,32,512]{2,1,0:T(8,128)(2,1)}), bf16[16,32,512]{2,1,0:T(8,128)(2,1)S(1)}, u32[]{:S(2)}, u32[]{:S(2)}) async-start(bf16[16,32,512]{2,1,0:T(8,128)(2,1)} %broadcast_in_dim.16), calls=%async_computation | async-start | bytes 1048576 | tf_op jit(solution)/shard_map/all_to_all | solution.py:22
  36.1 0.1 copy.44
  36.3 0.1 copy.45
  36.4 21.4 %all-to-all-done = bf16[16,32,512]{2,1,0:T(8,128)(2,1)S(1)} async-done(((bf16[16,32,512]{2,1,0:T(8,128)(2,1)}), bf16[16,32,512]{2,1,0:T(8,128)(2,1)S(1)}, u32[]{:S(2)}, u32[]{:S(2)}) %all-to-all-start) | async-done | bytes 524320 | tf_op jit(solution)/shard_map/all_to_all | solution.py:22
  57.8 0.2 fusion.39
  58.1 0.1 fusion.8
  58.2 0.2 fusion.40
  58.4 0.1 fusion.6
  58.5 0.2 fusion.10
  58.8 0.2 fusion.12
  59.0 0.8 copy.39
  59.9 3.4 %all-to-all-start.2 = ((f32[4,32,384]{2,1,0:T(8,128)}), f32[4,32,384]{2,1,0:T(8,128)S(1)}, u32[]{:S(2)}, u32[]{:S(2)}) async-start(f32[4,32,384]{2,1,0:T(8,128)} %bitcast.6), calls=%async_computation.2 | async-start | bytes 393216 | tf_op jit(solution)/shard_map/all_to_all | solution.py:26
  63.2 7.3 %all-to-all-done.2 = f32[4,32,384]{2,1,0:T(8,128)S(1)} async-done(((f32[4,32,384]{2,1,0:T(8,128)}), f32[4,32,384]{2,1,0:T(8,128)S(1)}, u32[]{:S(2)}, u32[]{:S(2)}) %all-to-all-start.2) | async-done | bytes 196640 | tf_op jit(solution)/shard_map/all_to_all | solution.py:26
  70.5 0.2 slice_reduce_fusion.1
  70.7 0.3 fusion.22
  71.0 0.1 fusion.23
  71.1 0.1 divide_convert_fusion
  71.2 0.3 convolution_convert_fusion
  71.5 0.7 reshape.71
  72.2 13.0 %all-to-all-start.3 = ((bf16[8,4,2560]{2,1,0:T(4,128)(2,1)}), bf16[8,4,2560]{2,1,0:T(4,128)(2,1)S(1)}, u32[]{:S(2)}, u32[]{:S(2)}) async-start(bf16[8,4,2560]{2,1,0:T(4,128)(2,1)} %reshape.71), calls=%async_computation.3 | async-start | bytes 327680 | tf_op jit(solution)/shard_map/all_to_all | solution.py:26
  85.3 0.1 slice_reduce_fusion.3
  85.4 5.7 %all-to-all-done.3 = bf16[8,4,2560]{2,1,0:T(4,128)(2,1)S(1)} async-done(((bf16[8,4,2560]{2,1,0:T(4,128)(2,1)}), bf16[8,4,2560]{2,1,0:T(4,128)(2,1)S(1)}, u32[]{:S(2)}, u32[]{:S(2)}) %all-to-all-start.3) | async-done | bytes 163872 | tf_op jit(solution)/shard_map/all_to_all | solution.py:26
  91.2 0.9 fusion.38
  92.2 0.1 add_convert_fusion.1
  92.3 0.1 broadcast_in_dim.22
  92.4 24.8 %all_to_all.45 = bf16[16,4,2688]{2,1,0:T(4,128)(2,1)S(1)} all-to-all(bf16[16,4,2688]{2,1,0:T(4,128)(2,1)S(1)} %broadcast_in_dim.22), channel_id=1, replica_groups=mesh['pool'=2,'y'=4,'z'=16,'tp'=4] {'z'}, dimensions={0} | all-to-all | bytes 688128 | tf_op jit(solution)/shard_map/all_to_all | solution.py:22
  117.2 0.1 reshape.72
  117.3 7.0 %collective-permute-start = (bf16[4,336,2560]{2,1,0:T(8,128)(2,1)}, bf16[4,336,2560]{2,1,0:T(8,128)(2,1)}, u32[]{:S(2)}, u32[]{:S(2)}) collective-permute-start(bf16[4,336,2560]{2,1,0:T(8,128)(2,1)} %bitcast.23), channel_id=1, source_target_pairs={{0,256},{256,0},{1,257},{257,1},{2,258},{258,2},{3,259},{259,3},{4... | collective-permute-start | bytes 20643848 | tf_op jit(solution)/shard_map/ppermute | solution.py:164
  124.3 1.2 broadcast_in_dim.23
  125.5 3.5 %all-to-all-start.5 = ((bf16[4,64,2688]{2,1,0:T(8,128)(2,1)}), bf16[4,64,2688]{2,1,0:T(8,128)(2,1)S(1)}, u32[]{:S(2)}, u32[]{:S(2)}) async-start(bf16[4,64,2688]{2,1,0:T(8,128)(2,1)} %broadcast_in_dim.23), calls=%async_computation.5 | async-start | bytes 2752512 | tf_op jit(solution)/shard_map/all_to_all | solution.py:22
  129.0 0.6 pad_add_fusion.ids_ref
  129.6 18.1 %all-to-all-done.5 = bf16[4,64,2688]{2,1,0:T(8,128)(2,1)S(1)} async-done(((bf16[4,64,2688]{2,1,0:T(8,128)(2,1)}), bf16[4,64,2688]{2,1,0:T(8,128)(2,1)S(1)}, u32[]{:S(2)}, u32[]{:S(2)}) %all-to-all-start.5) | async-done | bytes 1376288 | tf_op jit(solution)/shard_map/all_to_all | solution.py:22
  147.8 1.1 copy-done.1
  148.8 17.1 %shard_map.109 = bf16[256,2560]{1,0:T(8,128)(2,1)} custom-call(s32[2]{0:T(128)} %pad_add_fusion.ids_ref, bf16[256,2688]{1,0:T(8,128)(2,1)} %bitcast.25, bf16[4,336,2560]{2,1,0:T(8,128)(2,1)} %bitcast.24, bf16[4,336,2560]{2,1,0:T(8,128)(2,1)} %collective-permute-done.other_ref), custom_call_target="tpu_custom_call" | custom-call | flops 3523215360 | bytes 13762560 | tf_op jit(solution)/shard_map/pallas_call | solution.py:70
  165.9 20.4 %all_to_all.46 = bf16[4,64,2560]{2,1,0:T(8,128)(2,1)S(1)} all-to-all(bf16[4,64,2560]{2,1,0:T(8,128)(2,1)} %bitcast.26), channel_id=1, replica_groups=mesh['pool'=2,'y'=4,'z'=16,'tp'=4] {'tp'}, dimensions={0} | all-to-all | bytes 2621440 | tf_op jit(solution)/shard_map/all_to_all | solution.py:26
  186.4 0.2 reduce_sum.111
  186.6 0.1 reshape.75
  186.7 19.0 %all_to_all.47 = bf16[16,4,2560]{2,1,0:T(4,128)(2,1)S(1)} all-to-all(bf16[16,4,2560]{2,1,0:T(4,128)(2,1)S(1)} %reshape.75), channel_id=1, replica_groups=mesh['pool'=2,'y'=4,'z'=16,'tp'=4] {'z'}, dimensions={0} | all-to-all | bytes 655360 | tf_op jit(solution)/shard_map/all_to_all | solution.py:26
  205.7 0.1 convert_reduce_fusion
  205.9 0.1 reshape.76
  206.0 15.4 %all_to_all.48 = bf16[8,4,320]{2,1,0:T(4,128)(2,1)S(1)} all-to-all(bf16[8,4,320]{2,1,0:T(4,128)(2,1)S(1)} %bitcast.36), channel_id=1, replica_groups=mesh['pool'=2,'y'=4,'z'=16,'tp'=4] {'pool','tp'}, dimensions={0} | all-to-all | bytes 40960 | tf_op jit(solution)/shard_map/all_to_all | solution.py:26
  221.4 0.6 reshape.77
  (31 shorter events, 0.5 us)
Async XLA Ops:
  6.5 64.7 %copy-start = (bf16[256,2560]{1,0:T(8,128)(2,1)S(1)}, bf16[256,2560]{1,0:T(8,128)(2,1)}, u32[]{:S(2)}) copy-start(bf16[256,2560]{1,0:T(8,128)(2,1)} %param.15) | copy-start | bytes 3932164
  6.5 110.8 %all-gather.3.cloned.1.call-start = ((), (), s32[]{:S(2)}) async-start(), calls=%async_computation.9 | async-start | bytes 8601600 | tf_op jit(solution)/shard_map/all_gather | solution.py:112
  9.4 0.7 copy-start.3
  9.4 6.4 %copy-start.4 = (bf16[32,256]{1,0:T(8,128)(2,1)S(1)}, bf16[32,256]{1,0:T(8,128)(2,1)}, u32[]{:S(2)}) copy-start(bf16[32,256]{1,0:T(8,128)(2,1)} %param.14) | copy-start | bytes 49156
  9.4 6.4 %copy-start.5 = (bf16[32,256]{1,0:T(8,128)(2,1)S(1)}, bf16[32,256]{1,0:T(8,128)(2,1)}, u32[]{:S(2)}) copy-start(bf16[32,256]{1,0:T(8,128)(2,1)} %param.13) | copy-start | bytes 49156
  9.4 26.6 %copy-start.6 = (s32[32,2]{0,1:T(2,128)S(1)}, s32[32,2]{0,1:T(2,128)}, u32[]{:S(2)}) copy-start(s32[32,2]{0,1:T(2,128)} %param.17) | copy-start | bytes 772
  9.4 26.8 %copy-start.7 = (f32[32,2]{0,1:T(2,128)S(1)}, f32[32,2]{0,1:T(2,128)}, u32[]{:S(2)}) copy-start(f32[32,2]{0,1:T(2,128)} %param.18) | copy-start | bytes 772
  10.8 9.5 %all-to-all-start.1 = ((bf16[4,32,256]{2,1,0:T(8,128)(2,1)}), bf16[4,32,256]{2,1,0:T(8,128)(2,1)S(1)}, u32[]{:S(2)}, u32[]{:S(2)}) async-start(bf16[4,32,256]{2,1,0:T(8,128)(2,1)} %broadcast_in_dim.17), calls=%async_computation.1 | async-start | bytes 131072 | tf_op jit(solution)/shard_map/all_to_all | solution.py:22
  21.1 36.7 %all-to-all-start = ((bf16[16,32,512]{2,1,0:T(8,128)(2,1)}), bf16[16,32,512]{2,1,0:T(8,128)(2,1)S(1)}, u32[]{:S(2)}, u32[]{:S(2)}) async-start(bf16[16,32,512]{2,1,0:T(8,128)(2,1)} %broadcast_in_dim.16), calls=%async_computation | async-start | bytes 1048576 | tf_op jit(solution)/shard_map/all_to_all | solution.py:22
  59.0 26.3 %copy-start.2 = (f32[4,2560]{1,0:T(4,128)S(1)}, f32[4,2560]{1,0:T(4,128)}, u32[]{:S(2)}) copy-start(f32[4,2560]{1,0:T(4,128)} %param.16) | copy-start | bytes 122884
  59.9 10.6 %all-to-all-start.2 = ((f32[4,32,384]{2,1,0:T(8,128)}), f32[4,32,384]{2,1,0:T(8,128)S(1)}, u32[]{:S(2)}, u32[]{:S(2)}) async-start(f32[4,32,384]{2,1,0:T(8,128)} %bitcast.6), calls=%async_computation.2 | async-start | bytes 393216 | tf_op jit(solution)/shard_map/all_to_all | solution.py:26
  72.2 18.9 %all-to-all-start.3 = ((bf16[8,4,2560]{2,1,0:T(4,128)(2,1)}), bf16[8,4,2560]{2,1,0:T(4,128)(2,1)S(1)}, u32[]{:S(2)}, u32[]{:S(2)}) async-start(bf16[8,4,2560]{2,1,0:T(4,128)(2,1)} %reshape.71), calls=%async_computation.3 | async-start | bytes 327680 | tf_op jit(solution)/shard_map/all_to_all | solution.py:26
  117.3 30.4 %collective-permute-start = (bf16[4,336,2560]{2,1,0:T(8,128)(2,1)}, bf16[4,336,2560]{2,1,0:T(8,128)(2,1)}, u32[]{:S(2)}, u32[]{:S(2)}) collective-permute-start(bf16[4,336,2560]{2,1,0:T(8,128)(2,1)} %bitcast.23), channel_id=1, source_target_pairs={{0,256},{256,0},{1,257},{257,1},{2,258},{258,2},{3,259},{259,3},{4... | collective-permute-start | bytes 20643848 | tf_op jit(solution)/shard_map/ppermute | solution.py:164
  125.5 22.3 %all-to-all-start.5 = ((bf16[4,64,2688]{2,1,0:T(8,128)(2,1)}), bf16[4,64,2688]{2,1,0:T(8,128)(2,1)S(1)}, u32[]{:S(2)}, u32[]{:S(2)}) async-start(bf16[4,64,2688]{2,1,0:T(8,128)(2,1)} %broadcast_in_dim.23), calls=%async_computation.5 | async-start | bytes 2752512 | tf_op jit(solution)/shard_map/all_to_all | solution.py:22
  147.8 1.1 copy-start.1
Sparse Core Ops, SparseCore 0:
  9.6 85.6 all-gather.2

commit v3 on v2

v3 whole, which is shorter than its diff:
```python
import math

import jax
import jax.numpy as jnp
from jax import lax
from jax.experimental import pallas as pl
from jax.experimental.pallas import tpu as pltpu
from jax.sharding import Mesh
from jax.sharding import PartitionSpec as P

HD = 128
Y = 4
ZHI = 4
ZLO = 4
Z = ZHI * ZLO
RING = ("zhi", "zlo")
TP = 4
GROUP = ("pool", "tp")
F32 = jnp.float32
BF16 = jnp.bfloat16


def copies_of(x, count):
    return jnp.broadcast_to(x[None], (count,) + x.shape)


def spread(x, axis, count):
    return exchange(copies_of(x, count), axis)


def exchange(x, axis):
    return lax.all_to_all(x, axis, split_axis=0, concat_axis=0, tiled=True)


def pack_weights(w_gate, w_up, w_down):
    pad = -w_down.shape[0] % 16
    return jnp.concatenate(
        [jnp.pad(w, ((0, pad), (0, 0))) for w in (w_gate.T, w_up.T, w_down)], 0
    )


def ffn_kernel(ids_ref, x_ref, mine_ref, other_ref, o_ref, xt_ref, act_ref, down_ref):
    step = pl.program_id(0)
    width = o_ref.shape[1]
    hidden = mine_ref.shape[1] // 3
    weights = [
        (e, w, s) for s in range(mine_ref.shape[0]) for e, w in enumerate((mine_ref, other_ref))
    ]

    @pl.when(step == 0)
    def _():
        xt_ref[...] = x_ref[...].T

    route = xt_ref[width : width + 16].astype(F32)
    scales = []
    for e in range(2):
        scale = jnp.zeros((1, x_ref.shape[0]), F32)
        for k in range(2):
            value = route[2 + k : 3 + k] + route[4 + k : 5 + k]
            scale += jnp.where(route[k : k + 1] == ids_ref[e].astype(F32), value, 0.0)
        scales.append(scale)
    both = jnp.dot(
        jnp.concatenate([w[s, : 2 * hidden] for _, w, s in weights], 0),
        xt_ref[:width],
        preferred_element_type=F32,
    )
    acts = []
    for i, (e, _, _) in enumerate(weights):
        gate = both[2 * i * hidden : (2 * i + 1) * hidden]
        up = both[(2 * i + 1) * hidden : (2 * i + 2) * hidden]
        acts.append((gate / (1.0 + jnp.exp(-gate)) * up * scales[e]).astype(BF16))
    units = len(weights) * hidden
    here = pl.ds(pl.multiple_of(step * units, 16), units)
    act_ref[here] = jnp.concatenate(acts, 0)
    down_ref[here] = jnp.concatenate([w[s, 2 * hidden :] for _, w, s in weights], 0)

    @pl.when(step == pl.num_programs(0) - 1)
    def _():
        o_ref[...] = lax.dot_general(
            act_ref[...], down_ref[...], (((0,), (0,)), ((), ())), preferred_element_type=F32
        ).astype(BF16)


def ffn(ids, x, mine, other):
    rows = x.shape[0]
    parts, depth, width = mine.shape
    each = 2
    units = 2 * parts * (depth // 3)
    weights = pl.BlockSpec((each, depth, width), lambda i: (i, 0, 0))
    return pl.pallas_call(
        ffn_kernel,
        grid=(parts // each,),
        out_shape=jax.ShapeDtypeStruct((rows, width), BF16),
        in_specs=[
            pl.BlockSpec(memory_space=pltpu.SMEM),
            pl.BlockSpec(x.shape, lambda i: (0, 0)),
            weights,
            weights,
        ],
        out_specs=pl.BlockSpec((rows, width), lambda i: (0, 0)),
        scratch_shapes=[
            pltpu.VMEM((x.shape[1], rows), BF16),
            pltpu.VMEM((units, rows), BF16),
            pltpu.VMEM((units, width), BF16),
        ],
        compiler_params=pltpu.CompilerParams(vmem_limit_bytes=58 << 20),
        cost_estimate=pl.CostEstimate(
            flops=4 * rows * width * depth * parts,
            bytes_accessed=4 * width * depth * parts,
            transcendentals=0,
        ),
    )(ids, x, mine, other)


def body(
    tokens,
    query_proj,
    key_proj,
    value_proj,
    w_out,
    modulation,
    expert_ids,
    gate_values,
    w_gate,
    w_up,
    w_down,
):
    rows, width = tokens.shape
    heads = query_proj.shape[1] // HD
    own_rows = rows // (2 * TP)
    pool = lax.axis_index("pool")
    tp = lax.axis_index("tp")
    group = pool * TP + tp

    mine = lax.all_gather(pack_weights(w_gate[0], w_up[0], w_down[0]), "y", axis=0)

    blocks = [query_proj] + [
        lax.ppermute(query_proj, "zhi", [(i, (i - k) % ZHI) for i in range(ZHI)])
        for k in range(1, ZHI)
    ]
    first = (ZHI - lax.axis_index("zhi")) % ZHI * rows
    queries = lax.dynamic_slice_in_dim(
        jnp.concatenate(blocks + blocks[: ZHI - 1], 0), first, ZHI * rows, 0
    )
    copies = copies_of(jnp.concatenate([key_proj, value_proj], 1), Y * ZLO)
    key_value = exchange(copies, ("y", "zlo")).reshape(Y * ZLO * rows, 2 * heads * HD)
    parts = []
    stats = []
    for h in range(heads):
        cols = slice(h * HD, (h + 1) * HD)
        keys = key_value[:, cols]
        values = key_value[:, heads * HD + h * HD : heads * HD + (h + 1) * HD]
        scores = lax.dot_general(
            queries[:, cols], keys, (((1,), (1,)), ((), ())), preferred_element_type=F32
        ) * (1.0 / math.sqrt(HD))
        top = jnp.max(scores, axis=1, keepdims=True)
        weights = jnp.exp(scores - top)
        total = jnp.sum(weights, axis=1, keepdims=True)
        part = jnp.dot(weights.astype(BF16), values, preferred_element_type=F32)
        parts.append((part / total).astype(BF16))
        log_sum = top + jnp.log(total)
        high = lax.reduce_precision(log_sum, 8, 7)
        middle = lax.reduce_precision(log_sum - high, 8, 7)
        stats += [high, middle, log_sum - high - middle]
    stats = jnp.concatenate(stats, 1).astype(BF16)
    stats = jnp.pad(stats, ((0, 0), (0, HD - stats.shape[1])))
    partial = jnp.concatenate(parts + [stats], 1).reshape(ZHI, rows, (heads + 1) * HD)
    partial = exchange(partial, "zhi").astype(F32)
    outs = []
    for h in range(heads):
        log_sum = partial[:, :, heads * HD + 3 * h : heads * HD + 3 * h + 3]
        log_sum = jnp.sum(log_sum, axis=2, keepdims=True)
        scale = jnp.exp(log_sum - jnp.max(log_sum, axis=0, keepdims=True))
        acc = jnp.sum(scale * partial[:, :, h * HD : (h + 1) * HD], axis=0)
        outs.append(acc / jnp.sum(scale, axis=0))
    heads_out = jnp.concatenate(outs, 1).astype(BF16)

    projected = jnp.dot(heads_out, w_out, preferred_element_type=F32).astype(BF16)
    projected = exchange(projected.reshape(2 * TP, own_rows, width), GROUP)
    attention = jnp.sum(projected.astype(F32), axis=0)
    own_tokens = lax.dynamic_slice_in_dim(tokens, group * own_rows, own_rows, 0).astype(F32)
    resid = own_tokens + modulation[0] * attention
    row_mean = jnp.mean(resid, axis=1, keepdims=True)
    row_square = jnp.mean(resid * resid, axis=1, keepdims=True)
    inv_dev = lax.rsqrt(row_square - row_mean * row_mean + 1e-06)
    normed = ((resid - row_mean) * inv_dev * (1.0 + modulation[2]) + modulation[1]).astype(BF16)

    own_ids = lax.dynamic_slice_in_dim(expert_ids, group * own_rows, own_rows, 0)
    own_gates = lax.dynamic_slice_in_dim(gate_values, group * own_rows, own_rows, 0)
    gates_hi = lax.reduce_precision(own_gates, 8, 7)
    gates_lo = own_gates - gates_hi
    route = jnp.concatenate(
        [own_ids.astype(BF16), gates_hi.astype(BF16), gates_lo.astype(BF16)], 1
    )
    route = jnp.pad(route, ((0, 0), (0, HD - route.shape[1])))
    sent = jnp.concatenate([normed, route], 1)
    ring = spread(sent, RING, Z).reshape(Z * own_rows, width + HD)
    mine, ring = lax.optimization_barrier((mine, ring))
    other = lax.ppermute(mine, "pool", [(0, 1), (1, 0)])
    rows_in = spread(ring, "tp", TP).reshape(TP * Z * own_rows, width + HD)
    ids = jnp.stack([group, (1 - pool) * TP + tp]).astype(jnp.int32)
    mixed = ffn(ids, rows_in, mine, other)

    mixed = exchange(mixed.reshape(TP, Z * own_rows, width), "tp")
    mixed = jnp.sum(mixed.astype(F32), axis=0).astype(BF16)
    mixed = exchange(mixed.reshape(Z, own_rows, width), RING)
    mixture = jnp.sum(mixed.astype(F32), axis=0)
    block_out = (resid + modulation[3] * mixture).astype(BF16)
    block_out = block_out.reshape(own_rows, 2 * TP, width // (2 * TP)).transpose(1, 0, 2)
    return exchange(block_out, GROUP).reshape(rows, width // (2 * TP))


def solution(mesh):
    split = Mesh(
        mesh.devices.reshape(2, Y, ZHI, ZLO, TP), ("pool", "y", "zhi", "zlo", "tp")
    )
    seq = ("y", "zhi", "zlo")
    in_specs = (
        P(seq, None),
        P(seq, GROUP),
        P(seq, GROUP),
        P(seq, GROUP),
        P(GROUP, None),
        P(),
        P(seq, None),
        P(seq, None),
        P(GROUP, None, seq),
        P(GROUP, None, seq),
        P(GROUP, seq, None),
    )
    return jax.shard_map(
        body, mesh=split, in_specs=in_specs, out_specs=P(seq, GROUP), check_vma=False
    )
```

time: 230 us -> 211 us (0.917)
  waiting for transfers between devices: 57 us -> 38.6 us
  starting transfers between devices: 46.8 us -> 56.3 us
  Pallas kernels: 17.1 us -> 9.51 us
    all_to_all x3 -> x0, waiting for transfers between devices: 44 us -> none  [spread(): return lax.all_to_all(copies, axis, split_axis=0, concat_axis=0, tiled=True)]
    all_to_all x1 -> x0, blocking collectives: 24.8 us -> none  [spread(): return lax.all_to_all(copies, axis, split_axis=0, concat_axis=0, tiled=True)]
    all_to_all x2 -> x4, waiting for transfers between devices: 13 us -> 36.5 us  [exchange(): return lax.all_to_all(x, axis, split_axis=0, concat_axis=0, tiled=True)]
    all_to_all x3 -> x0, starting transfers between devices: 23.5 us -> none  [spread(): return lax.all_to_all(copies, axis, split_axis=0, concat_axis=0, tiled=True)]
    all_to_all x3 -> x4, blocking collectives: 54.8 us -> 77.9 us  [exchange(): return lax.all_to_all(x, axis, split_axis=0, concat_axis=0, tiled=True)]
    ppermute x0 -> x3, starting transfers between devices: none -> 21.9 us  [body(): lax.ppermute(query_proj, 'zhi', [(i, (i - k) % ZHI) for i in range(ZHI)])]
    all_to_all x2 -> x4, starting transfers between devices: 16.3 us -> 27.4 us  [exchange(): return lax.all_to_all(x, axis, split_axis=0, concat_axis=0, tiled=True)]
    pallas_call x1, Pallas kernels: 17.1 us -> 9.51 us  [ffn(): pl.pallas_call(ffn_kernel, grid=(parts // each,), out_shape=jax.ShapeDtyp...]
  transfers between devices with their start and end apart: 7 -> 9, of which waited for: 5 -> 4; matrix products, arithmetic and copies ran while one was open for 4% -> 4% of each run, Pallas kernels for 0% -> 0%
where the time goes in v3:
time: 211 us; the launch traced here: 210 us
  blocking collectives  77.9 us (37%)
  starting transfers between devices  56.3 us (27%)
  waiting for transfers between devices  38.6 us (18%)
  between operations  13.7 us (6%)
  Pallas kernels  9.51 us (5%)
  local copies, waits for them, and re-layouts  6.7 us (3%)
  other arithmetic  6.11 us (3%)
    all_to_all x4, blocking collectives, exchange(): return lax.all_to_all(x, axis, split_axis=0, concat_axis=0, tiled=True)  77.9 us
    all_to_all x4, waiting for transfers between devices, exchange(): return lax.all_to_all(x, axis, split_axis=0, concat_axis=0, tiled=True)  36.5 us
    all_to_all x4, starting transfers between devices, exchange(): return lax.all_to_all(x, axis, split_axis=0, concat_axis=0, tiled=True)  27.4 us
    ppermute x3, starting transfers between devices, body(): lax.ppermute(query_proj, 'zhi', [(i, (i - k) % ZHI) for i in range(ZHI)])  21.9 us
    pallas_call x1, Pallas kernels, ffn(): pl.pallas_call(ffn_kernel, grid=(parts // each,), out_shape=jax.ShapeDtyp...  9.51 us
    ppermute x1, starting transfers between devices, body(): other = lax.ppermute(mine, 'pool', [(0, 1), (1, 0)])  6.96 us
  transfers between devices with their start and end apart: 9, of which 4 were waited for; matrix products, arithmetic and copies ran while one was open for 4% of the time, Pallas kernels for 0%

profile of v3, /device:TPU:1, one launch (start us, length us, event | category | flops | bytes accessed | tf_op | source)
XLA Modules:
  0.0 210.3 jit_solution(14725705431670289953)
XLA Ops:
  6.5 2.9 %fusion.5 = bf16[336,2560]{1,0:T(8,128)(2,1)} fusion(bf16[108,2560]{1,0:T(8,128)(2,1)} %bitcast.40, bf16[108,2560]{1,0:T(8,128)(2,1)} %bitcast.41, bf16[108,2560]{1,0:T(8,128)(2,1)} %bitcast.42), kind=kLoop, calls=%fused_computation.10 | loop fusion | flops 12042240 | bytes 3379200 | tf_op jit(solution)/shard_map/concatenate | solution.py:37
  9.4 0.7 copy-done.4
  10.1 0.9 broadcast_in_dim.6
  11.0 9.2 %all-to-all-start = ((bf16[16,32,512]{2,1,0:T(8,128)(2,1)}), bf16[16,32,512]{2,1,0:T(8,128)(2,1)S(1)}, u32[]{:S(2)}, u32[]{:S(2)}) async-start(bf16[16,32,512]{2,1,0:T(8,128)(2,1)} %broadcast_in_dim.6), calls=%async_computation | async-start | bytes 1048576 | tf_op jit(solution)/shard_map/all_to_all | solution.py:32
  20.2 12.7 %collective-permute-start.1 = (bf16[32,256]{1,0:T(8,128)(2,1)S(1)}, bf16[32,256]{1,0:T(8,128)(2,1)S(1)}, u32[]{:S(2)}, u32[]{:S(2)}) collective-permute-start(bf16[32,256]{1,0:T(8,128)(2,1)S(1)} %copy-done.2), channel_id=1, source_target_pairs={{0,32},{16,48},{32,0},{48,16},{1,33},{17,49},{33,1},{49,17},{2,34}... | collective-permute-start | bytes 49160 | tf_op jit(solution)/shard_map/ppermute | solution.py:138
  33.0 3.1 %collective-permute-start = (bf16[32,256]{1,0:T(8,128)(2,1)S(1)}, bf16[32,256]{1,0:T(8,128)(2,1)S(1)}, u32[]{:S(2)}, u32[]{:S(2)}) collective-permute-start(bf16[32,256]{1,0:T(8,128)(2,1)S(1)} %copy-done.2), channel_id=1, source_target_pairs={{0,48},{16,0},{32,16},{48,32},{1,49},{17,1},{33,17},{49,33},{2,50}... | collective-permute-start | bytes 49160 | tf_op jit(solution)/shard_map/ppermute | solution.py:138
  36.1 6.1 %collective-permute-start.2 = (bf16[32,256]{1,0:T(8,128)(2,1)S(1)}, bf16[32,256]{1,0:T(8,128)(2,1)S(1)}, u32[]{:S(2)}, u32[]{:S(2)}) collective-permute-start(bf16[32,256]{1,0:T(8,128)(2,1)S(1)} %copy-done.2), channel_id=1, source_target_pairs={{0,16},{16,32},{32,48},{48,0},{1,17},{17,33},{33,49},{49,1},{2,18}... | collective-permute-start | bytes 49160 | tf_op jit(solution)/shard_map/ppermute | solution.py:138
  42.3 0.1 copy.41
  42.4 2.0 collective-permute-done.2
  44.5 0.3 fusion.43
  44.7 0.2 fusion.10
  44.9 0.3 fusion.42
  45.2 0.2 fusion.8
  45.5 0.3 fusion.7
  45.8 0.3 fusion.6
  46.1 0.7 copy.36
  46.8 7.3 %all-to-all-start.1 = ((bf16[4,32,384]{2,1,0:T(8,128)(2,1)}), bf16[4,32,384]{2,1,0:T(8,128)(2,1)S(1)}, u32[]{:S(2)}, u32[]{:S(2)}) async-start(bf16[4,32,384]{2,1,0:T(8,128)(2,1)} %bitcast.3), calls=%async_computation.1 | async-start | bytes 196608 | tf_op jit(solution)/shard_map/all_to_all | solution.py:32
  54.2 0.1 copy.42
  54.3 12.7 %all-to-all-done.1 = bf16[4,32,384]{2,1,0:T(8,128)(2,1)S(1)} async-done(((bf16[4,32,384]{2,1,0:T(8,128)(2,1)}), bf16[4,32,384]{2,1,0:T(8,128)(2,1)S(1)}, u32[]{:S(2)}, u32[]{:S(2)}) %all-to-all-start.1) | async-done | bytes 98336 | tf_op jit(solution)/shard_map/all_to_all | solution.py:32
  67.0 0.2 slice_reduce_fusion.1
  67.2 0.1 fusion.23
  67.3 0.1 divide_convert_fusion.1
  67.4 0.1 divide_convert_fusion
  67.5 0.3 convolution_convert_fusion
  67.8 0.7 reshape.206
  68.6 7.4 %all-to-all-start.2 = ((bf16[8,4,2560]{2,1,0:T(4,128)(2,1)}), bf16[8,4,2560]{2,1,0:T(4,128)(2,1)S(1)}, u32[]{:S(2)}, u32[]{:S(2)}) async-start(bf16[8,4,2560]{2,1,0:T(4,128)(2,1)} %reshape.206), calls=%async_computation.2 | async-start | bytes 327680 | tf_op jit(solution)/shard_map/all_to_all | solution.py:32
  76.0 0.1 slice_reduce_fusion.3
  76.2 5.7 %all-to-all-done.2 = bf16[8,4,2560]{2,1,0:T(4,128)(2,1)S(1)} async-done(((bf16[8,4,2560]{2,1,0:T(4,128)(2,1)}), bf16[8,4,2560]{2,1,0:T(4,128)(2,1)S(1)}, u32[]{:S(2)}, u32[]{:S(2)}) %all-to-all-start.2) | async-done | bytes 163872 | tf_op jit(solution)/shard_map/all_to_all | solution.py:32
  82.0 0.9 fusion.39
  82.9 0.1 add_convert_fusion.1
  83.0 0.1 broadcast_in_dim.7
  83.1 23.1 %all_to_all.40 = bf16[16,4,2688]{2,1,0:T(4,128)(2,1)S(1)} all-to-all(bf16[16,4,2688]{2,1,0:T(4,128)(2,1)S(1)} %broadcast_in_dim.7), channel_id=1, replica_groups=mesh['pool'=2,'y'=4,'zhi'=4,'zlo'=4,'tp'=4] {'zhi','zlo'}, dimensions={0} | all-to-all | bytes 688128 | tf_op jit(solution)/shard_map/all_to_all | solution.py:32
  106.2 0.1 reshape.207
  106.3 7.0 %collective-permute-start.3 = (bf16[4,336,2560]{2,1,0:T(8,128)(2,1)}, bf16[4,336,2560]{2,1,0:T(8,128)(2,1)}, u32[]{:S(2)}, u32[]{:S(2)}) collective-permute-start(bf16[4,336,2560]{2,1,0:T(8,128)(2,1)} %bitcast.32), channel_id=1, source_target_pairs={{0,256},{256,0},{1,257},{257,1},{2,258},{258,2},{3,259},{259,3},{4... | collective-permute-start | bytes 20643848 | tf_op jit(solution)/shard_map/ppermute | solution.py:199
  113.3 1.2 broadcast_in_dim.8
  114.5 3.5 %all-to-all-start.4 = ((bf16[4,64,2688]{2,1,0:T(8,128)(2,1)}), bf16[4,64,2688]{2,1,0:T(8,128)(2,1)S(1)}, u32[]{:S(2)}, u32[]{:S(2)}) async-start(bf16[4,64,2688]{2,1,0:T(8,128)(2,1)} %broadcast_in_dim.8), calls=%async_computation.4 | async-start | bytes 2752512 | tf_op jit(solution)/shard_map/all_to_all | solution.py:32
  118.0 0.6 pad_add_fusion.ids_ref
  118.6 18.1 %all-to-all-done.4 = bf16[4,64,2688]{2,1,0:T(8,128)(2,1)S(1)} async-done(((bf16[4,64,2688]{2,1,0:T(8,128)(2,1)}), bf16[4,64,2688]{2,1,0:T(8,128)(2,1)S(1)}, u32[]{:S(2)}, u32[]{:S(2)}) %all-to-all-start.4) | async-done | bytes 1376288 | tf_op jit(solution)/shard_map/all_to_all | solution.py:32
  136.8 1.1 copy-done.1
  137.8 9.5 %shard_map.109 = bf16[256,2560]{1,0:T(8,128)(2,1)} custom-call(s32[2]{0:T(128)} %pad_add_fusion.ids_ref, bf16[256,2688]{1,0:T(8,128)(2,1)} %bitcast.34, bf16[4,336,2560]{2,1,0:T(8,128)(2,1)} %bitcast.33, bf16[4,336,2560]{2,1,0:T(8,128)(2,1)} %collective-permute-done.3.other_ref), custom_call_target="tpu_custom_call" | custom-call | flops 3523215360 | bytes 13762560 | tf_op jit(solution)/shard_map/pallas_call | solution.py:90
  147.4 20.4 %all_to_all.41 = bf16[4,64,2560]{2,1,0:T(8,128)(2,1)S(1)} all-to-all(bf16[4,64,2560]{2,1,0:T(8,128)(2,1)} %bitcast.35), channel_id=1, replica_groups=mesh['pool'=2,'y'=4,'zhi'=4,'zlo'=4,'tp'=4] {'tp'}, dimensions={0} | all-to-all | bytes 2621440 | tf_op jit(solution)/shard_map/all_to_all | solution.py:32
  167.8 0.2 reduce_sum.131
  168.0 0.1 reshape.210
  168.1 19.0 %all_to_all.42 = bf16[16,4,2560]{2,1,0:T(4,128)(2,1)S(1)} all-to-all(bf16[16,4,2560]{2,1,0:T(4,128)(2,1)S(1)} %reshape.210), channel_id=1, replica_groups=mesh['pool'=2,'y'=4,'zhi'=4,'zlo'=4,'tp'=4] {'zhi','zlo'}, dimensions={0} | all-to-all | bytes 655360 | tf_op jit(solution)/shard_map/all_to_all | solution.py:32
  187.1 0.1 convert_reduce_fusion
  187.3 0.1 reshape.211
  187.4 15.4 %all_to_all.43 = bf16[8,4,320]{2,1,0:T(4,128)(2,1)S(1)} all-to-all(bf16[8,4,320]{2,1,0:T(4,128)(2,1)S(1)} %bitcast.43), channel_id=1, replica_groups=mesh['pool'=2,'y'=4,'zhi'=4,'zlo'=4,'tp'=4] {'pool','tp'}, dimensions={0} | all-to-all | bytes 40960 | tf_op jit(solution)/shard_map/all_to_all | solution.py:32
  202.8 0.6 reshape.212
  (47 shorter events, 0.6 us)
Async XLA Ops:
  6.5 61.0 %copy-start = (bf16[256,2560]{1,0:T(8,128)(2,1)S(1)}, bf16[256,2560]{1,0:T(8,128)(2,1)}, u32[]{:S(2)}) copy-start(bf16[256,2560]{1,0:T(8,128)(2,1)} %param.15) | copy-start | bytes 3932164
  6.5 99.8 %all-gather.3.cloned.1.call-start = ((), (), s32[]{:S(2)}) async-start(), calls=%async_computation.8 | async-start | bytes 8601600 | tf_op jit(solution)/shard_map/all_gather | solution.py:135
  9.4 0.7 copy-start.4
  9.4 0.7 copy-start.5
  9.4 10.8 %copy-start.2 = (bf16[32,256]{1,0:T(8,128)(2,1)S(1)}, bf16[32,256]{1,0:T(8,128)(2,1)}, u32[]{:S(2)}) copy-start(bf16[32,256]{1,0:T(8,128)(2,1)} %param.12) | copy-start | bytes 49156
  9.4 32.8 %copy-start.6 = (s32[32,2]{0,1:T(2,128)S(1)}, s32[32,2]{0,1:T(2,128)}, u32[]{:S(2)}) copy-start(s32[32,2]{0,1:T(2,128)} %param.17) | copy-start | bytes 772
  11.0 33.5 %all-to-all-start = ((bf16[16,32,512]{2,1,0:T(8,128)(2,1)}), bf16[16,32,512]{2,1,0:T(8,128)(2,1)S(1)}, u32[]{:S(2)}, u32[]{:S(2)}) async-start(bf16[16,32,512]{2,1,0:T(8,128)(2,1)} %broadcast_in_dim.6), calls=%async_computation | async-start | bytes 1048576 | tf_op jit(solution)/shard_map/all_to_all | solution.py:32
  20.2 33.9 %copy-start.7 = (f32[32,2]{0,1:T(2,128)S(1)}, f32[32,2]{0,1:T(2,128)}, u32[]{:S(2)}) copy-start(f32[32,2]{0,1:T(2,128)} %param.18) | copy-start | bytes 772
  20.2 22.2 %collective-permute-start.1 = (bf16[32,256]{1,0:T(8,128)(2,1)S(1)}, bf16[32,256]{1,0:T(8,128)(2,1)S(1)}, u32[]{:S(2)}, u32[]{:S(2)}) collective-permute-start(bf16[32,256]{1,0:T(8,128)(2,1)S(1)} %copy-done.2), channel_id=1, source_target_pairs={{0,32},{16,48},{32,0},{48,16},{1,33},{17,49},{33,1},{49,17},{2,34}... | collective-permute-start | bytes 49160 | tf_op jit(solution)/shard_map/ppermute | solution.py:138
  33.0 9.4 %collective-permute-start = (bf16[32,256]{1,0:T(8,128)(2,1)S(1)}, bf16[32,256]{1,0:T(8,128)(2,1)S(1)}, u32[]{:S(2)}, u32[]{:S(2)}) collective-permute-start(bf16[32,256]{1,0:T(8,128)(2,1)S(1)} %copy-done.2), channel_id=1, source_target_pairs={{0,48},{16,0},{32,16},{48,32},{1,49},{17,1},{33,17},{49,33},{2,50}... | collective-permute-start | bytes 49160 | tf_op jit(solution)/shard_map/ppermute | solution.py:138
  36.1 8.4 %collective-permute-start.2 = (bf16[32,256]{1,0:T(8,128)(2,1)S(1)}, bf16[32,256]{1,0:T(8,128)(2,1)S(1)}, u32[]{:S(2)}, u32[]{:S(2)}) collective-permute-start(bf16[32,256]{1,0:T(8,128)(2,1)S(1)} %copy-done.2), channel_id=1, source_target_pairs={{0,16},{16,32},{32,48},{48,0},{1,17},{17,33},{33,49},{49,1},{2,18}... | collective-permute-start | bytes 49160 | tf_op jit(solution)/shard_map/ppermute | solution.py:138
  46.1 30.0 %copy-start.3 = (f32[4,2560]{1,0:T(4,128)S(1)}, f32[4,2560]{1,0:T(4,128)}, u32[]{:S(2)}) copy-start(f32[4,2560]{1,0:T(4,128)} %param.16) | copy-start | bytes 122884
  46.8 20.2 %all-to-all-start.1 = ((bf16[4,32,384]{2,1,0:T(8,128)(2,1)}), bf16[4,32,384]{2,1,0:T(8,128)(2,1)S(1)}, u32[]{:S(2)}, u32[]{:S(2)}) async-start(bf16[4,32,384]{2,1,0:T(8,128)(2,1)} %bitcast.3), calls=%async_computation.1 | async-start | bytes 196608 | tf_op jit(solution)/shard_map/all_to_all | solution.py:32
  68.6 13.3 %all-to-all-start.2 = ((bf16[8,4,2560]{2,1,0:T(4,128)(2,1)}), bf16[8,4,2560]{2,1,0:T(4,128)(2,1)S(1)}, u32[]{:S(2)}, u32[]{:S(2)}) async-start(bf16[8,4,2560]{2,1,0:T(4,128)(2,1)} %reshape.206), calls=%async_computation.2 | async-start | bytes 327680 | tf_op jit(solution)/shard_map/all_to_all | solution.py:32
  106.3 30.4 %collective-permute-start.3 = (bf16[4,336,2560]{2,1,0:T(8,128)(2,1)}, bf16[4,336,2560]{2,1,0:T(8,128)(2,1)}, u32[]{:S(2)}, u32[]{:S(2)}) collective-permute-start(bf16[4,336,2560]{2,1,0:T(8,128)(2,1)} %bitcast.32), channel_id=1, source_target_pairs={{0,256},{256,0},{1,257},{257,1},{2,258},{258,2},{3,259},{259,3},{4... | collective-permute-start | bytes 20643848 | tf_op jit(solution)/shard_map/ppermute | solution.py:199
  114.5 22.3 %all-to-all-start.4 = ((bf16[4,64,2688]{2,1,0:T(8,128)(2,1)}), bf16[4,64,2688]{2,1,0:T(8,128)(2,1)S(1)}, u32[]{:S(2)}, u32[]{:S(2)}) async-start(bf16[4,64,2688]{2,1,0:T(8,128)(2,1)} %broadcast_in_dim.8), calls=%async_computation.4 | async-start | bytes 2752512 | tf_op jit(solution)/shard_map/all_to_all | solution.py:32
  136.8 1.1 copy-start.1
Sparse Core Ops, SparseCore 0:
  9.6 83.5 all-gather.2

commit v4 on v3

--- a/solution.py
+++ b/solution.py
@@ -10,10 +10,7 @@
 
 HD = 128
 Y = 4
-ZHI = 4
-ZLO = 4
-Z = ZHI * ZLO
-RING = ("zhi", "zlo")
+Z = 16
 TP = 4
 GROUP = ("pool", "tp")
 F32 = jnp.float32
@@ -134,16 +131,10 @@
 
     mine = lax.all_gather(pack_weights(w_gate[0], w_up[0], w_down[0]), "y", axis=0)
 
-    blocks = [query_proj] + [
-        lax.ppermute(query_proj, "zhi", [(i, (i - k) % ZHI) for i in range(ZHI)])
-        for k in range(1, ZHI)
-    ]
-    first = (ZHI - lax.axis_index("zhi")) % ZHI * rows
-    queries = lax.dynamic_slice_in_dim(
-        jnp.concatenate(blocks + blocks[: ZHI - 1], 0), first, ZHI * rows, 0
-    )
-    copies = copies_of(jnp.concatenate([key_proj, value_proj], 1), Y * ZLO)
-    key_value = exchange(copies, ("y", "zlo")).reshape(Y * ZLO * rows, 2 * heads * HD)
+    queries = spread(query_proj, "y", Y).reshape(Y * rows, heads * HD)
+    key_value = lax.all_gather(
+        jnp.concatenate([key_proj, value_proj], 1), "z", axis=0, tiled=True
+    )
     parts = []
     stats = []
     for h in range(heads):
@@ -164,8 +155,8 @@
         stats += [high, middle, log_sum - high - middle]
     stats = jnp.concatenate(stats, 1).astype(BF16)
     stats = jnp.pad(stats, ((0, 0), (0, HD - stats.shape[1])))
-    partial = jnp.concatenate(parts + [stats], 1).reshape(ZHI, rows, (heads + 1) * HD)
-    partial = exchange(partial, "zhi").astype(F32)
+    partial = jnp.concatenate(parts + [stats], 1).reshape(Y, rows, (heads + 1) * HD)
+    partial = exchange(partial, "y").astype(F32)
     outs = []
     for h in range(heads):
         log_sum = partial[:, :, heads * HD + 3 * h : heads * HD + 3 * h + 3]
@@ -194,7 +185,7 @@
     )
     route = jnp.pad(route, ((0, 0), (0, HD - route.shape[1])))
     sent = jnp.concatenate([normed, route], 1)
-    ring = spread(sent, RING, Z).reshape(Z * own_rows, width + HD)
+    ring = spread(sent, "z", Z).reshape(Z * own_rows, width + HD)
     mine, ring = lax.optimization_barrier((mine, ring))
     other = lax.ppermute(mine, "pool", [(0, 1), (1, 0)])
     rows_in = spread(ring, "tp", TP).reshape(TP * Z * own_rows, width + HD)
@@ -203,7 +194,7 @@
 
     mixed = exchange(mixed.reshape(TP, Z * own_rows, width), "tp")
     mixed = jnp.sum(mixed.astype(F32), axis=0).astype(BF16)
-    mixed = exchange(mixed.reshape(Z, own_rows, width), RING)
+    mixed = exchange(mixed.reshape(Z, own_rows, width), "z")
     mixture = jnp.sum(mixed.astype(F32), axis=0)
     block_out = (resid + modulation[3] * mixture).astype(BF16)
     block_out = block_out.reshape(own_rows, 2 * TP, width // (2 * TP)).transpose(1, 0, 2)
@@ -212,9 +203,9 @@
 
 def solution(mesh):
     split = Mesh(
-        mesh.devices.reshape(2, Y, ZHI, ZLO, TP), ("pool", "y", "zhi", "zlo", "tp")
-    )
-    seq = ("y", "zhi", "zlo")
+        mesh.devices.reshape(2, Y, Z, TP), ("pool", "y", "z", "tp")
+    )
+    seq = ("y", "z")
     in_specs = (
         P(seq, None),
         P(seq, GROUP),

time: 211 us -> 211 us (level)
  blocking collectives: 77.9 us -> 112 us
  starting transfers between devices: 56.3 us -> 32.3 us
  waiting for transfers between devices: 38.6 us -> 29.4 us
    all_gather x0 -> x1, blocking collectives: none -> 32.6 us  [body(): lax.all_gather(jnp.concatenate([key_proj, value_proj], 1), 'z', axis=0, t...]
    ppermute x3 -> x0, starting transfers between devices: 21.9 us -> none  [body(): lax.ppermute(query_proj, 'zhi', [(i, (i - k) % ZHI) for i in range(ZHI)])]
    all_to_all x4, waiting for transfers between devices: 36.5 us -> 29.3 us  [exchange(): return lax.all_to_all(x, axis, split_axis=0, concat_axis=0, tiled=True)]
  transfers between devices with their start and end apart: 9 -> 6, of which waited for: 4 -> 3; matrix products, arithmetic and copies ran while one was open for 4% -> 4% of each run, Pallas kernels for 0% -> 0%
where the time goes in v4:
time: 211 us; the launch traced here: 210 us
  blocking collectives  112 us (53%)
  starting transfers between devices  32.3 us (15%)
  waiting for transfers between devices  29.4 us (14%)
  between operations  13.6 us (6%)
  Pallas kernels  9.5 us (5%)
  local copies, waits for them, and re-layouts  6.42 us (3%)
  other arithmetic  5.89 us (3%)
    all_to_all x4, blocking collectives, exchange(): return lax.all_to_all(x, axis, split_axis=0, concat_axis=0, tiled=True)  79.4 us
    all_gather x1, blocking collectives, body(): lax.all_gather(jnp.concatenate([key_proj, value_proj], 1), 'z', axis=0, t...  32.6 us
    all_to_all x4, waiting for transfers between devices, exchange(): return lax.all_to_all(x, axis, split_axis=0, concat_axis=0, tiled=True)  29.3 us
    all_to_all x4, starting transfers between devices, exchange(): return lax.all_to_all(x, axis, split_axis=0, concat_axis=0, tiled=True)  25.4 us
    pallas_call x1, Pallas kernels, ffn(): pl.pallas_call(ffn_kernel, grid=(parts // each,), out_shape=jax.ShapeDtyp...  9.5 us
    ppermute x1, starting transfers between devices, body(): other = lax.ppermute(mine, 'pool', [(0, 1), (1, 0)])  6.96 us
  transfers between devices with their start and end apart: 6, of which 3 were waited for; matrix products, arithmetic and copies ran while one was open for 4% of the time, Pallas kernels for 0%

profile of v4, /device:TPU:1, one launch (start us, length us, event | category | flops | bytes accessed | tf_op | source)
XLA Modules:
  0.0 210.4 jit_solution(17490107220488862850)
XLA Ops:
  6.5 2.9 %fusion.5 = bf16[336,2560]{1,0:T(8,128)(2,1)} fusion(bf16[108,2560]{1,0:T(8,128)(2,1)} %bitcast.36, bf16[108,2560]{1,0:T(8,128)(2,1)} %bitcast.37, bf16[108,2560]{1,0:T(8,128)(2,1)} %bitcast.38), kind=kLoop, calls=%fused_computation.10 | loop fusion | flops 12042240 | bytes 3379200 | tf_op jit(solution)/shard_map/concatenate | solution.py:34
  9.4 0.7 copy-done.3
  10.1 0.6 broadcast_in_dim.6
  10.8 5.0 %all-to-all-start = ((bf16[4,32,256]{2,1,0:T(8,128)(2,1)}), bf16[4,32,256]{2,1,0:T(8,128)(2,1)S(1)}, u32[]{:S(2)}, u32[]{:S(2)}) async-start(bf16[4,32,256]{2,1,0:T(8,128)(2,1)} %broadcast_in_dim.6), calls=%async_computation | async-start | bytes 131072 | tf_op jit(solution)/shard_map/all_to_all | solution.py:29
  15.8 0.1 constant_dynamic-slice_fusion
  15.8 0.1 copy.42
  16.0 32.6 %all_gather.9 = bf16[512,512]{1,0:T(8,128)(2,1)S(1)} all-gather(bf16[32,512]{1,0:T(8,128)(2,1)S(1)} %pad_maximum_fusion), channel_id=1, replica_groups=mesh['pool'=2,'y'=4,'z'=16,'tp'=4] {'z'}, dimensions={0}, use_global_device_ids=true | all-gather | bytes 557056 | tf_op jit(solution)/shard_map/all_gather | solution.py:135
  48.6 0.2 fusion.42
  48.8 0.1 fusion.10
  48.9 0.2 fusion.41
  49.2 0.1 fusion.8
  49.3 0.2 fusion.7
  49.6 0.2 fusion.6
  49.8 0.7 copy.36
  50.6 4.3 %all-to-all-start.1 = ((bf16[4,32,384]{2,1,0:T(8,128)(2,1)}), bf16[4,32,384]{2,1,0:T(8,128)(2,1)S(1)}, u32[]{:S(2)}, u32[]{:S(2)}) async-start(bf16[4,32,384]{2,1,0:T(8,128)(2,1)} %bitcast.3), calls=%async_computation.1 | async-start | bytes 196608 | tf_op jit(solution)/shard_map/all_to_all | solution.py:29
  55.0 0.1 copy.41
  55.1 5.5 %all-to-all-done.1 = bf16[4,32,384]{2,1,0:T(8,128)(2,1)S(1)} async-done(((bf16[4,32,384]{2,1,0:T(8,128)(2,1)}), bf16[4,32,384]{2,1,0:T(8,128)(2,1)S(1)}, u32[]{:S(2)}, u32[]{:S(2)}) %all-to-all-start.1) | async-done | bytes 98336 | tf_op jit(solution)/shard_map/all_to_all | solution.py:29
  60.6 0.2 slice_reduce_fusion.1
  60.9 0.1 fusion.23
  61.0 0.1 divide_convert_fusion.1
  61.0 0.1 divide_convert_fusion
  61.1 0.3 convolution_convert_fusion
  61.4 0.7 reshape.206
  62.2 12.5 %all-to-all-start.2 = ((bf16[8,4,2560]{2,1,0:T(4,128)(2,1)}), bf16[8,4,2560]{2,1,0:T(4,128)(2,1)S(1)}, u32[]{:S(2)}, u32[]{:S(2)}) async-start(bf16[8,4,2560]{2,1,0:T(4,128)(2,1)} %reshape.206), calls=%async_computation.2 | async-start | bytes 327680 | tf_op jit(solution)/shard_map/all_to_all | solution.py:29
  74.6 0.1 fusion.34
  74.7 0.1 slice_reduce_fusion.3
  74.8 5.7 %all-to-all-done.2 = bf16[8,4,2560]{2,1,0:T(4,128)(2,1)S(1)} async-done(((bf16[8,4,2560]{2,1,0:T(4,128)(2,1)}), bf16[8,4,2560]{2,1,0:T(4,128)(2,1)S(1)}, u32[]{:S(2)}, u32[]{:S(2)}) %all-to-all-start.2) | async-done | bytes 163872 | tf_op jit(solution)/shard_map/all_to_all | solution.py:29
  80.6 0.1 convert_reduce_fusion.1
  80.6 0.9 fusion.38
  81.6 0.1 add_convert_fusion.1
  81.7 0.1 broadcast_in_dim.7
  81.8 24.5 %all_to_all.40 = bf16[16,4,2688]{2,1,0:T(4,128)(2,1)S(1)} all-to-all(bf16[16,4,2688]{2,1,0:T(4,128)(2,1)S(1)} %broadcast_in_dim.7), channel_id=1, replica_groups=mesh['pool'=2,'y'=4,'z'=16,'tp'=4] {'z'}, dimensions={0} | all-to-all | bytes 688128 | tf_op jit(solution)/shard_map/all_to_all | solution.py:29
  106.3 0.1 reshape.207
  106.5 7.0 %collective-permute-start = (bf16[4,336,2560]{2,1,0:T(8,128)(2,1)}, bf16[4,336,2560]{2,1,0:T(8,128)(2,1)}, u32[]{:S(2)}, u32[]{:S(2)}) collective-permute-start(bf16[4,336,2560]{2,1,0:T(8,128)(2,1)} %bitcast.32), channel_id=1, source_target_pairs={{0,256},{256,0},{1,257},{257,1},{2,258},{258,2},{3,259},{259,3},{4... | collective-permute-start | bytes 20643848 | tf_op jit(solution)/shard_map/ppermute | solution.py:190
  113.4 1.2 broadcast_in_dim.8
  114.6 3.5 %all-to-all-start.4 = ((bf16[4,64,2688]{2,1,0:T(8,128)(2,1)}), bf16[4,64,2688]{2,1,0:T(8,128)(2,1)S(1)}, u32[]{:S(2)}, u32[]{:S(2)}) async-start(bf16[4,64,2688]{2,1,0:T(8,128)(2,1)} %broadcast_in_dim.8), calls=%async_computation.4 | async-start | bytes 2752512 | tf_op jit(solution)/shard_map/all_to_all | solution.py:29
  118.2 0.6 pad_add_fusion.ids_ref
  118.8 18.1 %all-to-all-done.4 = bf16[4,64,2688]{2,1,0:T(8,128)(2,1)S(1)} async-done(((bf16[4,64,2688]{2,1,0:T(8,128)(2,1)}), bf16[4,64,2688]{2,1,0:T(8,128)(2,1)S(1)}, u32[]{:S(2)}, u32[]{:S(2)}) %all-to-all-start.4) | async-done | bytes 1376288 | tf_op jit(solution)/shard_map/all_to_all | solution.py:29
  136.9 1.1 copy-done.1
  138.0 9.5 %shard_map.109 = bf16[256,2560]{1,0:T(8,128)(2,1)} custom-call(s32[2]{0:T(128)} %pad_add_fusion.ids_ref, bf16[256,2688]{1,0:T(8,128)(2,1)} %bitcast.34, bf16[4,336,2560]{2,1,0:T(8,128)(2,1)} %bitcast.33, bf16[4,336,2560]{2,1,0:T(8,128)(2,1)} %collective-permute-done.other_ref), custom_call_target="tpu_custom_call" | custom-call | flops 3523215360 | bytes 13762560 | tf_op jit(solution)/shard_map/pallas_call | solution.py:87
  147.5 20.4 %all_to_all.41 = bf16[4,64,2560]{2,1,0:T(8,128)(2,1)S(1)} all-to-all(bf16[4,64,2560]{2,1,0:T(8,128)(2,1)} %bitcast.35), channel_id=1, replica_groups=mesh['pool'=2,'y'=4,'z'=16,'tp'=4] {'tp'}, dimensions={0} | all-to-all | bytes 2621440 | tf_op jit(solution)/shard_map/all_to_all | solution.py:29
  167.9 0.2 reduce_sum.131
  168.1 0.1 reshape.210
  168.2 19.0 %all_to_all.42 = bf16[16,4,2560]{2,1,0:T(4,128)(2,1)S(1)} all-to-all(bf16[16,4,2560]{2,1,0:T(4,128)(2,1)S(1)} %reshape.210), channel_id=1, replica_groups=mesh['pool'=2,'y'=4,'z'=16,'tp'=4] {'z'}, dimensions={0} | all-to-all | bytes 655360 | tf_op jit(solution)/shard_map/all_to_all | solution.py:29
  187.2 0.1 convert_reduce_fusion
  187.4 0.1 reshape.211
  187.5 15.4 %all_to_all.43 = bf16[8,4,320]{2,1,0:T(4,128)(2,1)S(1)} all-to-all(bf16[8,4,320]{2,1,0:T(4,128)(2,1)S(1)} %bitcast.41), channel_id=1, replica_groups=mesh['pool'=2,'y'=4,'z'=16,'tp'=4] {'pool','tp'}, dimensions={0} | all-to-all | bytes 40960 | tf_op jit(solution)/shard_map/all_to_all | solution.py:29
  202.9 0.6 reshape.212
  (35 shorter events, 0.4 us)
Async XLA Ops:
  6.5 54.6 %copy-start = (bf16[256,2560]{1,0:T(8,128)(2,1)S(1)}, bf16[256,2560]{1,0:T(8,128)(2,1)}, u32[]{:S(2)}) copy-start(bf16[256,2560]{1,0:T(8,128)(2,1)} %param.15) | copy-start | bytes 3932164
  6.5 99.9 %all-gather.3.cloned.1.call-start = ((), (), s32[]{:S(2)}) async-start(), calls=%async_computation.8 | async-start | bytes 8601600 | tf_op jit(solution)/shard_map/all_gather | solution.py:132
  9.4 0.7 copy-start.3
  9.4 6.4 %copy-start.6 = (f32[32,2]{0,1:T(2,128)S(1)}, f32[32,2]{0,1:T(2,128)}, u32[]{:S(2)}) copy-start(f32[32,2]{0,1:T(2,128)} %param.18) | copy-start | bytes 772
  9.4 6.5 %copy-start.4 = (bf16[32,256]{1,0:T(8,128)(2,1)S(1)}, bf16[32,256]{1,0:T(8,128)(2,1)}, u32[]{:S(2)}) copy-start(bf16[32,256]{1,0:T(8,128)(2,1)} %param.14) | copy-start | bytes 49156
  9.4 6.5 %copy-start.5 = (bf16[32,256]{1,0:T(8,128)(2,1)S(1)}, bf16[32,256]{1,0:T(8,128)(2,1)}, u32[]{:S(2)}) copy-start(bf16[32,256]{1,0:T(8,128)(2,1)} %param.13) | copy-start | bytes 49156
  10.8 37.8 %all-to-all-start = ((bf16[4,32,256]{2,1,0:T(8,128)(2,1)}), bf16[4,32,256]{2,1,0:T(8,128)(2,1)S(1)}, u32[]{:S(2)}, u32[]{:S(2)}) async-start(bf16[4,32,256]{2,1,0:T(8,128)(2,1)} %broadcast_in_dim.6), calls=%async_computation | async-start | bytes 131072 | tf_op jit(solution)/shard_map/all_to_all | solution.py:29
  15.9 39.0 %copy-start.7 = (s32[32,2]{0,1:T(2,128)S(1)}, s32[32,2]{0,1:T(2,128)}, u32[]{:S(2)}) copy-start(s32[32,2]{0,1:T(2,128)} %param.17) | copy-start | bytes 772
  49.8 24.9 %copy-start.2 = (f32[4,2560]{1,0:T(4,128)S(1)}, f32[4,2560]{1,0:T(4,128)}, u32[]{:S(2)}) copy-start(f32[4,2560]{1,0:T(4,128)} %param.16) | copy-start | bytes 122884
  50.6 10.0 %all-to-all-start.1 = ((bf16[4,32,384]{2,1,0:T(8,128)(2,1)}), bf16[4,32,384]{2,1,0:T(8,128)(2,1)S(1)}, u32[]{:S(2)}, u32[]{:S(2)}) async-start(bf16[4,32,384]{2,1,0:T(8,128)(2,1)} %bitcast.3), calls=%async_computation.1 | async-start | bytes 196608 | tf_op jit(solution)/shard_map/all_to_all | solution.py:29
  62.2 18.4 %all-to-all-start.2 = ((bf16[8,4,2560]{2,1,0:T(4,128)(2,1)}), bf16[8,4,2560]{2,1,0:T(4,128)(2,1)S(1)}, u32[]{:S(2)}, u32[]{:S(2)}) async-start(bf16[8,4,2560]{2,1,0:T(4,128)(2,1)} %reshape.206), calls=%async_computation.2 | async-start | bytes 327680 | tf_op jit(solution)/shard_map/all_to_all | solution.py:29
  106.5 30.4 %collective-permute-start = (bf16[4,336,2560]{2,1,0:T(8,128)(2,1)}, bf16[4,336,2560]{2,1,0:T(8,128)(2,1)}, u32[]{:S(2)}, u32[]{:S(2)}) collective-permute-start(bf16[4,336,2560]{2,1,0:T(8,128)(2,1)} %bitcast.32), channel_id=1, source_target_pairs={{0,256},{256,0},{1,257},{257,1},{2,258},{258,2},{3,259},{259,3},{4... | collective-permute-start | bytes 20643848 | tf_op jit(solution)/shard_map/ppermute | solution.py:190
  114.6 22.3 %all-to-all-start.4 = ((bf16[4,64,2688]{2,1,0:T(8,128)(2,1)}), bf16[4,64,2688]{2,1,0:T(8,128)(2,1)S(1)}, u32[]{:S(2)}, u32[]{:S(2)}) async-start(bf16[4,64,2688]{2,1,0:T(8,128)(2,1)} %broadcast_in_dim.8), calls=%async_computation.4 | async-start | bytes 2752512 | tf_op jit(solution)/shard_map/all_to_all | solution.py:29
  136.9 1.1 copy-start.1
Sparse Core Ops, SparseCore 0:
  9.6 84.6 all-gather.2

commit v5 on v4

--- a/solution.py
+++ b/solution.py
@@ -23,6 +23,11 @@
 
 def spread(x, axis, count):
     return exchange(copies_of(x, count), axis)
+
+
+def shift(x, axis, count):
+    size = lax.axis_size(axis)
+    return lax.ppermute(x, axis, [(i, (i + count) % size) for i in range(size)])
 
 
 def exchange(x, axis):
@@ -129,12 +134,19 @@
     tp = lax.axis_index("tp")
     group = pool * TP + tp
 
-    mine = lax.all_gather(pack_weights(w_gate[0], w_up[0], w_down[0]), "y", axis=0)
-
-    queries = spread(query_proj, "y", Y).reshape(Y * rows, heads * HD)
-    key_value = lax.all_gather(
-        jnp.concatenate([key_proj, value_proj], 1), "z", axis=0, tiled=True
-    )
+    key_value = spread(jnp.concatenate([key_proj, value_proj], 1), "z", Z)
+    key_value = key_value.reshape(Z * rows, 2 * heads * HD)
+    blocks = [query_proj] + [shift(query_proj, "y", -k) for k in range(1, Y)]
+    first = (Y - lax.axis_index("y")) % Y * rows
+    queries = lax.dynamic_slice_in_dim(
+        jnp.concatenate(blocks + blocks[: Y - 1], 0), first, Y * rows, 0
+    )
+
+    w_gate, w_up, w_down, queries = lax.optimization_barrier((w_gate, w_up, w_down, queries))
+    packed = pack_weights(w_gate[0], w_up[0], w_down[0])
+    before = shift(packed, "y", 1)
+    after = shift(packed, "y", -1)
+
     parts = []
     stats = []
     for h in range(heads):
@@ -167,7 +179,11 @@
     heads_out = jnp.concatenate(outs, 1).astype(BF16)
 
     projected = jnp.dot(heads_out, w_out, preferred_element_type=F32).astype(BF16)
-    projected = exchange(projected.reshape(2 * TP, own_rows, width), GROUP)
+    projected = projected.reshape(2 * TP, own_rows, width)
+    before, after, projected = lax.optimization_barrier((before, after, projected))
+    split = packed.shape[0] * 2 // 3
+    across = [shift(before[:split], "y", 1), shift(after[split:], "y", -1)]
+    projected = exchange(projected, GROUP)
     attention = jnp.sum(projected.astype(F32), axis=0)
     own_tokens = lax.dynamic_slice_in_dim(tokens, group * own_rows, own_rows, 0).astype(F32)
     resid = own_tokens + modulation[0] * attention
@@ -185,10 +201,13 @@
     )
     route = jnp.pad(route, ((0, 0), (0, HD - route.shape[1])))
     sent = jnp.concatenate([normed, route], 1)
-    ring = spread(sent, "z", Z).reshape(Z * own_rows, width + HD)
-    mine, ring = lax.optimization_barrier((mine, ring))
+    copies = copies_of(exchange(copies_of(sent, Z), "z").reshape(Z * own_rows, width + HD), TP)
+    packed, before, after, *across, copies = lax.optimization_barrier(
+        (packed, before, after, *across, copies)
+    )
+    mine = jnp.concatenate([packed, before, after, *across], 0).reshape(Y, -1, width)
     other = lax.ppermute(mine, "pool", [(0, 1), (1, 0)])
-    rows_in = spread(ring, "tp", TP).reshape(TP * Z * own_rows, width + HD)
+    rows_in = exchange(copies, "tp").reshape(TP * Z * own_rows, width + HD)
     ids = jnp.stack([group, (1 - pool) * TP + tp]).astype(jnp.int32)
     mixed = ffn(ids, rows_in, mine, other)
 

time: 211 us -> 251 us (1.19)
  blocking collectives: 112 us -> 60.9 us
  waiting for transfers between devices: 29.4 us -> 67.5 us
  starting transfers between devices: 32.3 us -> 67.7 us
  local copies, waits for them, and re-layouts: 6.42 us -> 29.3 us
  between operations: 13.6 us -> 0.27 us
  other arithmetic: 5.89 us -> 9.73 us
  matrix products: 1.26 us -> 4.48 us
    all_gather x1 -> x0, blocking collectives: 32.6 us -> none  [body(): lax.all_gather(jnp.concatenate([key_proj, value_proj], 1), 'z', axis=0, t...]
    ppermute x0 -> x7, starting transfers between devices: none -> 21.9 us  [shift(): return lax.ppermute(x, axis, [(i, (i + count) % size) for i in range(size)])]
    all_to_all x4 -> x5, waiting for transfers between devices: 29.3 us -> 50.6 us  [exchange(): return lax.all_to_all(x, axis, split_axis=0, concat_axis=0, tiled=True)]
    all_to_all x4 -> x3, blocking collectives: 79.4 us -> 60.9 us  [exchange(): return lax.all_to_all(x, axis, split_axis=0, concat_axis=0, tiled=True)]
    all_to_all x4 -> x5, starting transfers between devices: 25.4 us -> 42.4 us  [exchange(): return lax.all_to_all(x, axis, split_axis=0, concat_axis=0, tiled=True)]
    ppermute x0 -> x7, waiting for transfers between devices: none -> 16.8 us  [shift(): return lax.ppermute(x, axis, [(i, (i + count) % size) for i in range(size)])]
    unnamed x18 -> x22, local copies, waits for them, and re-layouts: 1.97 us -> 12.7 us
    slice x0 -> x2, local copies, waits for them, and re-layouts: none -> 4.28 us  [body(): across = [shift(before[:split], 'y', 1), shift(after[split:], 'y', -1)]]
  transfers between devices with their start and end apart: 6 -> 13, of which waited for: 3 -> 8; matrix products, arithmetic and copies ran while one was open for 4% -> 9% of each run, Pallas kernels for 0% -> 0%
where the time goes in v5:
time: 251 us; the launch traced here: 249 us
  starting transfers between devices  67.7 us (27%)
  waiting for transfers between devices  67.5 us (27%)
  blocking collectives  60.9 us (24%)
  local copies, waits for them, and re-layouts  29.3 us (12%)
  other arithmetic  9.73 us (4%)
  Pallas kernels  9.51 us (4%)
  matrix products  4.48 us (2%)
    all_to_all x3, blocking collectives, exchange(): return lax.all_to_all(x, axis, split_axis=0, concat_axis=0, tiled=True)  60.9 us
    all_to_all x5, waiting for transfers between devices, exchange(): return lax.all_to_all(x, axis, split_axis=0, concat_axis=0, tiled=True)  50.6 us
    all_to_all x5, starting transfers between devices, exchange(): return lax.all_to_all(x, axis, split_axis=0, concat_axis=0, tiled=True)  42.4 us
    ppermute x7, starting transfers between devices, shift(): return lax.ppermute(x, axis, [(i, (i + count) % size) for i in range(size)])  21.9 us
    ppermute x7, waiting for transfers between devices, shift(): return lax.ppermute(x, axis, [(i, (i + count) % size) for i in range(size)])  16.8 us
    unnamed x22, local copies, waits for them, and re-layouts  12.7 us
    pallas_call x1, Pallas kernels, ffn(): pl.pallas_call(ffn_kernel, grid=(parts // each,), out_shape=jax.ShapeDtyp...  9.51 us
  transfers between devices with their start and end apart: 13, of which 8 were waited for; matrix products, arithmetic and copies ran while one was open for 9% of the time, Pallas kernels for 0%

profile of v5, /device:TPU:1, one launch (start us, length us, event | category | flops | bytes accessed | tf_op | source)
XLA Modules:
  0.0 249.4 jit_solution(8925720016956713497)
XLA Ops:
  0.0 0.8 pad_maximum_fusion
  0.8 0.8 broadcast_in_dim.8
  1.7 15.7 %all-to-all-start = ((bf16[16,32,512]{2,1,0:T(8,128)(2,1)}), bf16[16,32,512]{2,1,0:T(8,128)(2,1)S(1)}, u32[]{:S(2)}, u32[]{:S(2)}) async-start(bf16[16,32,512]{2,1,0:T(8,128)(2,1)} %broadcast_in_dim.8), calls=%async_computation | async-start | bytes 1048576 | tf_op jit(solution)/shard_map/all_to_all | solution.py:34
  17.4 4.8 %collective-permute-start.1 = (bf16[32,256]{1,0:T(8,128)(2,1)}, bf16[32,256]{1,0:T(8,128)(2,1)S(1)}, u32[]{:S(2)}, u32[]{:S(2)}) collective-permute-start(bf16[32,256]{1,0:T(8,128)(2,1)} %param.12), channel_id=1, source_target_pairs={{0,128},{64,192},{128,0},{192,64},{1,129},{65,193},{129,1},{193,65... | collective-permute-start | bytes 49160 | tf_op jit(solution)/shard_map/ppermute | solution.py:30
  22.3 2.7 %collective-permute-start = (bf16[32,256]{1,0:T(8,128)(2,1)}, bf16[32,256]{1,0:T(8,128)(2,1)S(1)}, u32[]{:S(2)}, u32[]{:S(2)}) collective-permute-start(bf16[32,256]{1,0:T(8,128)(2,1)} %param.12), channel_id=1, source_target_pairs={{0,192},{64,0},{128,64},{192,128},{1,193},{65,1},{129,65},{193,129... | collective-permute-start | bytes 49160 | tf_op jit(solution)/shard_map/ppermute | solution.py:30
  25.0 2.6 %collective-permute-start.2 = (bf16[32,256]{1,0:T(8,128)(2,1)}, bf16[32,256]{1,0:T(8,128)(2,1)S(1)}, u32[]{:S(2)}, u32[]{:S(2)}) collective-permute-start(bf16[32,256]{1,0:T(8,128)(2,1)} %param.12), channel_id=1, source_target_pairs={{0,64},{64,128},{128,192},{192,0},{1,65},{65,129},{129,193},{193,1... | collective-permute-start | bytes 49160 | tf_op jit(solution)/shard_map/ppermute | solution.py:30
  29.8 1.4 collective-permute-done.2
  32.5 1.5 fusion.5
  34.0 2.5 %collective-permute-start.4 = (bf16[336,2560]{1,0:T(8,128)(2,1)S(1)}, bf16[336,2560]{1,0:T(8,128)(2,1)}, u32[]{:S(2)}, u32[]{:S(2)}) collective-permute-start(bf16[336,2560]{1,0:T(8,128)(2,1)S(1)} %fusion.5), channel_id=1, source_target_pairs={{0,192},{64,0},{128,64},{192,128},{1,193},{65,1},{129,65},{193,129... | collective-permute-start | bytes 5160968 | tf_op jit(solution)/shard_map/ppermute | solution.py:30
  36.6 2.8 %collective-permute-start.3 = (bf16[336,2560]{1,0:T(8,128)(2,1)S(1)}, bf16[336,2560]{1,0:T(8,128)(2,1)}, u32[]{:S(2)}, u32[]{:S(2)}) collective-permute-start(bf16[336,2560]{1,0:T(8,128)(2,1)S(1)} %fusion.5), channel_id=1, source_target_pairs={{0,64},{64,128},{128,192},{192,0},{1,65},{65,129},{129,193},{193,1... | collective-permute-start | bytes 5160968 | tf_op jit(solution)/shard_map/ppermute | solution.py:30
  39.3 0.9 all-to-all-done
  40.3 1.0 fusion.42
  41.5 0.9 fusion.7
  43.0 1.0 fusion.41
  45.5 1.3 concatenate.32
  46.8 1.2 fusion.6
  48.0 0.8 fusion.21
  48.8 0.8 copy.36
  49.6 4.2 %all-to-all-start.1 = ((bf16[4,32,384]{2,1,0:T(8,128)(2,1)}), bf16[4,32,384]{2,1,0:T(8,128)(2,1)S(1)}, u32[]{:S(2)}, u32[]{:S(2)}) async-start(bf16[4,32,384]{2,1,0:T(8,128)(2,1)} %bitcast.8), calls=%async_computation.1 | async-start | bytes 196608 | tf_op jit(solution)/shard_map/all_to_all | solution.py:34
  54.6 22.9 %all-to-all-done.1 = bf16[4,32,384]{2,1,0:T(8,128)(2,1)S(1)} async-done(((bf16[4,32,384]{2,1,0:T(8,128)(2,1)}), bf16[4,32,384]{2,1,0:T(8,128)(2,1)S(1)}, u32[]{:S(2)}, u32[]{:S(2)}) %all-to-all-start.1) | async-done | bytes 98336 | tf_op jit(solution)/shard_map/all_to_all | solution.py:34
  79.1 7.5 %all-to-all-start.2 = ((bf16[8,4,2560]{2,1,0:T(4,128)(2,1)}), bf16[8,4,2560]{2,1,0:T(4,128)(2,1)S(1)}, u32[]{:S(2)}, u32[]{:S(2)}) async-start(bf16[8,4,2560]{2,1,0:T(4,128)(2,1)} %reshape.206), calls=%async_computation.2 | async-start | bytes 327680 | tf_op jit(solution)/shard_map/all_to_all | solution.py:34
  87.3 1.0 slice_reduce_fusion.3
  88.4 3.7 %all-to-all-done.2 = bf16[8,4,2560]{2,1,0:T(4,128)(2,1)S(1)} async-done(((bf16[8,4,2560]{2,1,0:T(4,128)(2,1)}), bf16[8,4,2560]{2,1,0:T(4,128)(2,1)S(1)}, u32[]{:S(2)}, u32[]{:S(2)}) %all-to-all-start.2) | async-done | bytes 163872 | tf_op jit(solution)/shard_map/all_to_all | solution.py:34
  92.2 0.9 fusion.38
  93.3 0.8 broadcast_in_dim.9
  94.1 11.5 %all-to-all-start.3 = ((bf16[16,4,2688]{2,1,0:T(4,128)(2,1)}), bf16[16,4,2688]{2,1,0:T(4,128)(2,1)S(1)}, u32[]{:S(2)}, u32[]{:S(2)}) async-start(bf16[16,4,2688]{2,1,0:T(4,128)(2,1)} %broadcast_in_dim.9), calls=%async_computation.3 | async-start | bytes 688128 | tf_op jit(solution)/shard_map/all_to_all | solution.py:34
  105.6 2.4 slice.60
  107.9 1.9 collective-permute-start.5
  109.9 1.9 slice.61
  111.8 4.6 %collective-permute-start.6 = (bf16[112,2560]{1,0:T(8,128)(2,1)}, bf16[112,2560]{1,0:T(8,128)(2,1)}, u32[]{:S(2)}, u32[]{:S(2)}) collective-permute-start(bf16[112,2560]{1,0:T(8,128)(2,1)} %slice.61), channel_id=1, source_target_pairs={{0,192},{64,0},{128,64},{192,128},{1,193},{65,1},{129,65},{193,129... | collective-permute-start | bytes 1720328 | tf_op jit(solution)/shard_map/ppermute | solution.py:30
  116.3 5.0 %all-to-all-done.3 = bf16[16,4,2688]{2,1,0:T(4,128)(2,1)S(1)} async-done(((bf16[16,4,2688]{2,1,0:T(4,128)(2,1)}), bf16[16,4,2688]{2,1,0:T(4,128)(2,1)S(1)}, u32[]{:S(2)}, u32[]{:S(2)}) %all-to-all-start.3) | async-done | bytes 344096 | tf_op jit(solution)/shard_map/all_to_all | solution.py:34
  121.3 0.8 broadcast_in_dim.10
  122.1 5.9 %collective-permute-done.6 = bf16[112,2560]{1,0:T(8,128)(2,1)} collective-permute-done((bf16[112,2560]{1,0:T(8,128)(2,1)}, bf16[112,2560]{1,0:T(8,128)(2,1)}, u32[]{:S(2)}, u32[]{:S(2)}) %collective-permute-start.6) | collective-permute-done | bytes 573472 | tf_op jit(solution)/shard_map/ppermute | solution.py:30
  128.0 9.5 %collective-permute-done.5 = bf16[224,2560]{1,0:T(8,128)(2,1)} collective-permute-done((bf16[224,2560]{1,0:T(8,128)(2,1)}, bf16[224,2560]{1,0:T(8,128)(2,1)}, u32[]{:S(2)}, u32[]{:S(2)}) %collective-permute-start.5) | collective-permute-done | bytes 1146912 | tf_op jit(solution)/shard_map/ppermute | solution.py:30
  137.5 2.1 broadcast_in_dim.11
  139.7 1.3 constant_dynamic-update-slice_fusion.11
  141.0 2.8 %constant_dynamic-update-slice_fusion.10 = bf16[1344,2560]{1,0:T(8,128)(2,1)} fusion(bf16[1344,2560]{1,0:T(8,128)(2,1)} %constant_dynamic-update-slice_fusion.11, bf16[336,2560]{1,0:T(8,128)(2,1)} %collective-permute-done.3), kind=kLoop, calls=%fused_computation.57 | loop fusion | bytes 3440640
  143.8 2.8 %constant_dynamic-update-slice_fusion.9 = bf16[1344,2560]{1,0:T(8,128)(2,1)} fusion(bf16[1344,2560]{1,0:T(8,128)(2,1)} %constant_dynamic-update-slice_fusion.10, bf16[336,2560]{1,0:T(8,128)(2,1)} %collective-permute-done.4), kind=kLoop, calls=%fused_computation.56 | loop fusion | bytes 3440640
  146.6 2.4 constant_dynamic-update-slice_fusion.8
  149.0 1.9 constant_dynamic-update-slice_fusion.7
  150.9 3.4 %collective-permute-start.7 = (bf16[4,336,2560]{2,1,0:T(8,128)(2,1)}, bf16[4,336,2560]{2,1,0:T(8,128)(2,1)}, u32[]{:S(2)}, u32[]{:S(2)}) collective-permute-start(bf16[4,336,2560]{2,1,0:T(8,128)(2,1)} %bitcast.12.mine_ref), channel_id=1, source_target_pairs={{0,256},{256,0},{1,257},{257,1},{2,258},{258,2},{3,259},{259,3},{4... | collective-permute-start | bytes 20643848 | tf_op jit(solution)/shard_map/ppermute | solution.py:209
  154.3 3.6 %all-to-all-start.4 = ((bf16[4,64,2688]{2,1,0:T(8,128)(2,1)}), bf16[4,64,2688]{2,1,0:T(8,128)(2,1)S(1)}, u32[]{:S(2)}, u32[]{:S(2)}) async-start(bf16[4,64,2688]{2,1,0:T(8,128)(2,1)} %broadcast_in_dim.11), calls=%async_computation.4 | async-start | bytes 2752512 | tf_op jit(solution)/shard_map/all_to_all | solution.py:34
  158.5 18.1 %all-to-all-done.4 = bf16[4,64,2688]{2,1,0:T(8,128)(2,1)S(1)} async-done(((bf16[4,64,2688]{2,1,0:T(8,128)(2,1)}), bf16[4,64,2688]{2,1,0:T(8,128)(2,1)S(1)}, u32[]{:S(2)}, u32[]{:S(2)}) %all-to-all-start.4) | async-done | bytes 1376288 | tf_op jit(solution)/shard_map/all_to_all | solution.py:34
  176.6 1.1 copy-done.1
  177.7 9.5 %shard_map.109 = bf16[256,2560]{1,0:T(8,128)(2,1)} custom-call(s32[2]{0:T(128)} %pad_add_fusion.ids_ref, bf16[256,2688]{1,0:T(8,128)(2,1)} %bitcast.32, bf16[4,336,2560]{2,1,0:T(8,128)(2,1)} %bitcast.12.mine_ref, bf16[4,336,2560]{2,1,0:T(8,128)(2,1)} %collective-permute-done.7.other_ref), custom_call_target="tpu_custom_call" | custom-call | flops 3523215360 | bytes 13762560 | tf_op jit(solution)/shard_map/pallas_call | solution.py:92
  187.2 20.4 %all_to_all.40 = bf16[4,64,2560]{2,1,0:T(8,128)(2,1)S(1)} all-to-all(bf16[4,64,2560]{2,1,0:T(8,128)(2,1)} %bitcast.33), channel_id=1, replica_groups=mesh['pool'=2,'y'=4,'z'=16,'tp'=4] {'tp'}, dimensions={0} | all-to-all | bytes 2621440 | tf_op jit(solution)/shard_map/all_to_all | solution.py:34
  208.0 25.0 %all_to_all.41 = bf16[16,4,2560]{2,1,0:T(4,128)(2,1)S(1)} all-to-all(bf16[16,4,2560]{2,1,0:T(4,128)(2,1)S(1)} %reshape.210), channel_id=1, replica_groups=mesh['pool'=2,'y'=4,'z'=16,'tp'=4] {'z'}, dimensions={0} | all-to-all | bytes 655360 | tf_op jit(solution)/shard_map/all_to_all | solution.py:34
  233.3 15.4 %all_to_all.42 = bf16[8,4,320]{2,1,0:T(4,128)(2,1)S(1)} all-to-all(bf16[8,4,320]{2,1,0:T(4,128)(2,1)S(1)} %bitcast.41), channel_id=1, replica_groups=mesh['pool'=2,'y'=4,'z'=16,'tp'=4] {'pool','tp'}, dimensions={0} | all-to-all | bytes 40960 | tf_op jit(solution)/shard_map/all_to_all | solution.py:34
  (55 shorter events, 11.0 us)
Async XLA Ops:
  0.0 78.1 %copy-start = (bf16[256,2560]{1,0:T(8,128)(2,1)S(1)}, bf16[256,2560]{1,0:T(8,128)(2,1)}, u32[]{:S(2)}) copy-start(bf16[256,2560]{1,0:T(8,128)(2,1)} %param.15) | copy-start | bytes 3932164
  1.7 38.6 %all-to-all-start = ((bf16[16,32,512]{2,1,0:T(8,128)(2,1)}), bf16[16,32,512]{2,1,0:T(8,128)(2,1)S(1)}, u32[]{:S(2)}, u32[]{:S(2)}) async-start(bf16[16,32,512]{2,1,0:T(8,128)(2,1)} %broadcast_in_dim.8), calls=%async_computation | async-start | bytes 1048576 | tf_op jit(solution)/shard_map/all_to_all | solution.py:34
  17.4 12.3 %collective-permute-start.1 = (bf16[32,256]{1,0:T(8,128)(2,1)}, bf16[32,256]{1,0:T(8,128)(2,1)S(1)}, u32[]{:S(2)}, u32[]{:S(2)}) collective-permute-start(bf16[32,256]{1,0:T(8,128)(2,1)} %param.12), channel_id=1, source_target_pairs={{0,128},{64,192},{128,0},{192,64},{1,129},{65,193},{129,1},{193,65... | collective-permute-start | bytes 49160 | tf_op jit(solution)/shard_map/ppermute | solution.py:30
  22.3 7.5 %collective-permute-start = (bf16[32,256]{1,0:T(8,128)(2,1)}, bf16[32,256]{1,0:T(8,128)(2,1)S(1)}, u32[]{:S(2)}, u32[]{:S(2)}) collective-permute-start(bf16[32,256]{1,0:T(8,128)(2,1)} %param.12), channel_id=1, source_target_pairs={{0,192},{64,0},{128,64},{192,128},{1,193},{65,1},{129,65},{193,129... | collective-permute-start | bytes 49160 | tf_op jit(solution)/shard_map/ppermute | solution.py:30
  25.0 6.2 %collective-permute-start.2 = (bf16[32,256]{1,0:T(8,128)(2,1)}, bf16[32,256]{1,0:T(8,128)(2,1)S(1)}, u32[]{:S(2)}, u32[]{:S(2)}) collective-permute-start(bf16[32,256]{1,0:T(8,128)(2,1)} %param.12), channel_id=1, source_target_pairs={{0,64},{64,128},{128,192},{192,0},{1,65},{65,129},{129,193},{193,1... | collective-permute-start | bytes 49160 | tf_op jit(solution)/shard_map/ppermute | solution.py:30
  34.0 45.1 %collective-permute-start.4 = (bf16[336,2560]{1,0:T(8,128)(2,1)S(1)}, bf16[336,2560]{1,0:T(8,128)(2,1)}, u32[]{:S(2)}, u32[]{:S(2)}) collective-permute-start(bf16[336,2560]{1,0:T(8,128)(2,1)S(1)} %fusion.5), channel_id=1, source_target_pairs={{0,192},{64,0},{128,64},{192,128},{1,193},{65,1},{129,65},{193,129... | collective-permute-start | bytes 5160968 | tf_op jit(solution)/shard_map/ppermute | solution.py:30
  36.6 42.6 %collective-permute-start.3 = (bf16[336,2560]{1,0:T(8,128)(2,1)S(1)}, bf16[336,2560]{1,0:T(8,128)(2,1)}, u32[]{:S(2)}, u32[]{:S(2)}) collective-permute-start(bf16[336,2560]{1,0:T(8,128)(2,1)S(1)} %fusion.5), channel_id=1, source_target_pairs={{0,64},{64,128},{128,192},{192,0},{1,65},{65,129},{129,193},{193,1... | collective-permute-start | bytes 5160968 | tf_op jit(solution)/shard_map/ppermute | solution.py:30
  44.0 0.7 copy-start.2
  44.0 0.9 copy-start.3
  44.9 0.6 copy-start.4
  49.6 28.0 %all-to-all-start.1 = ((bf16[4,32,384]{2,1,0:T(8,128)(2,1)}), bf16[4,32,384]{2,1,0:T(8,128)(2,1)S(1)}, u32[]{:S(2)}, u32[]{:S(2)}) async-start(bf16[4,32,384]{2,1,0:T(8,128)(2,1)} %bitcast.8), calls=%async_computation.1 | async-start | bytes 196608 | tf_op jit(solution)/shard_map/all_to_all | solution.py:34
  79.1 13.0 %all-to-all-start.2 = ((bf16[8,4,2560]{2,1,0:T(4,128)(2,1)}), bf16[8,4,2560]{2,1,0:T(4,128)(2,1)S(1)}, u32[]{:S(2)}, u32[]{:S(2)}) async-start(bf16[8,4,2560]{2,1,0:T(4,128)(2,1)} %reshape.206), calls=%async_computation.2 | async-start | bytes 327680 | tf_op jit(solution)/shard_map/all_to_all | solution.py:34
  94.1 27.2 %all-to-all-start.3 = ((bf16[16,4,2688]{2,1,0:T(4,128)(2,1)}), bf16[16,4,2688]{2,1,0:T(4,128)(2,1)S(1)}, u32[]{:S(2)}, u32[]{:S(2)}) async-start(bf16[16,4,2688]{2,1,0:T(4,128)(2,1)} %broadcast_in_dim.9), calls=%async_computation.3 | async-start | bytes 688128 | tf_op jit(solution)/shard_map/all_to_all | solution.py:34
  107.9 29.6 %collective-permute-start.5 = (bf16[224,2560]{1,0:T(8,128)(2,1)}, bf16[224,2560]{1,0:T(8,128)(2,1)}, u32[]{:S(2)}, u32[]{:S(2)}) collective-permute-start(bf16[224,2560]{1,0:T(8,128)(2,1)} %slice.60), channel_id=1, source_target_pairs={{0,64},{64,128},{128,192},{192,0},{1,65},{65,129},{129,193},{193,1... | collective-permute-start | bytes 3440648 | tf_op jit(solution)/shard_map/ppermute | solution.py:30
  111.8 16.2 %collective-permute-start.6 = (bf16[112,2560]{1,0:T(8,128)(2,1)}, bf16[112,2560]{1,0:T(8,128)(2,1)}, u32[]{:S(2)}, u32[]{:S(2)}) collective-permute-start(bf16[112,2560]{1,0:T(8,128)(2,1)} %slice.61), channel_id=1, source_target_pairs={{0,192},{64,0},{128,64},{192,128},{1,193},{65,1},{129,65},{193,129... | collective-permute-start | bytes 1720328 | tf_op jit(solution)/shard_map/ppermute | solution.py:30
  150.9 25.7 %collective-permute-start.7 = (bf16[4,336,2560]{2,1,0:T(8,128)(2,1)}, bf16[4,336,2560]{2,1,0:T(8,128)(2,1)}, u32[]{:S(2)}, u32[]{:S(2)}) collective-permute-start(bf16[4,336,2560]{2,1,0:T(8,128)(2,1)} %bitcast.12.mine_ref), channel_id=1, source_target_pairs={{0,256},{256,0},{1,257},{257,1},{2,258},{258,2},{3,259},{259,3},{4... | collective-permute-start | bytes 20643848 | tf_op jit(solution)/shard_map/ppermute | solution.py:209
  154.3 22.3 %all-to-all-start.4 = ((bf16[4,64,2688]{2,1,0:T(8,128)(2,1)}), bf16[4,64,2688]{2,1,0:T(8,128)(2,1)S(1)}, u32[]{:S(2)}, u32[]{:S(2)}) async-start(bf16[4,64,2688]{2,1,0:T(8,128)(2,1)} %broadcast_in_dim.11), calls=%async_computation.4 | async-start | bytes 2752512 | tf_op jit(solution)/shard_map/all_to_all | solution.py:34
  176.6 1.1 copy-start.1

commit v6 on v2

v6 whole, which is shorter than its diff:
```python
import math

import jax
import jax.numpy as jnp
from jax import lax
from jax.experimental import pallas as pl
from jax.experimental.pallas import tpu as pltpu
from jax.sharding import Mesh
from jax.sharding import PartitionSpec as P

HD = 128
Y = 4
Z = 16
TP = 4
GROUP = ("pool", "tp")
F32 = jnp.float32
BF16 = jnp.bfloat16


def copies_of(x, count):
    return jnp.broadcast_to(x[None], (count,) + x.shape)


def spread(x, axis, count):
    return exchange(copies_of(x, count), axis)


def shift(x, axis, count):
    size = lax.axis_size(axis)
    return lax.ppermute(x, axis, [(i, (i + count) % size) for i in range(size)])


def swap(x):
    return lax.ppermute(x, "pool", [(0, 1), (1, 0)])


def exchange(x, axis):
    return lax.all_to_all(x, axis, split_axis=0, concat_axis=0, tiled=True)


def attention_kernel(q_ref, kv_ref, o_ref):
    heads = q_ref.shape[1] // HD
    lane = lax.broadcasted_iota(jnp.int32, (q_ref.shape[0], HD), 1)
    stats = jnp.zeros(lane.shape, F32)
    for h in range(heads):
        cols = slice(h * HD, (h + 1) * HD)
        values = kv_ref[:, (heads + h) * HD : (heads + h + 1) * HD]
        scores = lax.dot_general(
            q_ref[:, cols], kv_ref[:, cols], (((1,), (1,)), ((), ())), preferred_element_type=F32
        ) * (1.0 / math.sqrt(HD))
        top = jnp.max(scores, axis=1, keepdims=True)
        weights = jnp.exp(scores - top)
        total = jnp.sum(weights, axis=1, keepdims=True)
        part = jnp.dot(weights.astype(BF16), values, preferred_element_type=F32)
        o_ref[:, cols] = (part / total).astype(BF16)
        rest = top + jnp.log(total)
        for k in range(3):
            term = rest.astype(BF16).astype(F32)
            stats = jnp.where(lane == 3 * h + k, term, stats)
            rest = rest - term
    o_ref[:, heads * HD :] = stats.astype(BF16)


def attend(queries, key_value):
    rows, depth = queries.shape
    return pl.pallas_call(
        attention_kernel,
        out_shape=jax.ShapeDtypeStruct((rows, depth + HD), BF16),
        compiler_params=pltpu.CompilerParams(vmem_limit_bytes=16 << 20),
        cost_estimate=pl.CostEstimate(
            flops=4 * rows * depth * key_value.shape[0],
            bytes_accessed=2 * key_value.size,
            transcendentals=0,
        ),
    )(queries, key_value)


def project_kernel(partial_ref, w_ref, o_ref):
    heads = w_ref.shape[0] // HD
    outs = []
    for h in range(heads):
        first = heads * HD + 3 * h
        log_sums = []
        for y in range(Y):
            terms = partial_ref[y, :, heads * HD :].astype(F32)
            at = first - heads * HD
            log_sums.append(
                terms[:, at : at + 1] + terms[:, at + 1 : at + 2] + terms[:, at + 2 : at + 3]
            )
        top = log_sums[0]
        for y in range(1, Y):
            top = jnp.maximum(top, log_sums[y])
        acc = jnp.zeros((partial_ref.shape[1], HD), F32)
        total = jnp.zeros_like(top)
        for y in range(Y):
            scale = jnp.exp(log_sums[y] - top)
            total += scale
            acc += scale * partial_ref[y, :, h * HD : (h + 1) * HD].astype(F32)
        outs.append((acc / total).astype(BF16))
    o_ref[...] = jnp.dot(
        jnp.concatenate(outs, 1), w_ref[...], preferred_element_type=F32
    ).astype(BF16)


def project(partial, w_out):
    return pl.pallas_call(
        project_kernel,
        out_shape=jax.ShapeDtypeStruct((partial.shape[1], w_out.shape[1]), BF16),
        compiler_params=pltpu.CompilerParams(vmem_limit_bytes=16 << 20),
        cost_estimate=pl.CostEstimate(
            flops=2 * partial.shape[1] * w_out.size,
            bytes_accessed=2 * w_out.size,
            transcendentals=0,
        ),
    )(partial, w_out)


def pack_weights(w_gate, w_up, w_down):
    pad = -w_down.shape[0] % 16
    return jnp.concatenate(
        [jnp.pad(w, ((0, pad), (0, 0))) for w in (w_gate.T, w_up.T, w_down)], 0
    )


def ffn_kernel(ids_ref, x_hbm, *refs):
    parts = refs[: 2 * TP]
    o_ref, x_ref, w_ref, act_ref, down_ref, sems = refs[2 * TP :]
    width = o_ref.shape[1]
    hidden = w_ref.shape[1] // 3
    x_copy = pltpu.make_async_copy(x_hbm, x_ref, sems.at[2 * TP])
    x_copy.start()
    copies = []
    for i, part in enumerate(parts):
        copies.append(pltpu.make_async_copy(part, w_ref.at[i], sems.at[i]))
        copies[i].start()
    x_copy.wait()
    x = x_ref[:, :width]
    route = x_ref[:, width:].astype(F32).T
    scales = []
    for e in range(2 * TP):
        scale = jnp.zeros((1, x.shape[0]), F32)
        for k in range(2):
            value = route[2 + k : 3 + k] + route[4 + k : 5 + k]
            scale += jnp.where(route[k : k + 1] == ids_ref[e].astype(F32), value, 0.0)
        scales.append(scale)
    each = 4
    for first in range(0, 2 * TP, each):
        for i in range(first, first + each):
            copies[i].wait()
        both = lax.dot_general(
            jnp.concatenate([w_ref[i, : 2 * hidden] for i in range(first, first + each)], 0),
            x,
            (((1,), (1,)), ((), ())),
            preferred_element_type=F32,
        )
        for i in range(first, first + each):
            gate = both[2 * (i - first) * hidden : (2 * (i - first) + 1) * hidden]
            up = both[(2 * (i - first) + 1) * hidden : (2 * (i - first) + 2) * hidden]
            here = slice(i * hidden, (i + 1) * hidden)
            act = gate / (1.0 + jnp.exp(-gate)) * up * scales[i]
            act_ref[here] = act.astype(BF16)
            down_ref[here] = w_ref[i, 2 * hidden :]
    o_ref[...] = lax.dot_general(
        act_ref[...], down_ref[...], (((0,), (0,)), ((), ())), preferred_element_type=F32
    ).astype(BF16)


def ffn(ids, x, mine, other):
    rows = x.shape[0]
    depth, width = mine[0].shape
    units = 2 * TP * (depth // 3)
    return pl.pallas_call(
        ffn_kernel,
        out_shape=jax.ShapeDtypeStruct((rows, width), BF16),
        in_specs=[pl.BlockSpec(memory_space=pltpu.SMEM)]
        + [pl.BlockSpec(memory_space=pl.ANY)] * (1 + 2 * TP),
        out_specs=pl.BlockSpec(memory_space=pltpu.VMEM),
        scratch_shapes=[
            pltpu.VMEM(x.shape, BF16),
            pltpu.VMEM((2 * TP, depth, width), BF16),
            pltpu.VMEM((units, rows), BF16),
            pltpu.VMEM((units, width), BF16),
            pltpu.SemaphoreType.DMA((2 * TP + 1,)),
        ],
        compiler_params=pltpu.CompilerParams(vmem_limit_bytes=36 << 20),
        cost_estimate=pl.CostEstimate(
            flops=4 * rows * width * depth * TP,
            bytes_accessed=4 * width * depth * TP,
            transcendentals=0,
        ),
    )(ids, x, *mine, *other)


def body(
    tokens,
    query_proj,
    key_proj,
    value_proj,
    w_out,
    modulation,
    expert_ids,
    gate_values,
    w_gate,
    w_up,
    w_down,
):
    rows, width = tokens.shape
    heads = query_proj.shape[1] // HD
    own_rows = rows // (2 * TP)
    pool = lax.axis_index("pool")
    tp = lax.axis_index("tp")
    group = pool * TP + tp

    packed = pack_weights(w_gate[0], w_up[0], w_down[0])
    before = shift(packed, "tp", 1)
    after = shift(packed, "tp", -1)

    queries = spread(query_proj, "y", Y).reshape(Y * rows, heads * HD)
    queries, key_proj = lax.optimization_barrier((queries, key_proj))
    key_value = spread(jnp.concatenate([key_proj, value_proj], 1), "z", Z)
    key_value = key_value.reshape(Z * rows, 2 * heads * HD)
    partial = exchange(attend(queries, key_value).reshape(Y, rows, (heads + 1) * HD), "y")

    projected = project(partial, w_out).reshape(2 * TP, own_rows, width)
    before, after, projected = lax.optimization_barrier((before, after, projected))
    across = shift(before, "tp", 1)
    projected = exchange(projected, GROUP)
    attention = jnp.sum(projected.astype(F32), axis=0)
    own_tokens = lax.dynamic_slice_in_dim(tokens, group * own_rows, own_rows, 0).astype(F32)
    resid = own_tokens + modulation[0] * attention
    row_mean = jnp.mean(resid, axis=1, keepdims=True)
    row_square = jnp.mean(resid * resid, axis=1, keepdims=True)
    inv_dev = lax.rsqrt(row_square - row_mean * row_mean + 1e-06)
    normed = ((resid - row_mean) * inv_dev * (1.0 + modulation[2]) + modulation[1]).astype(BF16)

    own_ids = lax.dynamic_slice_in_dim(expert_ids, group * own_rows, own_rows, 0)
    own_gates = lax.dynamic_slice_in_dim(gate_values, group * own_rows, own_rows, 0)
    gates_hi = lax.reduce_precision(own_gates, 8, 7)
    gates_lo = own_gates - gates_hi
    route = jnp.concatenate(
        [own_ids.astype(BF16), gates_hi.astype(BF16), gates_lo.astype(BF16)], 1
    )
    route = jnp.pad(route, ((0, 0), (0, HD - route.shape[1])))
    sent = jnp.concatenate([normed, route], 1)
    copies = copies_of(sent, Z)
    packed, before, after, copies = lax.optimization_barrier((packed, before, after, copies))
    mine = [packed, before, after]
    other = [swap(w) for w in mine]
    copies = copies_of(exchange(copies, "z").reshape(Z * own_rows, width + HD), Y)
    across, copies = lax.optimization_barrier((across, copies))
    mine.append(across)
    other.append(swap(across))
    rows_in = exchange(copies, "y").reshape(Y * Z * own_rows, width + HD)
    near = (tp + jnp.array([0, TP - 1, 1, 2], jnp.int32)) % TP
    ids = jnp.concatenate([pool * TP + near, (1 - pool) * TP + near]).astype(jnp.int32)
    mixed = ffn(ids, rows_in, mine, other)

    mixed = exchange(mixed.reshape(Y, Z * own_rows, width), "y")
    mixed = jnp.sum(mixed.astype(F32), axis=0).astype(BF16)
    mixed = exchange(mixed.reshape(Z, own_rows, width), "z")
    mixture = jnp.sum(mixed.astype(F32), axis=0)
    block_out = (resid + modulation[3] * mixture).astype(BF16)
    block_out = block_out.reshape(own_rows, 2 * TP, width // (2 * TP)).transpose(1, 0, 2)
    return exchange(block_out, GROUP).reshape(rows, width // (2 * TP))


def solution(mesh):
    split = Mesh(
        mesh.devices.reshape(2, Y, Z, TP), ("pool", "y", "z", "tp")
    )
    seq = ("y", "z")
    in_specs = (
        P(seq, None),
        P(seq, GROUP),
        P(seq, GROUP),
        P(seq, GROUP),
        P(GROUP, None),
        P(),
        P(seq, None),
        P(seq, None),
        P(GROUP, None, seq),
        P(GROUP, None, seq),
        P(GROUP, seq, None),
    )
    return jax.shard_map(
        body, mesh=split, in_specs=in_specs, out_specs=P(seq, GROUP), check_vma=False
    )
```

time: 230 us -> 221 us (0.961)
  between operations: 13.6 us -> 0.27 us
  starting transfers between devices: 46.8 us -> 59.5 us
  waiting for transfers between devices: 57 us -> 67.5 us
  blocking collectives: 79.6 us -> 69.8 us
  Pallas kernels: 17.1 us -> 11.9 us
  other arithmetic: 6.07 us -> 3.74 us
    all_to_all x3 -> x0, waiting for transfers between devices: 44 us -> none  [spread(): return lax.all_to_all(copies, axis, split_axis=0, concat_axis=0, tiled=True)]
    all_to_all x2 -> x5, waiting for transfers between devices: 13 us -> 47.9 us  [exchange(): return lax.all_to_all(x, axis, split_axis=0, concat_axis=0, tiled=True)]
    all_to_all x1 -> x0, blocking collectives: 24.8 us -> none  [spread(): return lax.all_to_all(copies, axis, split_axis=0, concat_axis=0, tiled=True)]
    all_to_all x2 -> x5, starting transfers between devices: 16.3 us -> 40.1 us  [exchange(): return lax.all_to_all(x, axis, split_axis=0, concat_axis=0, tiled=True)]
    all_to_all x3 -> x0, starting transfers between devices: 23.5 us -> none  [spread(): return lax.all_to_all(copies, axis, split_axis=0, concat_axis=0, tiled=True)]
    ppermute x1 -> x7, waiting for transfers between devices: 0.01 us -> 19.6 us  [the longest x3 19.6 us: shift(): return lax.ppermute(x, axis, [(i, (i + count) % size) for i in range(size)])]
    all_to_all x3 -> x4, blocking collectives: 54.8 us -> 69.8 us  [exchange(): return lax.all_to_all(x, axis, split_axis=0, concat_axis=0, tiled=True)]
    ppermute x1 -> x7, starting transfers between devices: 6.96 us -> 19.4 us  [the longest x4 9.78 us: swap(): return lax.ppermute(x, 'pool', [(0, 1), (1, 0)])]
  transfers between devices with their start and end apart: 7 -> 12, of which waited for: 5 -> 8; matrix products, arithmetic and copies ran while one was open for 4% -> 3% of each run, Pallas kernels for 0% -> 1%
where the time goes in v6:
time: 221 us; the launch traced here: 220 us
  blocking collectives  69.8 us (32%)
  waiting for transfers between devices  67.5 us (31%)
  starting transfers between devices  59.5 us (27%)
  Pallas kernels  11.9 us (5%)
  local copies, waits for them, and re-layouts  7.07 us (3%)
  other arithmetic  3.74 us (2%)
    all_to_all x4, blocking collectives, exchange(): return lax.all_to_all(x, axis, split_axis=0, concat_axis=0, tiled=True)  69.8 us
    all_to_all x5, waiting for transfers between devices, exchange(): return lax.all_to_all(x, axis, split_axis=0, concat_axis=0, tiled=True)  47.9 us
    all_to_all x5, starting transfers between devices, exchange(): return lax.all_to_all(x, axis, split_axis=0, concat_axis=0, tiled=True)  40.1 us
    ppermute x3, waiting for transfers between devices, shift(): return lax.ppermute(x, axis, [(i, (i + count) % size) for i in range(size)])  19.6 us
    pallas_call x1, Pallas kernels, ffn(): pl.pallas_call(ffn_kernel, out_shape=jax.ShapeDtypeStruct((rows, width),...  10.1 us
    ppermute x4, starting transfers between devices, swap(): return lax.ppermute(x, 'pool', [(0, 1), (1, 0)])  9.78 us
    ppermute x3, starting transfers between devices, shift(): return lax.ppermute(x, axis, [(i, (i + count) % size) for i in range(size)])  9.59 us
  transfers between devices with their start and end apart: 12, of which 8 were waited for; matrix products, arithmetic and copies ran while one was open for 3% of the time, Pallas kernels for 1%

profile of v6, /device:TPU:1, one launch (start us, length us, event | category | flops | bytes accessed | tf_op | source)
XLA Modules:
  0.0 219.8 jit_solution(7761403938692190071)
XLA Ops:
  0.0 0.8 broadcast_in_dim.10
  0.8 9.3 %all_to_all.45 = bf16[4,32,256]{2,1,0:T(8,128)(2,1)S(1)} all-to-all(bf16[4,32,256]{2,1,0:T(8,128)(2,1)S(1)} %broadcast_in_dim.10), channel_id=1, replica_groups=mesh['pool'=2,'y'=4,'z'=16,'tp'=4] {'y'}, dimensions={0} | all-to-all | bytes 131072 | tf_op jit(solution)/shard_map/all_to_all | solution.py:38
  10.1 0.7 pad_maximum_fusion
  10.8 0.8 broadcast_in_dim.11
  11.7 14.9 %all-to-all-start.1 = ((bf16[16,32,512]{2,1,0:T(8,128)(2,1)}), bf16[16,32,512]{2,1,0:T(8,128)(2,1)S(1)}, u32[]{:S(2)}, u32[]{:S(2)}) async-start(bf16[16,32,512]{2,1,0:T(8,128)(2,1)} %broadcast_in_dim.11), calls=%async_computation.1 | async-start | bytes 1048576 | tf_op jit(solution)/shard_map/all_to_all | solution.py:38
  26.6 1.2 fusion.5.refs_0_
  27.8 4.4 %collective-permute-start.1 = (bf16[336,2560]{1,0:T(8,128)(2,1)S(1)}, bf16[336,2560]{1,0:T(8,128)(2,1)}, u32[]{:S(2)}, u32[]{:S(2)}) collective-permute-start(bf16[336,2560]{1,0:T(8,128)(2,1)S(1)} %fusion.5.refs_0_), channel_id=1, source_target_pairs={{0,3},{1,0},{2,1},{3,2},{4,7},{5,4},{6,5},{7,6},{8,11},{9,8},{10,9... | collective-permute-start | bytes 5160968 | tf_op jit(solution)/shard_map/ppermute | solution.py:30
  32.2 1.9 collective-permute-start
  34.2 0.1 constant_dynamic-slice_fusion
  34.3 0.1 copy.35
  34.4 14.0 %all-to-all-done.1 = bf16[16,32,512]{2,1,0:T(8,128)(2,1)S(1)} async-done(((bf16[16,32,512]{2,1,0:T(8,128)(2,1)}), bf16[16,32,512]{2,1,0:T(8,128)(2,1)S(1)}, u32[]{:S(2)}, u32[]{:S(2)}) %all-to-all-start.1) | async-done | bytes 524320 | tf_op jit(solution)/shard_map/all_to_all | solution.py:38
  48.4 1.3 shard_map.118
  49.7 3.3 %all-to-all-start.2 = ((bf16[4,32,384]{2,1,0:T(8,128)(2,1)}), bf16[4,32,384]{2,1,0:T(8,128)(2,1)S(1)}, u32[]{:S(2)}, u32[]{:S(2)}) async-start(bf16[4,32,384]{2,1,0:T(8,128)(2,1)} %bitcast.7), calls=%async_computation.2 | async-start | bytes 196608 | tf_op jit(solution)/shard_map/all_to_all | solution.py:38
  53.1 0.1 copy.34
  53.2 4.4 %all-to-all-done.2.partial_ref = bf16[4,32,384]{2,1,0:T(8,128)(2,1)S(1)} async-done(((bf16[4,32,384]{2,1,0:T(8,128)(2,1)}), bf16[4,32,384]{2,1,0:T(8,128)(2,1)S(1)}, u32[]{:S(2)}, u32[]{:S(2)}) %all-to-all-start.2) | async-done | bytes 98336 | tf_op jit(solution)/shard_map/all_to_all | solution.py:38
  57.7 1.3 copy-done.1
  59.0 0.5 shard_map.119
  59.4 0.7 reshape.52
  60.2 6.5 %collective-permute-done.1.refs_2_ = bf16[336,2560]{1,0:T(8,128)(2,1)} collective-permute-done((bf16[336,2560]{1,0:T(8,128)(2,1)S(1)}, bf16[336,2560]{1,0:T(8,128)(2,1)}, u32[]{:S(2)}, u32[]{:S(2)}) %collective-permute-start.1) | collective-permute-done | bytes 1720352 | tf_op jit(solution)/shard_map/ppermute | solution.py:30
  66.7 5.2 %collective-permute-done.refs_1_ = bf16[336,2560]{1,0:T(8,128)(2,1)} collective-permute-done((bf16[336,2560]{1,0:T(8,128)(2,1)S(1)}, bf16[336,2560]{1,0:T(8,128)(2,1)}, u32[]{:S(2)}, u32[]{:S(2)}) %collective-permute-start) | collective-permute-done | bytes 1720352 | tf_op jit(solution)/shard_map/ppermute | solution.py:30
  71.8 6.9 %all-to-all-start.3 = ((bf16[8,4,2560]{2,1,0:T(4,128)(2,1)}), bf16[8,4,2560]{2,1,0:T(4,128)(2,1)S(1)}, u32[]{:S(2)}, u32[]{:S(2)}) async-start(bf16[8,4,2560]{2,1,0:T(4,128)(2,1)} %reshape.52), calls=%async_computation.3 | async-start | bytes 327680 | tf_op jit(solution)/shard_map/all_to_all | solution.py:38
  78.7 0.1 fusion.11
  78.8 0.1 slice_reduce_fusion.1
  78.9 3.3 %collective-permute-start.2 = (bf16[336,2560]{1,0:T(8,128)(2,1)}, bf16[336,2560]{1,0:T(8,128)(2,1)}, u32[]{:S(2)}, u32[]{:S(2)}) collective-permute-start(bf16[336,2560]{1,0:T(8,128)(2,1)} %collective-permute-done.refs_1_), channel_id=1, source_target_pairs={{0,1},{1,2},{2,3},{3,0},{4,5},{5,6},{6,7},{7,4},{8,9},{9,10},{10,1... | collective-permute-start | bytes 5160968 | tf_op jit(solution)/shard_map/ppermute | solution.py:30
  82.2 2.0 all-to-all-done.3
  84.3 1.0 fusion.13
  85.3 0.1 add_convert_fusion.1
  85.4 0.8 broadcast_in_dim.12
  86.2 11.5 %all-to-all-start.4 = ((bf16[16,4,2688]{2,1,0:T(4,128)(2,1)}), bf16[16,4,2688]{2,1,0:T(4,128)(2,1)S(1)}, u32[]{:S(2)}, u32[]{:S(2)}) async-start(bf16[16,4,2688]{2,1,0:T(4,128)(2,1)} %broadcast_in_dim.12), calls=%async_computation.4 | async-start | bytes 688128 | tf_op jit(solution)/shard_map/all_to_all | solution.py:38
  97.7 2.6 %collective-permute-start.3 = (bf16[336,2560]{1,0:T(8,128)(2,1)S(1)}, bf16[336,2560]{1,0:T(8,128)(2,1)}, u32[]{:S(2)}, u32[]{:S(2)}) collective-permute-start(bf16[336,2560]{1,0:T(8,128)(2,1)S(1)} %fusion.5.refs_0_), channel_id=1, source_target_pairs={{0,256},{256,0},{1,257},{257,1},{2,258},{258,2},{3,259},{259,3},{4... | collective-permute-start | bytes 5160968 | tf_op jit(solution)/shard_map/ppermute | solution.py:34
  100.3 1.9 collective-permute-start.4
  102.2 2.4 %collective-permute-start.5 = (bf16[336,2560]{1,0:T(8,128)(2,1)}, bf16[336,2560]{1,0:T(8,128)(2,1)}, u32[]{:S(2)}, u32[]{:S(2)}) collective-permute-start(bf16[336,2560]{1,0:T(8,128)(2,1)} %collective-permute-done.1.refs_2_), channel_id=1, source_target_pairs={{0,256},{256,0},{1,257},{257,1},{2,258},{258,2},{3,259},{259,3},{4... | collective-permute-start | bytes 5160968 | tf_op jit(solution)/shard_map/ppermute | solution.py:34
  104.6 8.8 %all-to-all-done.4 = bf16[16,4,2688]{2,1,0:T(4,128)(2,1)S(1)} async-done(((bf16[16,4,2688]{2,1,0:T(4,128)(2,1)}), bf16[16,4,2688]{2,1,0:T(4,128)(2,1)S(1)}, u32[]{:S(2)}, u32[]{:S(2)}) %all-to-all-start.4) | async-done | bytes 344096 | tf_op jit(solution)/shard_map/all_to_all | solution.py:38
  113.4 0.1 broadcast_in_dim.13
  113.5 7.9 %collective-permute-done.2.refs_3_ = bf16[336,2560]{1,0:T(8,128)(2,1)} collective-permute-done((bf16[336,2560]{1,0:T(8,128)(2,1)}, bf16[336,2560]{1,0:T(8,128)(2,1)}, u32[]{:S(2)}, u32[]{:S(2)}) %collective-permute-start.2) | collective-permute-done | bytes 1720352 | tf_op jit(solution)/shard_map/ppermute | solution.py:30
  121.5 1.3 broadcast_in_dim.14
  122.7 2.9 %collective-permute-start.6 = (bf16[336,2560]{1,0:T(8,128)(2,1)}, bf16[336,2560]{1,0:T(8,128)(2,1)}, u32[]{:S(2)}, u32[]{:S(2)}) collective-permute-start(bf16[336,2560]{1,0:T(8,128)(2,1)} %collective-permute-done.2.refs_3_), channel_id=1, source_target_pairs={{0,256},{256,0},{1,257},{257,1},{2,258},{258,2},{3,259},{259,3},{4... | collective-permute-start | bytes 5160968 | tf_op jit(solution)/shard_map/ppermute | solution.py:34
  125.6 3.6 %all-to-all-start.5 = ((bf16[4,64,2688]{2,1,0:T(8,128)(2,1)}), bf16[4,64,2688]{2,1,0:T(8,128)(2,1)S(1)}, u32[]{:S(2)}, u32[]{:S(2)}) async-start(bf16[4,64,2688]{2,1,0:T(8,128)(2,1)} %broadcast_in_dim.14), calls=%async_computation.5 | async-start | bytes 2752512 | tf_op jit(solution)/shard_map/all_to_all | solution.py:38
  129.3 18.6 %all-to-all-done.5 = bf16[4,64,2688]{2,1,0:T(8,128)(2,1)S(1)} async-done(((bf16[4,64,2688]{2,1,0:T(8,128)(2,1)}), bf16[4,64,2688]{2,1,0:T(8,128)(2,1)S(1)}, u32[]{:S(2)}, u32[]{:S(2)}) %all-to-all-start.5) | async-done | bytes 1376288 | tf_op jit(solution)/shard_map/all_to_all | solution.py:38
  147.9 10.1 %shard_map.120 = bf16[256,2560]{1,0:T(8,128)(2,1)S(1)} custom-call(s32[8]{0:T(128)S(1)} %pad_add_fusion.ids_ref, bf16[256,2688]{1,0:T(8,128)(2,1)S(1)} %bitcast.15, bf16[336,2560]{1,0:T(8,128)(2,1)S(1)} %fusion.5.refs_0_, bf16[336,2560]{1,0:T(8,128)(2,1)} %collective-permute-done.refs_1_, bf16[336,2560]{1,0:T(8,128)(2,1)} %collective-permute-done.1.refs_2_, ...), custom_call_target="tpu_custom_call" | custom-call | flops 3523215360 | bytes 13762560 | tf_op jit(solution)/shard_map/pallas_call | solution.py:172
  158.1 19.4 %all_to_all.46 = bf16[4,64,2560]{2,1,0:T(8,128)(2,1)S(1)} all-to-all(bf16[4,64,2560]{2,1,0:T(8,128)(2,1)S(1)} %bitcast.16), channel_id=1, replica_groups=mesh['pool'=2,'y'=4,'z'=16,'tp'=4] {'y'}, dimensions={0} | all-to-all | bytes 2621440 | tf_op jit(solution)/shard_map/all_to_all | solution.py:38
  177.4 0.2 reduce_sum.51
  177.7 0.1 reshape.55
  177.7 25.0 %all_to_all.47 = bf16[16,4,2560]{2,1,0:T(4,128)(2,1)S(1)} all-to-all(bf16[16,4,2560]{2,1,0:T(4,128)(2,1)S(1)} %reshape.55), channel_id=1, replica_groups=mesh['pool'=2,'y'=4,'z'=16,'tp'=4] {'z'}, dimensions={0} | all-to-all | bytes 655360 | tf_op jit(solution)/shard_map/all_to_all | solution.py:38
  202.8 0.1 convert_reduce_fusion
  202.9 0.1 reshape.56
  203.1 16.1 %all_to_all.48 = bf16[8,4,320]{2,1,0:T(4,128)(2,1)S(1)} all-to-all(bf16[8,4,320]{2,1,0:T(4,128)(2,1)S(1)} %bitcast.22), channel_id=1, replica_groups=mesh['pool'=2,'y'=4,'z'=16,'tp'=4] {'pool','tp'}, dimensions={0} | all-to-all | bytes 40960 | tf_op jit(solution)/shard_map/all_to_all | solution.py:38
  219.2 0.6 reshape.57
  (28 shorter events, 0.4 us)
Async XLA Ops:
  0.0 34.2 %copy-start = (f32[32,2]{0,1:T(2,128)S(1)}, f32[32,2]{0,1:T(2,128)}, u32[]{:S(2)}) copy-start(f32[32,2]{0,1:T(2,128)} %param.19) | copy-start | bytes 772
  0.0 26.6 %copy-start.2 = (bf16[1,108,2560]{2,1,0:T(8,128)(2,1)S(1)}, bf16[1,108,2560]{2,1,0:T(8,128)(2,1)}, u32[]{:S(2)}) copy-start(bf16[1,108,2560]{2,1,0:T(8,128)(2,1)} %param.22) | copy-start | bytes 1658884
  0.0 26.6 %copy-start.3 = (bf16[1,2560,108]{1,2,0:T(8,128)(2,1)S(1)}, bf16[1,2560,108]{1,2,0:T(8,128)(2,1)}, u32[]{:S(2)}) copy-start(bf16[1,2560,108]{1,2,0:T(8,128)(2,1)} %param.21) | copy-start | bytes 1658884
  11.7 36.7 %all-to-all-start.1 = ((bf16[16,32,512]{2,1,0:T(8,128)(2,1)}), bf16[16,32,512]{2,1,0:T(8,128)(2,1)S(1)}, u32[]{:S(2)}, u32[]{:S(2)}) async-start(bf16[16,32,512]{2,1,0:T(8,128)(2,1)} %broadcast_in_dim.11), calls=%async_computation.1 | async-start | bytes 1048576 | tf_op jit(solution)/shard_map/all_to_all | solution.py:38
  26.6 26.4 %copy-start.5 = (s32[32,2]{0,1:T(2,128)S(1)}, s32[32,2]{0,1:T(2,128)}, u32[]{:S(2)}) copy-start(s32[32,2]{0,1:T(2,128)} %param.18) | copy-start | bytes 772
  27.8 51.0 %copy-start.4 = (f32[4,2560]{1,0:T(4,128)S(1)}, f32[4,2560]{1,0:T(4,128)}, u32[]{:S(2)}) copy-start(f32[4,2560]{1,0:T(4,128)} %param.17) | copy-start | bytes 122884
  27.8 38.8 %collective-permute-start.1 = (bf16[336,2560]{1,0:T(8,128)(2,1)S(1)}, bf16[336,2560]{1,0:T(8,128)(2,1)}, u32[]{:S(2)}, u32[]{:S(2)}) collective-permute-start(bf16[336,2560]{1,0:T(8,128)(2,1)S(1)} %fusion.5.refs_0_), channel_id=1, source_target_pairs={{0,3},{1,0},{2,1},{3,2},{4,7},{5,4},{6,5},{7,6},{8,11},{9,8},{10,9... | collective-permute-start | bytes 5160968 | tf_op jit(solution)/shard_map/ppermute | solution.py:30
  32.2 39.6 %collective-permute-start = (bf16[336,2560]{1,0:T(8,128)(2,1)S(1)}, bf16[336,2560]{1,0:T(8,128)(2,1)}, u32[]{:S(2)}, u32[]{:S(2)}) collective-permute-start(bf16[336,2560]{1,0:T(8,128)(2,1)S(1)} %fusion.5.refs_0_), channel_id=1, source_target_pairs={{0,1},{1,2},{2,3},{3,0},{4,5},{5,6},{6,7},{7,4},{8,9},{9,10},{10,1... | collective-permute-start | bytes 5160968 | tf_op jit(solution)/shard_map/ppermute | solution.py:30
  49.7 7.9 %all-to-all-start.2 = ((bf16[4,32,384]{2,1,0:T(8,128)(2,1)}), bf16[4,32,384]{2,1,0:T(8,128)(2,1)S(1)}, u32[]{:S(2)}, u32[]{:S(2)}) async-start(bf16[4,32,384]{2,1,0:T(8,128)(2,1)} %bitcast.7), calls=%async_computation.2 | async-start | bytes 196608 | tf_op jit(solution)/shard_map/all_to_all | solution.py:38
  57.7 1.3 copy-start.1
  71.8 12.4 %all-to-all-start.3 = ((bf16[8,4,2560]{2,1,0:T(4,128)(2,1)}), bf16[8,4,2560]{2,1,0:T(4,128)(2,1)S(1)}, u32[]{:S(2)}, u32[]{:S(2)}) async-start(bf16[8,4,2560]{2,1,0:T(4,128)(2,1)} %reshape.52), calls=%async_computation.3 | async-start | bytes 327680 | tf_op jit(solution)/shard_map/all_to_all | solution.py:38
  78.9 42.5 %collective-permute-start.2 = (bf16[336,2560]{1,0:T(8,128)(2,1)}, bf16[336,2560]{1,0:T(8,128)(2,1)}, u32[]{:S(2)}, u32[]{:S(2)}) collective-permute-start(bf16[336,2560]{1,0:T(8,128)(2,1)} %collective-permute-done.refs_1_), channel_id=1, source_target_pairs={{0,1},{1,2},{2,3},{3,0},{4,5},{5,6},{6,7},{7,4},{8,9},{9,10},{10,1... | collective-permute-start | bytes 5160968 | tf_op jit(solution)/shard_map/ppermute | solution.py:30
  86.2 27.2 %all-to-all-start.4 = ((bf16[16,4,2688]{2,1,0:T(4,128)(2,1)}), bf16[16,4,2688]{2,1,0:T(4,128)(2,1)S(1)}, u32[]{:S(2)}, u32[]{:S(2)}) async-start(bf16[16,4,2688]{2,1,0:T(4,128)(2,1)} %broadcast_in_dim.12), calls=%async_computation.4 | async-start | bytes 688128 | tf_op jit(solution)/shard_map/all_to_all | solution.py:38
  97.7 31.6 %collective-permute-start.3 = (bf16[336,2560]{1,0:T(8,128)(2,1)S(1)}, bf16[336,2560]{1,0:T(8,128)(2,1)}, u32[]{:S(2)}, u32[]{:S(2)}) collective-permute-start(bf16[336,2560]{1,0:T(8,128)(2,1)S(1)} %fusion.5.refs_0_), channel_id=1, source_target_pairs={{0,256},{256,0},{1,257},{257,1},{2,258},{258,2},{3,259},{259,3},{4... | collective-permute-start | bytes 5160968 | tf_op jit(solution)/shard_map/ppermute | solution.py:34
  100.3 29.0 %collective-permute-start.4 = (bf16[336,2560]{1,0:T(8,128)(2,1)}, bf16[336,2560]{1,0:T(8,128)(2,1)}, u32[]{:S(2)}, u32[]{:S(2)}) collective-permute-start(bf16[336,2560]{1,0:T(8,128)(2,1)} %collective-permute-done.refs_1_), channel_id=1, source_target_pairs={{0,256},{256,0},{1,257},{257,1},{2,258},{258,2},{3,259},{259,3},{4... | collective-permute-start | bytes 5160968 | tf_op jit(solution)/shard_map/ppermute | solution.py:34
  102.2 27.1 %collective-permute-start.5 = (bf16[336,2560]{1,0:T(8,128)(2,1)}, bf16[336,2560]{1,0:T(8,128)(2,1)}, u32[]{:S(2)}, u32[]{:S(2)}) collective-permute-start(bf16[336,2560]{1,0:T(8,128)(2,1)} %collective-permute-done.1.refs_2_), channel_id=1, source_target_pairs={{0,256},{256,0},{1,257},{257,1},{2,258},{258,2},{3,259},{259,3},{4... | collective-permute-start | bytes 5160968 | tf_op jit(solution)/shard_map/ppermute | solution.py:34
  122.7 6.5 %copy-start.6 = (s32[4]{0:T(128)S(1)}, s32[4]{0:T(128)}, u32[]{:S(2)}) copy-start(s32[4]{0:T(128)} %constant.45.clone) | copy-start | bytes 52
  122.7 25.2 %collective-permute-start.6 = (bf16[336,2560]{1,0:T(8,128)(2,1)}, bf16[336,2560]{1,0:T(8,128)(2,1)}, u32[]{:S(2)}, u32[]{:S(2)}) collective-permute-start(bf16[336,2560]{1,0:T(8,128)(2,1)} %collective-permute-done.2.refs_3_), channel_id=1, source_target_pairs={{0,256},{256,0},{1,257},{257,1},{2,258},{258,2},{3,259},{259,3},{4... | collective-permute-start | bytes 5160968 | tf_op jit(solution)/shard_map/ppermute | solution.py:34
  125.6 22.3 %all-to-all-start.5 = ((bf16[4,64,2688]{2,1,0:T(8,128)(2,1)}), bf16[4,64,2688]{2,1,0:T(8,128)(2,1)S(1)}, u32[]{:S(2)}, u32[]{:S(2)}) async-start(bf16[4,64,2688]{2,1,0:T(8,128)(2,1)} %broadcast_in_dim.14), calls=%async_computation.5 | async-start | bytes 2752512 | tf_op jit(solution)/shard_map/all_to_all | solution.py:38

commit v7 on v6

--- a/solution.py
+++ b/solution.py
@@ -73,46 +73,6 @@
             transcendentals=0,
         ),
     )(queries, key_value)
-
-
-def project_kernel(partial_ref, w_ref, o_ref):
-    heads = w_ref.shape[0] // HD
-    outs = []
-    for h in range(heads):
-        first = heads * HD + 3 * h
-        log_sums = []
-        for y in range(Y):
-            terms = partial_ref[y, :, heads * HD :].astype(F32)
-            at = first - heads * HD
-            log_sums.append(
-                terms[:, at : at + 1] + terms[:, at + 1 : at + 2] + terms[:, at + 2 : at + 3]
-            )
-        top = log_sums[0]
-        for y in range(1, Y):
-            top = jnp.maximum(top, log_sums[y])
-        acc = jnp.zeros((partial_ref.shape[1], HD), F32)
-        total = jnp.zeros_like(top)
-        for y in range(Y):
-            scale = jnp.exp(log_sums[y] - top)
-            total += scale
-            acc += scale * partial_ref[y, :, h * HD : (h + 1) * HD].astype(F32)
-        outs.append((acc / total).astype(BF16))
-    o_ref[...] = jnp.dot(
-        jnp.concatenate(outs, 1), w_ref[...], preferred_element_type=F32
-    ).astype(BF16)
-
-
-def project(partial, w_out):
-    return pl.pallas_call(
-        project_kernel,
-        out_shape=jax.ShapeDtypeStruct((partial.shape[1], w_out.shape[1]), BF16),
-        compiler_params=pltpu.CompilerParams(vmem_limit_bytes=16 << 20),
-        cost_estimate=pl.CostEstimate(
-            flops=2 * partial.shape[1] * w_out.size,
-            bytes_accessed=2 * w_out.size,
-            transcendentals=0,
-        ),
-    )(partial, w_out)
 
 
 def pack_weights(w_gate, w_up, w_down):
@@ -216,13 +176,27 @@
     after = shift(packed, "tp", -1)
 
     queries = spread(query_proj, "y", Y).reshape(Y * rows, heads * HD)
-    queries, key_proj = lax.optimization_barrier((queries, key_proj))
-    key_value = spread(jnp.concatenate([key_proj, value_proj], 1), "z", Z)
-    key_value = key_value.reshape(Z * rows, 2 * heads * HD)
-    partial = exchange(attend(queries, key_value).reshape(Y, rows, (heads + 1) * HD), "y")
-
-    projected = project(partial, w_out).reshape(2 * TP, own_rows, width)
-    before, after, projected = lax.optimization_barrier((before, after, projected))
+    key_value = lax.all_gather(
+        jnp.concatenate([key_proj, value_proj], 1), "z", axis=0, tiled=True
+    )
+    partial = attend(queries, key_value)
+
+    packed, before, after, partial = lax.optimization_barrier((packed, before, after, partial))
+    mine = [packed, before, after]
+    other = [swap(w) for w in mine]
+    partial = exchange(partial.reshape(Y, rows, (heads + 1) * HD), "y").astype(F32)
+    outs = []
+    for h in range(heads):
+        log_sum = partial[:, :, heads * HD + 3 * h : heads * HD + 3 * h + 3]
+        log_sum = jnp.sum(log_sum, axis=2, keepdims=True)
+        scale = jnp.exp(log_sum - jnp.max(log_sum, axis=0, keepdims=True))
+        acc = jnp.sum(scale * partial[:, :, h * HD : (h + 1) * HD], axis=0)
+        outs.append(acc / jnp.sum(scale, axis=0))
+    heads_out = jnp.concatenate(outs, 1).astype(BF16)
+
+    projected = jnp.dot(heads_out, w_out, preferred_element_type=F32).astype(BF16)
+    projected = projected.reshape(2 * TP, own_rows, width)
+    before, projected, *other = lax.optimization_barrier((before, projected, *other))
     across = shift(before, "tp", 1)
     projected = exchange(projected, GROUP)
     attention = jnp.sum(projected.astype(F32), axis=0)
@@ -243,9 +217,6 @@
     route = jnp.pad(route, ((0, 0), (0, HD - route.shape[1])))
     sent = jnp.concatenate([normed, route], 1)
     copies = copies_of(sent, Z)
-    packed, before, after, copies = lax.optimization_barrier((packed, before, after, copies))
-    mine = [packed, before, after]
-    other = [swap(w) for w in mine]
     copies = copies_of(exchange(copies, "z").reshape(Z * own_rows, width + HD), Y)
     across, copies = lax.optimization_barrier((across, copies))
     mine.append(across)

time: 221 us -> 219 us (level)
  blocking collectives: 69.8 us -> 115 us
  waiting for transfers between devices: 67.5 us -> 35.9 us
  starting transfers between devices: 59.5 us -> 43.7 us
    all_gather x0 -> x1, blocking collectives: none -> 34.4 us  [body(): lax.all_gather(jnp.concatenate([key_proj, value_proj], 1), 'z', axis=0, t...]
    all_to_all x5 -> x4, waiting for transfers between devices: 47.9 us -> 24.5 us  [exchange(): return lax.all_to_all(x, axis, split_axis=0, concat_axis=0, tiled=True)]
    all_to_all x5 -> x4, starting transfers between devices: 40.1 us -> 19 us  [exchange(): return lax.all_to_all(x, axis, split_axis=0, concat_axis=0, tiled=True)]
    all_to_all x4, blocking collectives: 69.8 us -> 80.6 us  [exchange(): return lax.all_to_all(x, axis, split_axis=0, concat_axis=0, tiled=True)]
    ppermute x3, waiting for transfers between devices: 19.6 us -> 11.4 us  [shift(): return lax.ppermute(x, axis, [(i, (i + count) % size) for i in range(size)])]
    ppermute x4, starting transfers between devices: 9.78 us -> 14.3 us  [swap(): return lax.ppermute(x, 'pool', [(0, 1), (1, 0)])]
  transfers between devices with their start and end apart: 12 -> 11, of which waited for: 8 -> 4; matrix products, arithmetic and copies ran while one was open for 3% -> 3% of each run, Pallas kernels for 1% -> 1%
where the time goes in v7:
time: 219 us; the launch traced here: 218 us
  blocking collectives  115 us (53%)
  starting transfers between devices  43.7 us (20%)
  waiting for transfers between devices  35.9 us (16%)
  Pallas kernels  11.7 us (5%)
  local copies, waits for them, and re-layouts  6.86 us (3%)
  other arithmetic  3.95 us (2%)
    all_to_all x4, blocking collectives, exchange(): return lax.all_to_all(x, axis, split_axis=0, concat_axis=0, tiled=True)  80.6 us
    all_gather x1, blocking collectives, body(): lax.all_gather(jnp.concatenate([key_proj, value_proj], 1), 'z', axis=0, t...  34.4 us
    all_to_all x4, waiting for transfers between devices, exchange(): return lax.all_to_all(x, axis, split_axis=0, concat_axis=0, tiled=True)  24.5 us
    all_to_all x4, starting transfers between devices, exchange(): return lax.all_to_all(x, axis, split_axis=0, concat_axis=0, tiled=True)  19 us
    ppermute x4, starting transfers between devices, swap(): return lax.ppermute(x, 'pool', [(0, 1), (1, 0)])  14.3 us
    ppermute x3, waiting for transfers between devices, shift(): return lax.ppermute(x, axis, [(i, (i + count) % size) for i in range(size)])  11.4 us
    ppermute x3, starting transfers between devices, shift(): return lax.ppermute(x, axis, [(i, (i + count) % size) for i in range(size)])  10.4 us
    pallas_call x1, Pallas kernels, ffn(): pl.pallas_call(ffn_kernel, out_shape=jax.ShapeDtypeStruct((rows, width),...  10.2 us
  transfers between devices with their start and end apart: 11, of which 4 were waited for; matrix products, arithmetic and copies ran while one was open for 3% of the time, Pallas kernels for 1%

profile of v7, /device:TPU:1, one launch (start us, length us, event | category | flops | bytes accessed | tf_op | source)
XLA Modules:
  0.0 217.7 jit_solution(7509123865734712424)
XLA Ops:
  0.0 1.6 fusion.5.refs_0_
  1.7 5.2 %collective-permute-start.1 = (bf16[336,2560]{1,0:T(8,128)(2,1)S(1)}, bf16[336,2560]{1,0:T(8,128)(2,1)}, u32[]{:S(2)}, u32[]{:S(2)}) collective-permute-start(bf16[336,2560]{1,0:T(8,128)(2,1)S(1)} %fusion.5.refs_0_), channel_id=1, source_target_pairs={{0,3},{1,0},{2,1},{3,2},{4,7},{5,4},{6,5},{7,6},{8,11},{9,8},{10,9... | collective-permute-start | bytes 5160968 | tf_op jit(solution)/shard_map/ppermute | solution.py:30
  6.9 1.9 collective-permute-start
  8.8 0.6 broadcast_in_dim.8
  9.4 4.2 %all-to-all-start = ((bf16[4,32,256]{2,1,0:T(8,128)(2,1)}), bf16[4,32,256]{2,1,0:T(8,128)(2,1)}, u32[]{:S(2)}, u32[]{:S(2)}) async-start(bf16[4,32,256]{2,1,0:T(8,128)(2,1)} %broadcast_in_dim.8), calls=%async_computation | async-start | bytes 131072 | tf_op jit(solution)/shard_map/all_to_all | solution.py:38
  13.6 34.4 %all_gather.3.kv_ref = bf16[512,512]{1,0:T(8,128)(2,1)S(1)} all-gather(bf16[32,512]{1,0:T(8,128)(2,1)S(1)} %pad_maximum_fusion), channel_id=1, replica_groups=mesh['pool'=2,'y'=4,'z'=16,'tp'=4] {'z'}, dimensions={0}, use_global_device_ids=true | all-gather | bytes 557056 | tf_op jit(solution)/shard_map/all_gather | solution.py:179
  48.1 1.5 shard_map.118
  49.6 0.6 copy-done.1
  50.3 7.1 %collective-permute-start.2 = (bf16[336,2560]{1,0:T(8,128)(2,1)S(1)}, bf16[336,2560]{1,0:T(8,128)(2,1)}, u32[]{:S(2)}, u32[]{:S(2)}) collective-permute-start(bf16[336,2560]{1,0:T(8,128)(2,1)S(1)} %fusion.5.refs_0_), channel_id=1, source_target_pairs={{0,256},{256,0},{1,257},{257,1},{2,258},{258,2},{3,259},{259,3},{4... | collective-permute-start | bytes 5160968 | tf_op jit(solution)/shard_map/ppermute | solution.py:34
  57.4 1.9 collective-permute-start.4
  59.3 2.4 %collective-permute-start.3 = (bf16[336,2560]{1,0:T(8,128)(2,1)}, bf16[336,2560]{1,0:T(8,128)(2,1)}, u32[]{:S(2)}, u32[]{:S(2)}) collective-permute-start(bf16[336,2560]{1,0:T(8,128)(2,1)} %collective-permute-done.refs_1_), channel_id=1, source_target_pairs={{0,256},{256,0},{1,257},{257,1},{2,258},{258,2},{3,259},{259,3},{4... | collective-permute-start | bytes 5160968 | tf_op jit(solution)/shard_map/ppermute | solution.py:34
  61.8 0.8 constant_dynamic-slice_fusion
  62.5 0.1 copy.35
  62.6 4.6 %all-to-all-start.1 = ((bf16[4,32,384]{2,1,0:T(8,128)(2,1)}), bf16[4,32,384]{2,1,0:T(8,128)(2,1)S(1)}, u32[]{:S(2)}, u32[]{:S(2)}) async-start(bf16[4,32,384]{2,1,0:T(8,128)(2,1)} %bitcast.16), calls=%async_computation.1 | async-start | bytes 196608 | tf_op jit(solution)/shard_map/all_to_all | solution.py:38
  67.2 0.7 constant_dynamic-slice_fusion.1
  68.0 0.1 copy.34
  68.1 3.8 %all-to-all-done.1 = bf16[4,32,384]{2,1,0:T(8,128)(2,1)S(1)} async-done(((bf16[4,32,384]{2,1,0:T(8,128)(2,1)}), bf16[4,32,384]{2,1,0:T(8,128)(2,1)S(1)}, u32[]{:S(2)}, u32[]{:S(2)}) %all-to-all-start.1) | async-done | bytes 98336 | tf_op jit(solution)/shard_map/all_to_all | solution.py:38
  71.9 0.2 slice_reduce_fusion.1
  72.1 0.1 fusion.7
  72.2 0.1 divide_convert_fusion.1
  72.3 0.1 divide_convert_fusion
  72.4 0.3 convolution_convert_fusion
  72.7 0.7 reshape.99
  73.5 5.8 %all-to-all-start.2 = ((bf16[8,4,2560]{2,1,0:T(4,128)(2,1)}), bf16[8,4,2560]{2,1,0:T(4,128)(2,1)S(1)}, u32[]{:S(2)}, u32[]{:S(2)}) async-start(bf16[8,4,2560]{2,1,0:T(4,128)(2,1)} %reshape.99), calls=%async_computation.2 | async-start | bytes 327680 | tf_op jit(solution)/shard_map/all_to_all | solution.py:38
  79.3 0.1 fusion.16
  79.4 0.1 slice_reduce_fusion.3
  79.5 3.3 %collective-permute-start.5 = (bf16[336,2560]{1,0:T(8,128)(2,1)}, bf16[336,2560]{1,0:T(8,128)(2,1)}, u32[]{:S(2)}, u32[]{:S(2)}) collective-permute-start(bf16[336,2560]{1,0:T(8,128)(2,1)} %collective-permute-done.refs_1_), channel_id=1, source_target_pairs={{0,1},{1,2},{2,3},{3,0},{4,5},{5,6},{6,7},{7,4},{8,9},{9,10},{10,1... | collective-permute-start | bytes 5160968 | tf_op jit(solution)/shard_map/ppermute | solution.py:30
  82.8 2.0 all-to-all-done.2
  84.8 0.1 convert_reduce_fusion.1
  84.9 0.9 fusion.19
  85.9 0.1 add_convert_fusion.1
  86.0 0.1 broadcast_in_dim.9
  86.1 23.6 %all_to_all.40 = bf16[16,4,2688]{2,1,0:T(4,128)(2,1)} all-to-all(bf16[16,4,2688]{2,1,0:T(4,128)(2,1)S(1)} %broadcast_in_dim.9), channel_id=1, replica_groups=mesh['pool'=2,'y'=4,'z'=16,'tp'=4] {'z'}, dimensions={0} | all-to-all | bytes 688128 | tf_op jit(solution)/shard_map/all_to_all | solution.py:38
  109.7 1.1 broadcast_in_dim.10
  110.8 11.4 %collective-permute-done.5.refs_3_ = bf16[336,2560]{1,0:T(8,128)(2,1)} collective-permute-done((bf16[336,2560]{1,0:T(8,128)(2,1)}, bf16[336,2560]{1,0:T(8,128)(2,1)}, u32[]{:S(2)}, u32[]{:S(2)}) %collective-permute-start.5) | collective-permute-done | bytes 1720352 | tf_op jit(solution)/shard_map/ppermute | solution.py:30
  122.1 1.2 broadcast_in_dim.11
  123.3 2.8 %collective-permute-start.6 = (bf16[336,2560]{1,0:T(8,128)(2,1)}, bf16[336,2560]{1,0:T(8,128)(2,1)}, u32[]{:S(2)}, u32[]{:S(2)}) collective-permute-start(bf16[336,2560]{1,0:T(8,128)(2,1)} %collective-permute-done.5.refs_3_), channel_id=1, source_target_pairs={{0,256},{256,0},{1,257},{257,1},{2,258},{258,2},{3,259},{259,3},{4... | collective-permute-start | bytes 5160968 | tf_op jit(solution)/shard_map/ppermute | solution.py:34
  126.1 4.3 %all-to-all-start.4 = ((bf16[4,64,2688]{2,1,0:T(8,128)(2,1)}), bf16[4,64,2688]{2,1,0:T(8,128)(2,1)}, u32[]{:S(2)}, u32[]{:S(2)}) async-start(bf16[4,64,2688]{2,1,0:T(8,128)(2,1)} %broadcast_in_dim.11), calls=%async_computation.4 | async-start | bytes 2752512 | tf_op jit(solution)/shard_map/all_to_all | solution.py:38
  130.6 18.7 %all-to-all-done.4 = bf16[4,64,2688]{2,1,0:T(8,128)(2,1)} async-done(((bf16[4,64,2688]{2,1,0:T(8,128)(2,1)}), bf16[4,64,2688]{2,1,0:T(8,128)(2,1)}, u32[]{:S(2)}, u32[]{:S(2)}) %all-to-all-start.4) | async-done | bytes 1376288 | tf_op jit(solution)/shard_map/all_to_all | solution.py:38
  149.3 10.2 %shard_map.119 = bf16[256,2560]{1,0:T(8,128)(2,1)S(1)} custom-call(s32[8]{0:T(128)S(1)} %pad_add_fusion.ids_ref, bf16[256,2688]{1,0:T(8,128)(2,1)} %bitcast.7.x_hbm, bf16[336,2560]{1,0:T(8,128)(2,1)S(1)} %fusion.5.refs_0_, bf16[336,2560]{1,0:T(8,128)(2,1)} %collective-permute-done.refs_1_, bf16[336,2560]{1,0:T(8,128)(2,1)} %collective-permute-done.1.refs_2_, ...), custom_call_target="tpu_custom_call" | custom-call | flops 3523215360 | bytes 13762560 | tf_op jit(solution)/shard_map/pallas_call | solution.py:132
  159.4 19.4 %all_to_all.41 = bf16[4,64,2560]{2,1,0:T(8,128)(2,1)S(1)} all-to-all(bf16[4,64,2560]{2,1,0:T(8,128)(2,1)S(1)} %bitcast.15), channel_id=1, replica_groups=mesh['pool'=2,'y'=4,'z'=16,'tp'=4] {'y'}, dimensions={0} | all-to-all | bytes 2621440 | tf_op jit(solution)/shard_map/all_to_all | solution.py:38
  178.8 0.2 reduce_sum.111
  179.1 0.1 reshape.102
  179.1 21.6 %all_to_all.42 = bf16[16,4,2560]{2,1,0:T(4,128)(2,1)S(1)} all-to-all(bf16[16,4,2560]{2,1,0:T(4,128)(2,1)S(1)} %reshape.102), channel_id=1, replica_groups=mesh['pool'=2,'y'=4,'z'=16,'tp'=4] {'z'}, dimensions={0} | all-to-all | bytes 655360 | tf_op jit(solution)/shard_map/all_to_all | solution.py:38
  200.7 0.1 convert_reduce_fusion
  200.9 0.1 reshape.103
  201.0 16.1 %all_to_all.43 = bf16[8,4,320]{2,1,0:T(4,128)(2,1)S(1)} all-to-all(bf16[8,4,320]{2,1,0:T(4,128)(2,1)S(1)} %bitcast.20), channel_id=1, replica_groups=mesh['pool'=2,'y'=4,'z'=16,'tp'=4] {'pool','tp'}, dimensions={0} | all-to-all | bytes 40960 | tf_op jit(solution)/shard_map/all_to_all | solution.py:38
  217.1 0.6 reshape.104
  (34 shorter events, 0.3 us)
Async XLA Ops:
  0.0 72.4 %copy-start = (bf16[256,2560]{1,0:T(8,128)(2,1)S(1)}, bf16[256,2560]{1,0:T(8,128)(2,1)}, u32[]{:S(2)}) copy-start(bf16[256,2560]{1,0:T(8,128)(2,1)} %param.16) | copy-start | bytes 3932164
  0.0 8.8 %copy-start.3 = (bf16[32,256]{1,0:T(8,128)(2,1)S(1)}, bf16[32,256]{1,0:T(8,128)(2,1)}, u32[]{:S(2)}) copy-start(bf16[32,256]{1,0:T(8,128)(2,1)} %param.13) | copy-start | bytes 49156
  0.0 13.6 %copy-start.4 = (bf16[32,256]{1,0:T(8,128)(2,1)S(1)}, bf16[32,256]{1,0:T(8,128)(2,1)}, u32[]{:S(2)}) copy-start(bf16[32,256]{1,0:T(8,128)(2,1)} %param.15) | copy-start | bytes 49156
  0.0 13.6 %copy-start.5 = (bf16[32,256]{1,0:T(8,128)(2,1)S(1)}, bf16[32,256]{1,0:T(8,128)(2,1)}, u32[]{:S(2)}) copy-start(bf16[32,256]{1,0:T(8,128)(2,1)} %param.14) | copy-start | bytes 49156
  1.7 48.6 %collective-permute-start.1 = (bf16[336,2560]{1,0:T(8,128)(2,1)S(1)}, bf16[336,2560]{1,0:T(8,128)(2,1)}, u32[]{:S(2)}, u32[]{:S(2)}) collective-permute-start(bf16[336,2560]{1,0:T(8,128)(2,1)S(1)} %fusion.5.refs_0_), channel_id=1, source_target_pairs={{0,3},{1,0},{2,1},{3,2},{4,7},{5,4},{6,5},{7,6},{8,11},{9,8},{10,9... | collective-permute-start | bytes 5160968 | tf_op jit(solution)/shard_map/ppermute | solution.py:30
  6.9 43.4 %collective-permute-start = (bf16[336,2560]{1,0:T(8,128)(2,1)S(1)}, bf16[336,2560]{1,0:T(8,128)(2,1)}, u32[]{:S(2)}, u32[]{:S(2)}) collective-permute-start(bf16[336,2560]{1,0:T(8,128)(2,1)S(1)} %fusion.5.refs_0_), channel_id=1, source_target_pairs={{0,1},{1,2},{2,3},{3,0},{4,5},{5,6},{6,7},{7,4},{8,9},{9,10},{10,1... | collective-permute-start | bytes 5160968 | tf_op jit(solution)/shard_map/ppermute | solution.py:30
  9.4 38.6 %all-to-all-start = ((bf16[4,32,256]{2,1,0:T(8,128)(2,1)}), bf16[4,32,256]{2,1,0:T(8,128)(2,1)}, u32[]{:S(2)}, u32[]{:S(2)}) async-start(bf16[4,32,256]{2,1,0:T(8,128)(2,1)} %broadcast_in_dim.8), calls=%async_computation | async-start | bytes 131072 | tf_op jit(solution)/shard_map/all_to_all | solution.py:38
  49.6 0.6 copy-start.1
  50.2 29.2 %copy-start.2 = (f32[4,2560]{1,0:T(4,128)S(1)}, f32[4,2560]{1,0:T(4,128)}, u32[]{:S(2)}) copy-start(f32[4,2560]{1,0:T(4,128)} %param.17) | copy-start | bytes 122884
  50.3 23.2 %collective-permute-start.2 = (bf16[336,2560]{1,0:T(8,128)(2,1)S(1)}, bf16[336,2560]{1,0:T(8,128)(2,1)}, u32[]{:S(2)}, u32[]{:S(2)}) collective-permute-start(bf16[336,2560]{1,0:T(8,128)(2,1)S(1)} %fusion.5.refs_0_), channel_id=1, source_target_pairs={{0,256},{256,0},{1,257},{257,1},{2,258},{258,2},{3,259},{259,3},{4... | collective-permute-start | bytes 5160968 | tf_op jit(solution)/shard_map/ppermute | solution.py:34
  57.4 16.1 %collective-permute-start.4 = (bf16[336,2560]{1,0:T(8,128)(2,1)}, bf16[336,2560]{1,0:T(8,128)(2,1)}, u32[]{:S(2)}, u32[]{:S(2)}) collective-permute-start(bf16[336,2560]{1,0:T(8,128)(2,1)} %collective-permute-done.1.refs_2_), channel_id=1, source_target_pairs={{0,256},{256,0},{1,257},{257,1},{2,258},{258,2},{3,259},{259,3},{4... | collective-permute-start | bytes 5160968 | tf_op jit(solution)/shard_map/ppermute | solution.py:34
  59.3 14.2 %collective-permute-start.3 = (bf16[336,2560]{1,0:T(8,128)(2,1)}, bf16[336,2560]{1,0:T(8,128)(2,1)}, u32[]{:S(2)}, u32[]{:S(2)}) collective-permute-start(bf16[336,2560]{1,0:T(8,128)(2,1)} %collective-permute-done.refs_1_), channel_id=1, source_target_pairs={{0,256},{256,0},{1,257},{257,1},{2,258},{258,2},{3,259},{259,3},{4... | collective-permute-start | bytes 5160968 | tf_op jit(solution)/shard_map/ppermute | solution.py:34
  62.6 9.3 %all-to-all-start.1 = ((bf16[4,32,384]{2,1,0:T(8,128)(2,1)}), bf16[4,32,384]{2,1,0:T(8,128)(2,1)S(1)}, u32[]{:S(2)}, u32[]{:S(2)}) async-start(bf16[4,32,384]{2,1,0:T(8,128)(2,1)} %bitcast.16), calls=%async_computation.1 | async-start | bytes 196608 | tf_op jit(solution)/shard_map/all_to_all | solution.py:38
  73.5 11.4 %all-to-all-start.2 = ((bf16[8,4,2560]{2,1,0:T(4,128)(2,1)}), bf16[8,4,2560]{2,1,0:T(4,128)(2,1)S(1)}, u32[]{:S(2)}, u32[]{:S(2)}) async-start(bf16[8,4,2560]{2,1,0:T(4,128)(2,1)} %reshape.99), calls=%async_computation.2 | async-start | bytes 327680 | tf_op jit(solution)/shard_map/all_to_all | solution.py:38
  79.5 42.6 %collective-permute-start.5 = (bf16[336,2560]{1,0:T(8,128)(2,1)}, bf16[336,2560]{1,0:T(8,128)(2,1)}, u32[]{:S(2)}, u32[]{:S(2)}) collective-permute-start(bf16[336,2560]{1,0:T(8,128)(2,1)} %collective-permute-done.refs_1_), channel_id=1, source_target_pairs={{0,1},{1,2},{2,3},{3,0},{4,5},{5,6},{6,7},{7,4},{8,9},{9,10},{10,1... | collective-permute-start | bytes 5160968 | tf_op jit(solution)/shard_map/ppermute | solution.py:30
  123.3 7.2 %copy-start.6 = (s32[4]{0:T(128)S(1)}, s32[4]{0:T(128)}, u32[]{:S(2)}) copy-start(s32[4]{0:T(128)} %constant.47.clone) | copy-start | bytes 52
  123.3 26.0 %collective-permute-start.6 = (bf16[336,2560]{1,0:T(8,128)(2,1)}, bf16[336,2560]{1,0:T(8,128)(2,1)}, u32[]{:S(2)}, u32[]{:S(2)}) collective-permute-start(bf16[336,2560]{1,0:T(8,128)(2,1)} %collective-permute-done.5.refs_3_), channel_id=1, source_target_pairs={{0,256},{256,0},{1,257},{257,1},{2,258},{258,2},{3,259},{259,3},{4... | collective-permute-start | bytes 5160968 | tf_op jit(solution)/shard_map/ppermute | solution.py:34
  126.1 23.1 %all-to-all-start.4 = ((bf16[4,64,2688]{2,1,0:T(8,128)(2,1)}), bf16[4,64,2688]{2,1,0:T(8,128)(2,1)}, u32[]{:S(2)}, u32[]{:S(2)}) async-start(bf16[4,64,2688]{2,1,0:T(8,128)(2,1)} %broadcast_in_dim.11), calls=%async_computation.4 | async-start | bytes 2752512 | tf_op jit(solution)/shard_map/all_to_all | solution.py:38

commit v8 on v7

--- a/solution.py
+++ b/solution.py
@@ -1,3 +1,4 @@
+import functools
 import math
 
 import jax
@@ -82,12 +83,13 @@
     )
 
 
-def ffn_kernel(ids_ref, x_hbm, *refs):
-    parts = refs[: 2 * TP]
-    o_ref, x_ref, w_ref, act_ref, down_ref, sems = refs[2 * TP :]
+def ffn_kernel(count, ids_ref, x_hbm, *refs):
+    parts = refs[:count]
+    sums = refs[count : len(refs) - 6]
+    o_ref, x_ref, w_ref, act_ref, down_ref, sems = refs[len(refs) - 6 :]
     width = o_ref.shape[1]
     hidden = w_ref.shape[1] // 3
-    x_copy = pltpu.make_async_copy(x_hbm, x_ref, sems.at[2 * TP])
+    x_copy = pltpu.make_async_copy(x_hbm, x_ref, sems.at[count])
     x_copy.start()
     copies = []
     for i, part in enumerate(parts):
@@ -96,59 +98,62 @@
     x_copy.wait()
     x = x_ref[:, :width]
     route = x_ref[:, width:].astype(F32).T
-    scales = []
-    for e in range(2 * TP):
-        scale = jnp.zeros((1, x.shape[0]), F32)
-        for k in range(2):
-            value = route[2 + k : 3 + k] + route[4 + k : 5 + k]
-            scale += jnp.where(route[k : k + 1] == ids_ref[e].astype(F32), value, 0.0)
-        scales.append(scale)
-    each = 4
-    for first in range(0, 2 * TP, each):
-        for i in range(first, first + each):
+    each = 3
+    for first in range(0, count, each):
+        group = range(first, min(first + each, count))
+        for i in group:
             copies[i].wait()
         both = lax.dot_general(
-            jnp.concatenate([w_ref[i, : 2 * hidden] for i in range(first, first + each)], 0),
+            jnp.concatenate([w_ref[i, : 2 * hidden] for i in group], 0),
             x,
             (((1,), (1,)), ((), ())),
             preferred_element_type=F32,
         )
-        for i in range(first, first + each):
+        for i in group:
+            scale = jnp.zeros((1, x.shape[0]), F32)
+            for k in range(2):
+                value = route[2 + k : 3 + k] + route[4 + k : 5 + k]
+                scale += jnp.where(route[k : k + 1] == ids_ref[i].astype(F32), value, 0.0)
             gate = both[2 * (i - first) * hidden : (2 * (i - first) + 1) * hidden]
             up = both[(2 * (i - first) + 1) * hidden : (2 * (i - first) + 2) * hidden]
             here = slice(i * hidden, (i + 1) * hidden)
-            act = gate / (1.0 + jnp.exp(-gate)) * up * scales[i]
-            act_ref[here] = act.astype(BF16)
+            act_ref[here] = (gate / (1.0 + jnp.exp(-gate)) * up * scale).astype(BF16)
             down_ref[here] = w_ref[i, 2 * hidden :]
-    o_ref[...] = lax.dot_general(
+    out = lax.dot_general(
         act_ref[...], down_ref[...], (((0,), (0,)), ((), ())), preferred_element_type=F32
-    ).astype(BF16)
-
-
-def ffn(ids, x, mine, other):
+    )
+    for so_far in sums:
+        out += so_far[...]
+    o_ref[...] = out.astype(o_ref.dtype)
+
+
+def ffn(ids, x, parts, sums, dtype):
     rows = x.shape[0]
-    depth, width = mine[0].shape
-    units = 2 * TP * (depth // 3)
+    count = len(parts)
+    depth, width = parts[0].shape
+    units = count * (depth // 3)
+    vmem = pl.BlockSpec(memory_space=pltpu.VMEM)
     return pl.pallas_call(
-        ffn_kernel,
-        out_shape=jax.ShapeDtypeStruct((rows, width), BF16),
+        functools.partial(ffn_kernel, count),
+        out_shape=jax.ShapeDtypeStruct((rows, width), dtype),
         in_specs=[pl.BlockSpec(memory_space=pltpu.SMEM)]
-        + [pl.BlockSpec(memory_space=pl.ANY)] * (1 + 2 * TP),
-        out_specs=pl.BlockSpec(memory_space=pltpu.VMEM),
+        + [pl.BlockSpec(memory_space=pl.ANY)] * (1 + count)
+        + [vmem] * len(sums),
+        out_specs=vmem,
         scratch_shapes=[
             pltpu.VMEM(x.shape, BF16),
-            pltpu.VMEM((2 * TP, depth, width), BF16),
+            pltpu.VMEM((count, depth, width), BF16),
             pltpu.VMEM((units, rows), BF16),
             pltpu.VMEM((units, width), BF16),
-            pltpu.SemaphoreType.DMA((2 * TP + 1,)),
+            pltpu.SemaphoreType.DMA((count + 1,)),
         ],
-        compiler_params=pltpu.CompilerParams(vmem_limit_bytes=36 << 20),
+        compiler_params=pltpu.CompilerParams(vmem_limit_bytes=30 << 20),
         cost_estimate=pl.CostEstimate(
-            flops=4 * rows * width * depth * TP,
-            bytes_accessed=4 * width * depth * TP,
+            flops=16 * rows * width * depth * count,
+            bytes_accessed=16 * width * depth * count,
             transcendentals=0,
         ),
-    )(ids, x, *mine, *other)
+    )(ids, x, *parts, *sums)
 
 
 def body(
@@ -181,9 +186,8 @@
     )
     partial = attend(queries, key_value)
 
-    packed, before, after, partial = lax.optimization_barrier((packed, before, after, partial))
-    mine = [packed, before, after]
-    other = [swap(w) for w in mine]
+    before, after, partial = lax.optimization_barrier((before, after, partial))
+    across = shift(before, "tp", 1)
     partial = exchange(partial.reshape(Y, rows, (heads + 1) * HD), "y").astype(F32)
     outs = []
     for h in range(heads):
@@ -196,8 +200,6 @@
 
     projected = jnp.dot(heads_out, w_out, preferred_element_type=F32).astype(BF16)
     projected = projected.reshape(2 * TP, own_rows, width)
-    before, projected, *other = lax.optimization_barrier((before, projected, *other))
-    across = shift(before, "tp", 1)
     projected = exchange(projected, GROUP)
     attention = jnp.sum(projected.astype(F32), axis=0)
     own_tokens = lax.dynamic_slice_in_dim(tokens, group * own_rows, own_rows, 0).astype(F32)
@@ -218,13 +220,15 @@
     sent = jnp.concatenate([normed, route], 1)
     copies = copies_of(sent, Z)
     copies = copies_of(exchange(copies, "z").reshape(Z * own_rows, width + HD), Y)
-    across, copies = lax.optimization_barrier((across, copies))
-    mine.append(across)
-    other.append(swap(across))
+    packed, before, after, copies = lax.optimization_barrier((packed, before, after, copies))
+    early = [packed, before, after]
+    across_tied, _ = lax.optimization_barrier((across, copies))
+    late = [across] + [swap(w) for w in early + [across_tied]]
     rows_in = exchange(copies, "y").reshape(Y * Z * own_rows, width + HD)
     near = (tp + jnp.array([0, TP - 1, 1, 2], jnp.int32)) % TP
     ids = jnp.concatenate([pool * TP + near, (1 - pool) * TP + near]).astype(jnp.int32)
-    mixed = ffn(ids, rows_in, mine, other)
+    mixed = ffn(ids[:3], rows_in, early, [], F32)
+    mixed = ffn(ids[3:], rows_in, late, [mixed], BF16)
 
     mixed = exchange(mixed.reshape(Y, Z * own_rows, width), "y")
     mixed = jnp.sum(mixed.astype(F32), axis=0).astype(BF16)

time: 219 us -> 204 us (0.932)
  waiting for transfers between devices: 35.9 us -> 5.84 us
  starting transfers between devices: 43.7 us -> 49.9 us
  Pallas kernels: 11.7 us -> 15.9 us
  blocking collectives: 115 us -> 118 us
    all_to_all x4, waiting for transfers between devices: 24.5 us -> 5.82 us  [exchange(): return lax.all_to_all(x, axis, split_axis=0, concat_axis=0, tiled=True)]
    ppermute x3, waiting for transfers between devices: 11.4 us -> 0.01 us  [shift(): return lax.ppermute(x, axis, [(i, (i + count) % size) for i in range(size)])]
    all_to_all x4, starting transfers between devices: 19 us -> 24 us  [exchange(): return lax.all_to_all(x, axis, split_axis=0, concat_axis=0, tiled=True)]
    pallas_call x1 -> x2, Pallas kernels: 10.2 us -> 14.4 us  [ffn(): pl.pallas_call(functools.partial(ffn_kernel, count), out_shape=jax.ShapeD...]
    all_to_all x4, blocking collectives: 80.6 us -> 84.3 us  [exchange(): return lax.all_to_all(x, axis, split_axis=0, concat_axis=0, tiled=True)]
  transfers between devices with their start and end apart: 11 -> 11, of which waited for: 4 -> 2; matrix products, arithmetic and copies ran while one was open for 3% -> 4% of each run, Pallas kernels for 1% -> 4%
where the time goes in v8:
time: 204 us; the launch traced here: 203 us
  blocking collectives  118 us (58%)
  starting transfers between devices  49.9 us (24%)
  Pallas kernels  15.9 us (8%)
  local copies, waits for them, and re-layouts  7.6 us (4%)
  waiting for transfers between devices  5.84 us (3%)
  other arithmetic  5.22 us (3%)
    all_to_all x4, blocking collectives, exchange(): return lax.all_to_all(x, axis, split_axis=0, concat_axis=0, tiled=True)  84.3 us
    all_gather x1, blocking collectives, body(): lax.all_gather(jnp.concatenate([key_proj, value_proj], 1), 'z', axis=0, t...  34 us
    all_to_all x4, starting transfers between devices, exchange(): return lax.all_to_all(x, axis, split_axis=0, concat_axis=0, tiled=True)  24 us
    ppermute x4, starting transfers between devices, swap(): return lax.ppermute(x, 'pool', [(0, 1), (1, 0)])  15.4 us
    pallas_call x2, Pallas kernels, ffn(): pl.pallas_call(functools.partial(ffn_kernel, count), out_shape=jax.ShapeD...  14.4 us
    ppermute x3, starting transfers between devices, shift(): return lax.ppermute(x, axis, [(i, (i + count) % size) for i in range(size)])  10.4 us
    all_to_all x4, waiting for transfers between devices, exchange(): return lax.all_to_all(x, axis, split_axis=0, concat_axis=0, tiled=True)  5.82 us
  transfers between devices with their start and end apart: 11, of which 2 were waited for; matrix products, arithmetic and copies ran while one was open for 4% of the time, Pallas kernels for 4%

profile of v8, /device:TPU:1, one launch (start us, length us, event | category | flops | bytes accessed | tf_op | source)
XLA Modules:
  0.0 203.3 jit_solution(7440927123047289214)
XLA Ops:
  0.0 1.6 fusion.5.refs_0_
  1.7 4.0 %collective-permute-start = (bf16[336,2560]{1,0:T(8,128)(2,1)S(1)}, bf16[336,2560]{1,0:T(8,128)(2,1)}, u32[]{:S(2)}, u32[]{:S(2)}) collective-permute-start(bf16[336,2560]{1,0:T(8,128)(2,1)S(1)} %fusion.5.refs_0_), channel_id=1, source_target_pairs={{0,1},{1,2},{2,3},{3,0},{4,5},{5,6},{6,7},{7,4},{8,9},{9,10},{10,1... | collective-permute-start | bytes 5160968 | tf_op jit(solution)/shard_map/ppermute | solution.py:31
  5.6 3.2 %collective-permute-start.1 = (bf16[336,2560]{1,0:T(8,128)(2,1)S(1)}, bf16[336,2560]{1,0:T(8,128)(2,1)}, u32[]{:S(2)}, u32[]{:S(2)}) collective-permute-start(bf16[336,2560]{1,0:T(8,128)(2,1)S(1)} %fusion.5.refs_0_), channel_id=1, source_target_pairs={{0,3},{1,0},{2,1},{3,2},{4,7},{5,4},{6,5},{7,6},{8,11},{9,8},{10,9... | collective-permute-start | bytes 5160968 | tf_op jit(solution)/shard_map/ppermute | solution.py:31
  8.8 0.6 broadcast_in_dim.8
  9.4 4.4 %all-to-all-start = ((bf16[4,32,256]{2,1,0:T(8,128)(2,1)}), bf16[4,32,256]{2,1,0:T(8,128)(2,1)}, u32[]{:S(2)}, u32[]{:S(2)}) async-start(bf16[4,32,256]{2,1,0:T(8,128)(2,1)} %broadcast_in_dim.8), calls=%async_computation | async-start | bytes 131072 | tf_op jit(solution)/shard_map/all_to_all | solution.py:39
  13.9 0.7 copy.35
  14.6 34.0 %all_gather.3.kv_ref = bf16[512,512]{1,0:T(8,128)(2,1)S(1)} all-gather(bf16[32,512]{1,0:T(8,128)(2,1)S(1)} %pad_maximum_fusion), channel_id=1, replica_groups=mesh['pool'=2,'y'=4,'z'=16,'tp'=4] {'z'}, dimensions={0}, use_global_device_ids=true | all-gather | bytes 557056 | tf_op jit(solution)/shard_map/all_gather | solution.py:184
  48.6 1.3 reduce-precision_convert_fusion
  49.9 1.5 shard_map.118
  51.4 0.6 copy-done.1
  52.1 4.3 %all-to-all-start.1 = ((bf16[4,32,384]{2,1,0:T(8,128)(2,1)}), bf16[4,32,384]{2,1,0:T(8,128)(2,1)S(1)}, u32[]{:S(2)}, u32[]{:S(2)}) async-start(bf16[4,32,384]{2,1,0:T(8,128)(2,1)} %bitcast.17), calls=%async_computation.1 | async-start | bytes 196608 | tf_op jit(solution)/shard_map/all_to_all | solution.py:39
  56.4 0.7 constant_dynamic-slice_fusion.1
  57.2 0.1 copy.34
  57.3 3.8 %all-to-all-done.1 = bf16[4,32,384]{2,1,0:T(8,128)(2,1)S(1)} async-done(((bf16[4,32,384]{2,1,0:T(8,128)(2,1)}), bf16[4,32,384]{2,1,0:T(8,128)(2,1)S(1)}, u32[]{:S(2)}, u32[]{:S(2)}) %all-to-all-start.1) | async-done | bytes 98336 | tf_op jit(solution)/shard_map/all_to_all | solution.py:39
  61.1 0.2 slice_reduce_fusion.1
  61.3 0.1 fusion.7
  61.4 0.1 divide_convert_fusion.1
  61.5 0.1 divide_convert_fusion
  61.6 0.3 convolution_convert_fusion
  61.9 0.8 reshape.99
  62.7 10.9 %all-to-all-start.2 = ((bf16[8,4,2560]{2,1,0:T(4,128)(2,1)}), bf16[8,4,2560]{2,1,0:T(4,128)(2,1)S(1)}, u32[]{:S(2)}, u32[]{:S(2)}) async-start(bf16[8,4,2560]{2,1,0:T(4,128)(2,1)} %reshape.99), calls=%async_computation.2 | async-start | bytes 327680 | tf_op jit(solution)/shard_map/all_to_all | solution.py:39
  73.5 0.1 fusion.16
  73.6 0.1 slice_reduce_fusion.3
  73.7 3.3 %collective-permute-start.2 = (bf16[336,2560]{1,0:T(8,128)(2,1)}, bf16[336,2560]{1,0:T(8,128)(2,1)}, u32[]{:S(2)}, u32[]{:S(2)}) collective-permute-start(bf16[336,2560]{1,0:T(8,128)(2,1)} %collective-permute-done.refs_1_), channel_id=1, source_target_pairs={{0,1},{1,2},{2,3},{3,0},{4,5},{5,6},{6,7},{7,4},{8,9},{9,10},{10,1... | collective-permute-start | bytes 5160968 | tf_op jit(solution)/shard_map/ppermute | solution.py:31
  77.0 2.0 all-to-all-done.2
  79.0 0.1 convert_reduce_fusion.1
  79.1 0.9 fusion.19
  80.1 0.1 add_convert_fusion.1
  80.2 0.1 broadcast_in_dim.9
  80.3 22.1 %all_to_all.40 = bf16[16,4,2688]{2,1,0:T(4,128)(2,1)S(1)} all-to-all(bf16[16,4,2688]{2,1,0:T(4,128)(2,1)S(1)} %broadcast_in_dim.9), channel_id=1, replica_groups=mesh['pool'=2,'y'=4,'z'=16,'tp'=4] {'z'}, dimensions={0} | all-to-all | bytes 688128 | tf_op jit(solution)/shard_map/all_to_all | solution.py:39
  102.3 0.8 broadcast_in_dim.10
  103.2 2.2 %broadcast_in_dim.11 = bf16[4,64,2688]{2,1,0:T(8,128)(2,1)} broadcast(bf16[64,2688]{1,0:T(8,128)(2,1)} %broadcast_in_dim.10), dimensions={1,2} | broadcast | bytes 1720320 | tf_op jit(solution)/shard_map/broadcast_in_dim | solution.py:22
  105.3 4.4 %all-to-all-start.4 = ((bf16[4,64,2688]{2,1,0:T(8,128)(2,1)}), bf16[4,64,2688]{2,1,0:T(8,128)(2,1)}, u32[]{:S(2)}, u32[]{:S(2)}) async-start(bf16[4,64,2688]{2,1,0:T(8,128)(2,1)} %broadcast_in_dim.11), calls=%async_computation.4 | async-start | bytes 2752512 | tf_op jit(solution)/shard_map/all_to_all | solution.py:39
  109.8 9.2 %collective-permute-start.3 = (bf16[336,2560]{1,0:T(8,128)(2,1)S(1)}, bf16[336,2560]{1,0:T(8,128)(2,1)}, u32[]{:S(2)}, u32[]{:S(2)}) collective-permute-start(bf16[336,2560]{1,0:T(8,128)(2,1)S(1)} %fusion.5.refs_0_), channel_id=1, source_target_pairs={{0,256},{256,0},{1,257},{257,1},{2,258},{258,2},{3,259},{259,3},{4... | collective-permute-start | bytes 5160968 | tf_op jit(solution)/shard_map/ppermute | solution.py:35
  119.0 1.9 collective-permute-start.4
  120.9 2.4 %collective-permute-start.5 = (bf16[336,2560]{1,0:T(8,128)(2,1)}, bf16[336,2560]{1,0:T(8,128)(2,1)}, u32[]{:S(2)}, u32[]{:S(2)}) collective-permute-start(bf16[336,2560]{1,0:T(8,128)(2,1)} %collective-permute-done.1.refs_2_), channel_id=1, source_target_pairs={{0,256},{256,0},{1,257},{257,1},{2,258},{258,2},{3,259},{259,3},{4... | collective-permute-start | bytes 5160968 | tf_op jit(solution)/shard_map/ppermute | solution.py:35
  123.3 1.9 collective-permute-start.6
  125.3 0.1 pad_add_fusion
  125.4 6.3 %shard_map.119.refs_5_ = f32[256,2560]{1,0:T(8,128)S(1)} custom-call(s32[3]{0:T(128)S(1)} %bitcast.18, bf16[256,2688]{1,0:T(8,128)(2,1)} %bitcast.7.x_hbm, bf16[336,2560]{1,0:T(8,128)(2,1)S(1)} %fusion.5.refs_0_, bf16[336,2560]{1,0:T(8,128)(2,1)} %collective-permute-done.refs_1_, bf16[336,2560]{1,0:T(8,128)(2,1)} %collective-permute-done.1.refs_2_), custom_call_target="tpu_custom_call" | custom-call | flops 10569646080 | bytes 41287680 | tf_op jit(solution)/shard_map/pallas_call | solution.py:136
  131.8 8.1 %shard_map.120 = bf16[256,2560]{1,0:T(8,128)(2,1)S(1)} custom-call(s32[5]{0:T(128)S(1)} %slice.36.ids_ref, bf16[256,2688]{1,0:T(8,128)(2,1)} %bitcast.7.x_hbm, bf16[336,2560]{1,0:T(8,128)(2,1)} %collective-permute-done.2.refs_0_, bf16[336,2560]{1,0:T(8,128)(2,1)} %collective-permute-done.3.refs_1_, bf16[336,2560]{1,0:T(8,128)(2,1)} %collective-permute-done.4.refs_2_, ...), custom_call_target="tpu_custom_call" | custom-call | flops 17616076800 | bytes 68812800 | tf_op jit(solution)/shard_map/pallas_call | solution.py:136
  139.9 19.7 %all_to_all.41 = bf16[4,64,2560]{2,1,0:T(8,128)(2,1)S(1)} all-to-all(bf16[4,64,2560]{2,1,0:T(8,128)(2,1)S(1)} %bitcast.16), channel_id=1, replica_groups=mesh['pool'=2,'y'=4,'z'=16,'tp'=4] {'y'}, dimensions={0} | all-to-all | bytes 2621440 | tf_op jit(solution)/shard_map/all_to_all | solution.py:39
  159.6 0.2 reduce_sum.111
  159.8 0.1 reshape.102
  159.9 27.0 %all_to_all.42 = bf16[16,4,2560]{2,1,0:T(4,128)(2,1)S(1)} all-to-all(bf16[16,4,2560]{2,1,0:T(4,128)(2,1)S(1)} %reshape.102), channel_id=1, replica_groups=mesh['pool'=2,'y'=4,'z'=16,'tp'=4] {'z'}, dimensions={0} | all-to-all | bytes 655360 | tf_op jit(solution)/shard_map/all_to_all | solution.py:39
  186.9 0.1 convert_reduce_fusion
  187.0 0.1 reshape.103
  187.2 15.5 %all_to_all.43 = bf16[8,4,320]{2,1,0:T(4,128)(2,1)S(1)} all-to-all(bf16[8,4,320]{2,1,0:T(4,128)(2,1)S(1)} %bitcast.22), channel_id=1, replica_groups=mesh['pool'=2,'y'=4,'z'=16,'tp'=4] {'pool','tp'}, dimensions={0} | all-to-all | bytes 40960 | tf_op jit(solution)/shard_map/all_to_all | solution.py:39
  202.7 0.6 reshape.104
  (42 shorter events, 0.4 us)
Async XLA Ops:
  0.0 61.6 %copy-start = (bf16[256,2560]{1,0:T(8,128)(2,1)S(1)}, bf16[256,2560]{1,0:T(8,128)(2,1)}, u32[]{:S(2)}) copy-start(bf16[256,2560]{1,0:T(8,128)(2,1)} %param.16) | copy-start | bytes 3932164
  0.0 8.8 %copy-start.3 = (bf16[32,256]{1,0:T(8,128)(2,1)S(1)}, bf16[32,256]{1,0:T(8,128)(2,1)}, u32[]{:S(2)}) copy-start(bf16[32,256]{1,0:T(8,128)(2,1)} %param.13) | copy-start | bytes 49156
  0.0 13.8 %copy-start.8 = (f32[32,2]{0,1:T(2,128)S(1)}, f32[32,2]{0,1:T(2,128)}, u32[]{:S(2)}) copy-start(f32[32,2]{0,1:T(2,128)} %param.19) | copy-start | bytes 772
  0.0 14.6 %copy-start.4 = (bf16[32,256]{1,0:T(8,128)(2,1)S(1)}, bf16[32,256]{1,0:T(8,128)(2,1)}, u32[]{:S(2)}) copy-start(bf16[32,256]{1,0:T(8,128)(2,1)} %param.15) | copy-start | bytes 49156
  0.0 14.5 %copy-start.5 = (bf16[32,256]{1,0:T(8,128)(2,1)S(1)}, bf16[32,256]{1,0:T(8,128)(2,1)}, u32[]{:S(2)}) copy-start(bf16[32,256]{1,0:T(8,128)(2,1)} %param.14) | copy-start | bytes 49156
  1.7 50.4 %collective-permute-start = (bf16[336,2560]{1,0:T(8,128)(2,1)S(1)}, bf16[336,2560]{1,0:T(8,128)(2,1)}, u32[]{:S(2)}, u32[]{:S(2)}) collective-permute-start(bf16[336,2560]{1,0:T(8,128)(2,1)S(1)} %fusion.5.refs_0_), channel_id=1, source_target_pairs={{0,1},{1,2},{2,3},{3,0},{4,5},{5,6},{6,7},{7,4},{8,9},{9,10},{10,1... | collective-permute-start | bytes 5160968 | tf_op jit(solution)/shard_map/ppermute | solution.py:31
  5.6 46.4 %collective-permute-start.1 = (bf16[336,2560]{1,0:T(8,128)(2,1)S(1)}, bf16[336,2560]{1,0:T(8,128)(2,1)}, u32[]{:S(2)}, u32[]{:S(2)}) collective-permute-start(bf16[336,2560]{1,0:T(8,128)(2,1)S(1)} %fusion.5.refs_0_), channel_id=1, source_target_pairs={{0,3},{1,0},{2,1},{3,2},{4,7},{5,4},{6,5},{7,6},{8,11},{9,8},{10,9... | collective-permute-start | bytes 5160968 | tf_op jit(solution)/shard_map/ppermute | solution.py:31
  9.4 40.4 %all-to-all-start = ((bf16[4,32,256]{2,1,0:T(8,128)(2,1)}), bf16[4,32,256]{2,1,0:T(8,128)(2,1)}, u32[]{:S(2)}, u32[]{:S(2)}) async-start(bf16[4,32,256]{2,1,0:T(8,128)(2,1)} %broadcast_in_dim.8), calls=%async_computation | async-start | bytes 131072 | tf_op jit(solution)/shard_map/all_to_all | solution.py:39
  51.4 0.6 copy-start.1
  52.0 21.5 %copy-start.6 = (bf16[4,2]{1,0:T(4,128)(2,1)S(1)}, bf16[4,2]{1,0:T(4,128)(2,1)}, u32[]{:S(2)}) copy-start(bf16[4,2]{1,0:T(4,128)(2,1)} %get-tuple-element.38) | copy-start | bytes 52
  52.0 21.5 %copy-start.7 = (bf16[4,2]{1,0:T(4,128)(2,1)S(1)}, bf16[4,2]{1,0:T(4,128)(2,1)}, u32[]{:S(2)}) copy-start(bf16[4,2]{1,0:T(4,128)(2,1)} %get-tuple-element.39) | copy-start | bytes 52
  52.0 21.6 %copy-start.2 = (f32[4,2560]{1,0:T(4,128)S(1)}, f32[4,2560]{1,0:T(4,128)}, u32[]{:S(2)}) copy-start(f32[4,2560]{1,0:T(4,128)} %param.17) | copy-start | bytes 122884
  52.1 9.0 %all-to-all-start.1 = ((bf16[4,32,384]{2,1,0:T(8,128)(2,1)}), bf16[4,32,384]{2,1,0:T(8,128)(2,1)S(1)}, u32[]{:S(2)}, u32[]{:S(2)}) async-start(bf16[4,32,384]{2,1,0:T(8,128)(2,1)} %bitcast.17), calls=%async_computation.1 | async-start | bytes 196608 | tf_op jit(solution)/shard_map/all_to_all | solution.py:39
  62.7 16.4 %all-to-all-start.2 = ((bf16[8,4,2560]{2,1,0:T(4,128)(2,1)}), bf16[8,4,2560]{2,1,0:T(4,128)(2,1)S(1)}, u32[]{:S(2)}, u32[]{:S(2)}) async-start(bf16[8,4,2560]{2,1,0:T(4,128)(2,1)} %reshape.99), calls=%async_computation.2 | async-start | bytes 327680 | tf_op jit(solution)/shard_map/all_to_all | solution.py:39
  73.7 49.6 %collective-permute-start.2 = (bf16[336,2560]{1,0:T(8,128)(2,1)}, bf16[336,2560]{1,0:T(8,128)(2,1)}, u32[]{:S(2)}, u32[]{:S(2)}) collective-permute-start(bf16[336,2560]{1,0:T(8,128)(2,1)} %collective-permute-done.refs_1_), channel_id=1, source_target_pairs={{0,1},{1,2},{2,3},{3,0},{4,5},{5,6},{6,7},{7,4},{8,9},{9,10},{10,1... | collective-permute-start | bytes 5160968 | tf_op jit(solution)/shard_map/ppermute | solution.py:31
  105.3 19.9 %copy-start.9 = (s32[4]{0:T(128)S(1)}, s32[4]{0:T(128)}, u32[]{:S(2)}) copy-start(s32[4]{0:T(128)} %constant.47.clone) | copy-start | bytes 52
  105.3 20.1 %all-to-all-start.4 = ((bf16[4,64,2688]{2,1,0:T(8,128)(2,1)}), bf16[4,64,2688]{2,1,0:T(8,128)(2,1)}, u32[]{:S(2)}, u32[]{:S(2)}) async-start(bf16[4,64,2688]{2,1,0:T(8,128)(2,1)} %broadcast_in_dim.11), calls=%async_computation.4 | async-start | bytes 2752512 | tf_op jit(solution)/shard_map/all_to_all | solution.py:39
  109.8 22.0 %collective-permute-start.3 = (bf16[336,2560]{1,0:T(8,128)(2,1)S(1)}, bf16[336,2560]{1,0:T(8,128)(2,1)}, u32[]{:S(2)}, u32[]{:S(2)}) collective-permute-start(bf16[336,2560]{1,0:T(8,128)(2,1)S(1)} %fusion.5.refs_0_), channel_id=1, source_target_pairs={{0,256},{256,0},{1,257},{257,1},{2,258},{258,2},{3,259},{259,3},{4... | collective-permute-start | bytes 5160968 | tf_op jit(solution)/shard_map/ppermute | solution.py:35
  119.0 12.8 %collective-permute-start.4 = (bf16[336,2560]{1,0:T(8,128)(2,1)}, bf16[336,2560]{1,0:T(8,128)(2,1)}, u32[]{:S(2)}, u32[]{:S(2)}) collective-permute-start(bf16[336,2560]{1,0:T(8,128)(2,1)} %collective-permute-done.refs_1_), channel_id=1, source_target_pairs={{0,256},{256,0},{1,257},{257,1},{2,258},{258,2},{3,259},{259,3},{4... | collective-permute-start | bytes 5160968 | tf_op jit(solution)/shard_map/ppermute | solution.py:35
  120.9 10.9 %collective-permute-start.5 = (bf16[336,2560]{1,0:T(8,128)(2,1)}, bf16[336,2560]{1,0:T(8,128)(2,1)}, u32[]{:S(2)}, u32[]{:S(2)}) collective-permute-start(bf16[336,2560]{1,0:T(8,128)(2,1)} %collective-permute-done.1.refs_2_), channel_id=1, source_target_pairs={{0,256},{256,0},{1,257},{257,1},{2,258},{258,2},{3,259},{259,3},{4... | collective-permute-start | bytes 5160968 | tf_op jit(solution)/shard_map/ppermute | solution.py:35
  123.3 8.5 %collective-permute-start.6 = (bf16[336,2560]{1,0:T(8,128)(2,1)}, bf16[336,2560]{1,0:T(8,128)(2,1)}, u32[]{:S(2)}, u32[]{:S(2)}) collective-permute-start(bf16[336,2560]{1,0:T(8,128)(2,1)} %collective-permute-done.2.refs_0_), channel_id=1, source_target_pairs={{0,256},{256,0},{1,257},{257,1},{2,258},{258,2},{3,259},{259,3},{4... | collective-permute-start | bytes 5160968 | tf_op jit(solution)/shard_map/ppermute | solution.py:35

commit v9 on v8

--- a/solution.py
+++ b/solution.py
@@ -83,77 +83,134 @@
     )
 
 
-def ffn_kernel(count, ids_ref, x_hbm, *refs):
-    parts = refs[:count]
-    sums = refs[count : len(refs) - 6]
-    o_ref, x_ref, w_ref, act_ref, down_ref, sems = refs[len(refs) - 6 :]
-    width = o_ref.shape[1]
-    hidden = w_ref.shape[1] // 3
-    x_copy = pltpu.make_async_copy(x_hbm, x_ref, sems.at[count])
+def hidden_units(ids_ref, x, weights, route):
+    hidden = weights[0].shape[0] // 2
+    both = lax.dot_general(
+        jnp.concatenate(weights, 0), x, (((1,), (1,)), ((), ())), preferred_element_type=F32
+    )
+    acts = []
+    for i in range(len(weights)):
+        scale = jnp.zeros((1, x.shape[0]), F32)
+        for k in range(2):
+            value = route[2 + k : 3 + k] + route[4 + k : 5 + k]
+            scale += jnp.where(route[k : k + 1] == ids_ref[i].astype(F32), value, 0.0)
+        gate = both[2 * i * hidden : (2 * i + 1) * hidden]
+        up = both[(2 * i + 1) * hidden : (2 * i + 2) * hidden]
+        acts.append((gate / (1.0 + jnp.exp(-gate)) * up * scale).astype(BF16))
+    return jnp.concatenate(acts, 0)
+
+
+def early_kernel(ids_ref, x_hbm, *refs):
+    o_ref, x_ref, w_ref, sems = refs[-4:]
+    parts = refs[:-4]
+    width = w_ref.shape[2]
+    copies = [pltpu.make_async_copy(x_hbm, x_ref, sems.at[len(parts)])]
+    for i, part in enumerate(parts):
+        copies.append(
+            pltpu.make_async_copy(part.at[pl.ds(0, w_ref.shape[1])], w_ref.at[i], sems.at[i])
+        )
+    for copy in copies:
+        copy.start()
+    for copy in copies:
+        copy.wait()
+    o_ref[...] = hidden_units(
+        ids_ref,
+        x_ref[:, :width],
+        [w_ref[i] for i in range(len(parts))],
+        x_ref[:, width:].astype(F32).T,
+    )
+
+
+def late_kernel(count, ids_ref, x_hbm, units_ref, *refs):
+    o_ref, x_ref, w_ref, act_ref, down_ref, sems = refs[-6:]
+    parts = refs[:-6]
+    width = w_ref.shape[2]
+    hidden = w_ref.shape[1] // 2
+    early = len(parts) - count
+    x_copy = pltpu.make_async_copy(x_hbm, x_ref, sems.at[0])
     x_copy.start()
-    copies = []
+    wide = []
+    for i, part in enumerate(parts[early:]):
+        wide.append(
+            pltpu.make_async_copy(part.at[pl.ds(0, 2 * hidden)], w_ref.at[i], sems.at[1 + i])
+        )
+        wide[i].start()
+    tall = []
     for i, part in enumerate(parts):
-        copies.append(pltpu.make_async_copy(part, w_ref.at[i], sems.at[i]))
-        copies[i].start()
+        tall.append(
+            pltpu.make_async_copy(
+                part.at[pl.ds(2 * hidden, hidden)],
+                down_ref.at[pl.ds(i * hidden, hidden)],
+                sems.at[1 + count + i],
+            )
+        )
+        tall[i].start()
+    act_ref[: early * hidden] = units_ref[...]
     x_copy.wait()
     x = x_ref[:, :width]
     route = x_ref[:, width:].astype(F32).T
     each = 3
     for first in range(0, count, each):
-        group = range(first, min(first + each, count))
-        for i in group:
-            copies[i].wait()
-        both = lax.dot_general(
-            jnp.concatenate([w_ref[i, : 2 * hidden] for i in group], 0),
+        last = min(first + each, count)
+        for i in range(first, last):
+            wide[i].wait()
+        act_ref[(early + first) * hidden : (early + last) * hidden] = hidden_units(
+            ids_ref.at[pl.ds(first, last - first)],
             x,
-            (((1,), (1,)), ((), ())),
-            preferred_element_type=F32,
+            [w_ref[i] for i in range(first, last)],
+            route,
         )
-        for i in group:
-            scale = jnp.zeros((1, x.shape[0]), F32)
-            for k in range(2):
-                value = route[2 + k : 3 + k] + route[4 + k : 5 + k]
-                scale += jnp.where(route[k : k + 1] == ids_ref[i].astype(F32), value, 0.0)
-            gate = both[2 * (i - first) * hidden : (2 * (i - first) + 1) * hidden]
-            up = both[(2 * (i - first) + 1) * hidden : (2 * (i - first) + 2) * hidden]
-            here = slice(i * hidden, (i + 1) * hidden)
-            act_ref[here] = (gate / (1.0 + jnp.exp(-gate)) * up * scale).astype(BF16)
-            down_ref[here] = w_ref[i, 2 * hidden :]
-    out = lax.dot_general(
+    for copy in tall:
+        copy.wait()
+    o_ref[...] = lax.dot_general(
         act_ref[...], down_ref[...], (((0,), (0,)), ((), ())), preferred_element_type=F32
-    )
-    for so_far in sums:
-        out += so_far[...]
-    o_ref[...] = out.astype(o_ref.dtype)
-
-
-def ffn(ids, x, parts, sums, dtype):
+    ).astype(BF16)
+
+
+def ffn(ids, x, first, last):
     rows = x.shape[0]
-    count = len(parts)
-    depth, width = parts[0].shape
-    units = count * (depth // 3)
+    depth, width = first[0].shape
+    hidden = depth // 3
+    early, late = len(first), len(last)
+    smem = pl.BlockSpec(memory_space=pltpu.SMEM)
     vmem = pl.BlockSpec(memory_space=pltpu.VMEM)
-    return pl.pallas_call(
-        functools.partial(ffn_kernel, count),
-        out_shape=jax.ShapeDtypeStruct((rows, width), dtype),
-        in_specs=[pl.BlockSpec(memory_space=pltpu.SMEM)]
-        + [pl.BlockSpec(memory_space=pl.ANY)] * (1 + count)
-        + [vmem] * len(sums),
+    whole = pl.BlockSpec(memory_space=pl.ANY)
+    units = pl.pallas_call(
+        early_kernel,
+        out_shape=jax.ShapeDtypeStruct((early * hidden, rows), BF16),
+        in_specs=[smem] + [whole] * (1 + early),
         out_specs=vmem,
         scratch_shapes=[
             pltpu.VMEM(x.shape, BF16),
-            pltpu.VMEM((count, depth, width), BF16),
-            pltpu.VMEM((units, rows), BF16),
-            pltpu.VMEM((units, width), BF16),
-            pltpu.SemaphoreType.DMA((count + 1,)),
+            pltpu.VMEM((early, 2 * hidden, width), BF16),
+            pltpu.SemaphoreType.DMA((early + 1,)),
         ],
         compiler_params=pltpu.CompilerParams(vmem_limit_bytes=30 << 20),
         cost_estimate=pl.CostEstimate(
-            flops=16 * rows * width * depth * count,
-            bytes_accessed=16 * width * depth * count,
+            flops=16 * rows * width * depth * early,
+            bytes_accessed=16 * width * depth * early,
             transcendentals=0,
         ),
-    )(ids, x, *parts, *sums)
+    )(ids[:early], x, *first)
+    return pl.pallas_call(
+        functools.partial(late_kernel, late),
+        out_shape=jax.ShapeDtypeStruct((rows, width), BF16),
+        in_specs=[smem, whole, vmem] + [whole] * (early + late),
+        out_specs=vmem,
+        scratch_shapes=[
+            pltpu.VMEM(x.shape, BF16),
+            pltpu.VMEM((late, 2 * hidden, width), BF16),
+            pltpu.VMEM(((early + late) * hidden, rows), BF16),
+            pltpu.VMEM(((early + late) * hidden, width), BF16),
+            pltpu.SemaphoreType.DMA((1 + early + 2 * late,)),
+        ],
+        compiler_params=pltpu.CompilerParams(vmem_limit_bytes=30 << 20),
+        cost_estimate=pl.CostEstimate(
+            flops=4 * rows * width * depth * late,
+            bytes_accessed=2 * width * depth * (early + late),
+            transcendentals=0,
+        ),
+    )(ids[early:], x, units, *first, *last)
 
 
 def body(
@@ -227,8 +284,7 @@
     rows_in = exchange(copies, "y").reshape(Y * Z * own_rows, width + HD)
     near = (tp + jnp.array([0, TP - 1, 1, 2], jnp.int32)) % TP
     ids = jnp.concatenate([pool * TP + near, (1 - pool) * TP + near]).astype(jnp.int32)
-    mixed = ffn(ids[:3], rows_in, early, [], F32)
-    mixed = ffn(ids[3:], rows_in, late, [mixed], BF16)
+    mixed = ffn(ids, rows_in, early, late)
 
     mixed = exchange(mixed.reshape(Y, Z * own_rows, width), "y")
     mixed = jnp.sum(mixed.astype(F32), axis=0).astype(BF16)

time: 204 us -> 203 us (level)
  Pallas kernels: 15.9 us -> 13.5 us
    pallas_call x2, Pallas kernels: 14.4 us -> 11.9 us  [the longest x1 8.21 us: ffn(): pl.pallas_call(functools.partial(late_kernel, late), out_shape=jax.ShapeD...]
  transfers between devices with their start and end apart: 11 -> 11, of which waited for: 2 -> 3; matrix products, arithmetic and copies ran while one was open for 4% -> 4% of each run, Pallas kernels for 4% -> 3%
where the time goes in v9:
time: 203 us; the launch traced here: 202 us
  blocking collectives  118 us (58%)
  starting transfers between devices  50.2 us (25%)
  Pallas kernels  13.5 us (7%)
  local copies, waits for them, and re-layouts  7.6 us (4%)
  waiting for transfers between devices  6.53 us (3%)
  other arithmetic  5.22 us (3%)
    all_to_all x4, blocking collectives, exchange(): return lax.all_to_all(x, axis, split_axis=0, concat_axis=0, tiled=True)  83.6 us
    all_gather x1, blocking collectives, body(): lax.all_gather(jnp.concatenate([key_proj, value_proj], 1), 'z', axis=0, t...  34.4 us
    all_to_all x4, starting transfers between devices, exchange(): return lax.all_to_all(x, axis, split_axis=0, concat_axis=0, tiled=True)  24.3 us
    ppermute x4, starting transfers between devices, swap(): return lax.ppermute(x, 'pool', [(0, 1), (1, 0)])  15.4 us
    ppermute x3, starting transfers between devices, shift(): return lax.ppermute(x, axis, [(i, (i + count) % size) for i in range(size)])  10.4 us
    pallas_call x1, Pallas kernels, ffn(): pl.pallas_call(functools.partial(late_kernel, late), out_shape=jax.ShapeD...  8.21 us
    all_to_all x4, waiting for transfers between devices, exchange(): return lax.all_to_all(x, axis, split_axis=0, concat_axis=0, tiled=True)  5.81 us
  transfers between devices with their start and end apart: 11, of which 3 were waited for; matrix products, arithmetic and copies ran while one was open for 4% of the time, Pallas kernels for 3%

profile of v9, /device:TPU:1, one launch (start us, length us, event | category | flops | bytes accessed | tf_op | source)
XLA Modules:
  0.0 201.6 jit_solution(16186187195576394019)
XLA Ops:
  0.0 1.6 fusion.5.refs_0_
  1.7 5.2 %collective-permute-start.1 = (bf16[336,2560]{1,0:T(8,128)(2,1)S(1)}, bf16[336,2560]{1,0:T(8,128)(2,1)}, u32[]{:S(2)}, u32[]{:S(2)}) collective-permute-start(bf16[336,2560]{1,0:T(8,128)(2,1)S(1)} %fusion.5.refs_0_), channel_id=1, source_target_pairs={{0,3},{1,0},{2,1},{3,2},{4,7},{5,4},{6,5},{7,6},{8,11},{9,8},{10,9... | collective-permute-start | bytes 5160968 | tf_op jit(solution)/shard_map/ppermute | solution.py:31
  6.9 1.9 collective-permute-start
  8.8 0.6 broadcast_in_dim.8
  9.4 4.2 %all-to-all-start = ((bf16[4,32,256]{2,1,0:T(8,128)(2,1)}), bf16[4,32,256]{2,1,0:T(8,128)(2,1)}, u32[]{:S(2)}, u32[]{:S(2)}) async-start(bf16[4,32,256]{2,1,0:T(8,128)(2,1)} %broadcast_in_dim.8), calls=%async_computation | async-start | bytes 131072 | tf_op jit(solution)/shard_map/all_to_all | solution.py:39
  13.7 0.7 copy.35
  14.4 34.4 %all_gather.3.kv_ref = bf16[512,512]{1,0:T(8,128)(2,1)S(1)} all-gather(bf16[32,512]{1,0:T(8,128)(2,1)S(1)} %pad_maximum_fusion), channel_id=1, replica_groups=mesh['pool'=2,'y'=4,'z'=16,'tp'=4] {'z'}, dimensions={0}, use_global_device_ids=true | all-gather | bytes 557056 | tf_op jit(solution)/shard_map/all_gather | solution.py:241
  48.8 1.3 reduce-precision_convert_fusion
  50.1 1.5 shard_map.118
  51.6 0.6 copy-done.1
  52.3 4.2 %all-to-all-start.1 = ((bf16[4,32,384]{2,1,0:T(8,128)(2,1)}), bf16[4,32,384]{2,1,0:T(8,128)(2,1)S(1)}, u32[]{:S(2)}, u32[]{:S(2)}) async-start(bf16[4,32,384]{2,1,0:T(8,128)(2,1)} %bitcast.17), calls=%async_computation.1 | async-start | bytes 196608 | tf_op jit(solution)/shard_map/all_to_all | solution.py:39
  56.5 0.7 constant_dynamic-slice_fusion.1
  57.3 0.1 copy.34
  57.4 3.8 %all-to-all-done.1 = bf16[4,32,384]{2,1,0:T(8,128)(2,1)S(1)} async-done(((bf16[4,32,384]{2,1,0:T(8,128)(2,1)}), bf16[4,32,384]{2,1,0:T(8,128)(2,1)S(1)}, u32[]{:S(2)}, u32[]{:S(2)}) %all-to-all-start.1) | async-done | bytes 98336 | tf_op jit(solution)/shard_map/all_to_all | solution.py:39
  61.2 0.2 slice_reduce_fusion.1
  61.4 0.1 fusion.7
  61.5 0.1 divide_convert_fusion.1
  61.6 0.1 divide_convert_fusion
  61.7 0.3 convolution_convert_fusion
  62.0 0.8 reshape.99
  62.8 11.5 %all-to-all-start.2 = ((bf16[8,4,2560]{2,1,0:T(4,128)(2,1)}), bf16[8,4,2560]{2,1,0:T(4,128)(2,1)S(1)}, u32[]{:S(2)}, u32[]{:S(2)}) async-start(bf16[8,4,2560]{2,1,0:T(4,128)(2,1)} %reshape.99), calls=%async_computation.2 | async-start | bytes 327680 | tf_op jit(solution)/shard_map/all_to_all | solution.py:39
  74.3 0.1 fusion.16
  74.3 0.1 slice_reduce_fusion.3
  74.4 3.3 %collective-permute-start.2 = (bf16[336,2560]{1,0:T(8,128)(2,1)}, bf16[336,2560]{1,0:T(8,128)(2,1)}, u32[]{:S(2)}, u32[]{:S(2)}) collective-permute-start(bf16[336,2560]{1,0:T(8,128)(2,1)} %collective-permute-done.refs_1_), channel_id=1, source_target_pairs={{0,1},{1,2},{2,3},{3,0},{4,5},{5,6},{6,7},{7,4},{8,9},{9,10},{10,1... | collective-permute-start | bytes 5160968 | tf_op jit(solution)/shard_map/ppermute | solution.py:31
  77.7 2.0 all-to-all-done.2
  79.8 0.1 convert_reduce_fusion.1
  79.8 0.9 fusion.19
  80.8 0.1 add_convert_fusion.1
  80.9 0.1 broadcast_in_dim.9
  81.0 22.1 %all_to_all.40 = bf16[16,4,2688]{2,1,0:T(4,128)(2,1)S(1)} all-to-all(bf16[16,4,2688]{2,1,0:T(4,128)(2,1)S(1)} %broadcast_in_dim.9), channel_id=1, replica_groups=mesh['pool'=2,'y'=4,'z'=16,'tp'=4] {'z'}, dimensions={0} | all-to-all | bytes 688128 | tf_op jit(solution)/shard_map/all_to_all | solution.py:39
  103.1 0.8 broadcast_in_dim.10
  103.9 2.2 %broadcast_in_dim.11 = bf16[4,64,2688]{2,1,0:T(8,128)(2,1)} broadcast(bf16[64,2688]{1,0:T(8,128)(2,1)} %broadcast_in_dim.10), dimensions={1,2} | broadcast | bytes 1720320 | tf_op jit(solution)/shard_map/broadcast_in_dim | solution.py:22
  106.1 4.4 %all-to-all-start.4 = ((bf16[4,64,2688]{2,1,0:T(8,128)(2,1)}), bf16[4,64,2688]{2,1,0:T(8,128)(2,1)}, u32[]{:S(2)}, u32[]{:S(2)}) async-start(bf16[4,64,2688]{2,1,0:T(8,128)(2,1)} %broadcast_in_dim.11), calls=%async_computation.4 | async-start | bytes 2752512 | tf_op jit(solution)/shard_map/all_to_all | solution.py:39
  110.5 9.2 %collective-permute-start.3 = (bf16[336,2560]{1,0:T(8,128)(2,1)S(1)}, bf16[336,2560]{1,0:T(8,128)(2,1)}, u32[]{:S(2)}, u32[]{:S(2)}) collective-permute-start(bf16[336,2560]{1,0:T(8,128)(2,1)S(1)} %fusion.5.refs_0_), channel_id=1, source_target_pairs={{0,256},{256,0},{1,257},{257,1},{2,258},{258,2},{3,259},{259,3},{4... | collective-permute-start | bytes 5160968 | tf_op jit(solution)/shard_map/ppermute | solution.py:35
  119.7 1.9 collective-permute-start.4
  121.6 2.4 %collective-permute-start.5 = (bf16[336,2560]{1,0:T(8,128)(2,1)}, bf16[336,2560]{1,0:T(8,128)(2,1)}, u32[]{:S(2)}, u32[]{:S(2)}) collective-permute-start(bf16[336,2560]{1,0:T(8,128)(2,1)} %collective-permute-done.1.refs_2_), channel_id=1, source_target_pairs={{0,256},{256,0},{1,257},{257,1},{2,258},{258,2},{3,259},{259,3},{4... | collective-permute-start | bytes 5160968 | tf_op jit(solution)/shard_map/ppermute | solution.py:35
  124.0 1.9 collective-permute-start.6
  126.2 3.7 %shard_map.119.units_ref = bf16[336,256]{1,0:T(8,128)(2,1)S(1)} custom-call(s32[3]{0:T(128)S(1)} %bitcast.18, bf16[256,2688]{1,0:T(8,128)(2,1)} %bitcast.7.x_hbm, bf16[336,2560]{1,0:T(8,128)(2,1)S(1)} %fusion.5.refs_0_, bf16[336,2560]{1,0:T(8,128)(2,1)} %collective-permute-done.refs_1_, bf16[336,2560]{1,0:T(8,128)(2,1)} %collective-permute-done.1.refs_2_), custom_call_target="tpu_custom_call" | custom-call | flops 10569646080 | bytes 41287680 | tf_op jit(solution)/shard_map/pallas_call | solution.py:178
  129.9 0.7 collective-permute-done.6.refs_7_
  130.6 8.2 %shard_map.120 = bf16[256,2560]{1,0:T(8,128)(2,1)S(1)} custom-call(s32[5]{0:T(128)S(1)} %slice.36.ids_ref, bf16[256,2688]{1,0:T(8,128)(2,1)} %bitcast.7.x_hbm, bf16[336,256]{1,0:T(8,128)(2,1)S(1)} %shard_map.119.units_ref, bf16[336,2560]{1,0:T(8,128)(2,1)S(1)} %fusion.5.refs_0_, bf16[336,2560]{1,0:T(8,128)(2,1)} %collective-permute-done.refs_1_, ...), custom_call_target="tpu_custom_call" | custom-call | flops 4404019200 | bytes 13762560 | tf_op jit(solution)/shard_map/pallas_call | solution.py:195
  138.9 20.4 %all_to_all.41 = bf16[4,64,2560]{2,1,0:T(8,128)(2,1)S(1)} all-to-all(bf16[4,64,2560]{2,1,0:T(8,128)(2,1)S(1)} %bitcast.16), channel_id=1, replica_groups=mesh['pool'=2,'y'=4,'z'=16,'tp'=4] {'y'}, dimensions={0} | all-to-all | bytes 2621440 | tf_op jit(solution)/shard_map/all_to_all | solution.py:39
  159.3 0.2 reduce_sum.111
  159.5 0.1 reshape.102
  159.6 25.6 %all_to_all.42 = bf16[16,4,2560]{2,1,0:T(4,128)(2,1)S(1)} all-to-all(bf16[16,4,2560]{2,1,0:T(4,128)(2,1)S(1)} %reshape.102), channel_id=1, replica_groups=mesh['pool'=2,'y'=4,'z'=16,'tp'=4] {'z'}, dimensions={0} | all-to-all | bytes 655360 | tf_op jit(solution)/shard_map/all_to_all | solution.py:39
  185.2 0.1 convert_reduce_fusion
  185.3 0.1 reshape.103
  185.5 15.6 %all_to_all.43 = bf16[8,4,320]{2,1,0:T(4,128)(2,1)S(1)} all-to-all(bf16[8,4,320]{2,1,0:T(4,128)(2,1)S(1)} %bitcast.22), channel_id=1, replica_groups=mesh['pool'=2,'y'=4,'z'=16,'tp'=4] {'pool','tp'}, dimensions={0} | all-to-all | bytes 40960 | tf_op jit(solution)/shard_map/all_to_all | solution.py:39
  201.0 0.6 reshape.104
  (42 shorter events, 0.4 us)
Async XLA Ops:
  0.0 61.7 %copy-start = (bf16[256,2560]{1,0:T(8,128)(2,1)S(1)}, bf16[256,2560]{1,0:T(8,128)(2,1)}, u32[]{:S(2)}) copy-start(bf16[256,2560]{1,0:T(8,128)(2,1)} %param.16) | copy-start | bytes 3932164
  0.0 8.8 %copy-start.3 = (bf16[32,256]{1,0:T(8,128)(2,1)S(1)}, bf16[32,256]{1,0:T(8,128)(2,1)}, u32[]{:S(2)}) copy-start(bf16[32,256]{1,0:T(8,128)(2,1)} %param.13) | copy-start | bytes 49156
  0.0 13.6 %copy-start.8 = (f32[32,2]{0,1:T(2,128)S(1)}, f32[32,2]{0,1:T(2,128)}, u32[]{:S(2)}) copy-start(f32[32,2]{0,1:T(2,128)} %param.19) | copy-start | bytes 772
  0.0 14.4 %copy-start.4 = (bf16[32,256]{1,0:T(8,128)(2,1)S(1)}, bf16[32,256]{1,0:T(8,128)(2,1)}, u32[]{:S(2)}) copy-start(bf16[32,256]{1,0:T(8,128)(2,1)} %param.15) | copy-start | bytes 49156
  0.0 14.4 %copy-start.5 = (bf16[32,256]{1,0:T(8,128)(2,1)S(1)}, bf16[32,256]{1,0:T(8,128)(2,1)}, u32[]{:S(2)}) copy-start(bf16[32,256]{1,0:T(8,128)(2,1)} %param.14) | copy-start | bytes 49156
  1.7 50.6 %collective-permute-start.1 = (bf16[336,2560]{1,0:T(8,128)(2,1)S(1)}, bf16[336,2560]{1,0:T(8,128)(2,1)}, u32[]{:S(2)}, u32[]{:S(2)}) collective-permute-start(bf16[336,2560]{1,0:T(8,128)(2,1)S(1)} %fusion.5.refs_0_), channel_id=1, source_target_pairs={{0,3},{1,0},{2,1},{3,2},{4,7},{5,4},{6,5},{7,6},{8,11},{9,8},{10,9... | collective-permute-start | bytes 5160968 | tf_op jit(solution)/shard_map/ppermute | solution.py:31
  6.9 45.4 %collective-permute-start = (bf16[336,2560]{1,0:T(8,128)(2,1)S(1)}, bf16[336,2560]{1,0:T(8,128)(2,1)}, u32[]{:S(2)}, u32[]{:S(2)}) collective-permute-start(bf16[336,2560]{1,0:T(8,128)(2,1)S(1)} %fusion.5.refs_0_), channel_id=1, source_target_pairs={{0,1},{1,2},{2,3},{3,0},{4,5},{5,6},{6,7},{7,4},{8,9},{9,10},{10,1... | collective-permute-start | bytes 5160968 | tf_op jit(solution)/shard_map/ppermute | solution.py:31
  9.4 40.7 %all-to-all-start = ((bf16[4,32,256]{2,1,0:T(8,128)(2,1)}), bf16[4,32,256]{2,1,0:T(8,128)(2,1)}, u32[]{:S(2)}, u32[]{:S(2)}) async-start(bf16[4,32,256]{2,1,0:T(8,128)(2,1)} %broadcast_in_dim.8), calls=%async_computation | async-start | bytes 131072 | tf_op jit(solution)/shard_map/all_to_all | solution.py:39
  51.6 0.6 copy-start.1
  52.3 22.0 %copy-start.6 = (bf16[4,2]{1,0:T(4,128)(2,1)S(1)}, bf16[4,2]{1,0:T(4,128)(2,1)}, u32[]{:S(2)}) copy-start(bf16[4,2]{1,0:T(4,128)(2,1)} %get-tuple-element.38) | copy-start | bytes 52
  52.3 22.0 %copy-start.7 = (bf16[4,2]{1,0:T(4,128)(2,1)S(1)}, bf16[4,2]{1,0:T(4,128)(2,1)}, u32[]{:S(2)}) copy-start(bf16[4,2]{1,0:T(4,128)(2,1)} %get-tuple-element.39) | copy-start | bytes 52
  52.3 22.0 %copy-start.2 = (f32[4,2560]{1,0:T(4,128)S(1)}, f32[4,2560]{1,0:T(4,128)}, u32[]{:S(2)}) copy-start(f32[4,2560]{1,0:T(4,128)} %param.17) | copy-start | bytes 122884
  52.3 8.9 %all-to-all-start.1 = ((bf16[4,32,384]{2,1,0:T(8,128)(2,1)}), bf16[4,32,384]{2,1,0:T(8,128)(2,1)S(1)}, u32[]{:S(2)}, u32[]{:S(2)}) async-start(bf16[4,32,384]{2,1,0:T(8,128)(2,1)} %bitcast.17), calls=%async_computation.1 | async-start | bytes 196608 | tf_op jit(solution)/shard_map/all_to_all | solution.py:39
  62.8 17.0 %all-to-all-start.2 = ((bf16[8,4,2560]{2,1,0:T(4,128)(2,1)}), bf16[8,4,2560]{2,1,0:T(4,128)(2,1)S(1)}, u32[]{:S(2)}, u32[]{:S(2)}) async-start(bf16[8,4,2560]{2,1,0:T(4,128)(2,1)} %reshape.99), calls=%async_computation.2 | async-start | bytes 327680 | tf_op jit(solution)/shard_map/all_to_all | solution.py:39
  74.4 49.6 %collective-permute-start.2 = (bf16[336,2560]{1,0:T(8,128)(2,1)}, bf16[336,2560]{1,0:T(8,128)(2,1)}, u32[]{:S(2)}, u32[]{:S(2)}) collective-permute-start(bf16[336,2560]{1,0:T(8,128)(2,1)} %collective-permute-done.refs_1_), channel_id=1, source_target_pairs={{0,1},{1,2},{2,3},{3,0},{4,5},{5,6},{6,7},{7,4},{8,9},{9,10},{10,1... | collective-permute-start | bytes 5160968 | tf_op jit(solution)/shard_map/ppermute | solution.py:31
  106.1 19.9 %copy-start.9 = (s32[4]{0:T(128)S(1)}, s32[4]{0:T(128)}, u32[]{:S(2)}) copy-start(s32[4]{0:T(128)} %constant.47.clone) | copy-start | bytes 52
  106.1 20.1 %all-to-all-start.4 = ((bf16[4,64,2688]{2,1,0:T(8,128)(2,1)}), bf16[4,64,2688]{2,1,0:T(8,128)(2,1)}, u32[]{:S(2)}, u32[]{:S(2)}) async-start(bf16[4,64,2688]{2,1,0:T(8,128)(2,1)} %broadcast_in_dim.11), calls=%async_computation.4 | async-start | bytes 2752512 | tf_op jit(solution)/shard_map/all_to_all | solution.py:39
  110.5 19.4 %collective-permute-start.3 = (bf16[336,2560]{1,0:T(8,128)(2,1)S(1)}, bf16[336,2560]{1,0:T(8,128)(2,1)}, u32[]{:S(2)}, u32[]{:S(2)}) collective-permute-start(bf16[336,2560]{1,0:T(8,128)(2,1)S(1)} %fusion.5.refs_0_), channel_id=1, source_target_pairs={{0,256},{256,0},{1,257},{257,1},{2,258},{258,2},{3,259},{259,3},{4... | collective-permute-start | bytes 5160968 | tf_op jit(solution)/shard_map/ppermute | solution.py:35
  119.7 10.2 %collective-permute-start.4 = (bf16[336,2560]{1,0:T(8,128)(2,1)}, bf16[336,2560]{1,0:T(8,128)(2,1)}, u32[]{:S(2)}, u32[]{:S(2)}) collective-permute-start(bf16[336,2560]{1,0:T(8,128)(2,1)} %collective-permute-done.refs_1_), channel_id=1, source_target_pairs={{0,256},{256,0},{1,257},{257,1},{2,258},{258,2},{3,259},{259,3},{4... | collective-permute-start | bytes 5160968 | tf_op jit(solution)/shard_map/ppermute | solution.py:35
  121.6 8.3 %collective-permute-start.5 = (bf16[336,2560]{1,0:T(8,128)(2,1)}, bf16[336,2560]{1,0:T(8,128)(2,1)}, u32[]{:S(2)}, u32[]{:S(2)}) collective-permute-start(bf16[336,2560]{1,0:T(8,128)(2,1)} %collective-permute-done.1.refs_2_), channel_id=1, source_target_pairs={{0,256},{256,0},{1,257},{257,1},{2,258},{258,2},{3,259},{259,3},{4... | collective-permute-start | bytes 5160968 | tf_op jit(solution)/shard_map/ppermute | solution.py:35
  124.0 6.6 %collective-permute-start.6 = (bf16[336,2560]{1,0:T(8,128)(2,1)}, bf16[336,2560]{1,0:T(8,128)(2,1)}, u32[]{:S(2)}, u32[]{:S(2)}) collective-permute-start(bf16[336,2560]{1,0:T(8,128)(2,1)} %collective-permute-done.2.refs_3_), channel_id=1, source_target_pairs={{0,256},{256,0},{1,257},{257,1},{2,258},{258,2},{3,259},{259,3},{4... | collective-permute-start | bytes 5160968 | tf_op jit(solution)/shard_map/ppermute | solution.py:35

commit v10 on v9

--- a/solution.py
+++ b/solution.py
@@ -100,11 +100,11 @@
     return jnp.concatenate(acts, 0)
 
 
-def early_kernel(ids_ref, x_hbm, *refs):
-    o_ref, x_ref, w_ref, sems = refs[-4:]
-    parts = refs[:-4]
+def early_kernel(ids_ref, x_ref, *refs):
+    o_ref, w_ref, sems = refs[-3:]
+    parts = refs[:-3]
     width = w_ref.shape[2]
-    copies = [pltpu.make_async_copy(x_hbm, x_ref, sems.at[len(parts)])]
+    copies = []
     for i, part in enumerate(parts):
         copies.append(
             pltpu.make_async_copy(part.at[pl.ds(0, w_ref.shape[1])], w_ref.at[i], sems.at[i])
@@ -121,18 +121,16 @@
     )
 
 
-def late_kernel(count, ids_ref, x_hbm, units_ref, *refs):
-    o_ref, x_ref, w_ref, act_ref, down_ref, sems = refs[-6:]
-    parts = refs[:-6]
+def late_kernel(count, ids_ref, x_ref, units_ref, *refs):
+    o_ref, w_ref, act_ref, down_ref, sems = refs[-5:]
+    parts = refs[:-5]
     width = w_ref.shape[2]
     hidden = w_ref.shape[1] // 2
     early = len(parts) - count
-    x_copy = pltpu.make_async_copy(x_hbm, x_ref, sems.at[0])
-    x_copy.start()
     wide = []
     for i, part in enumerate(parts[early:]):
         wide.append(
-            pltpu.make_async_copy(part.at[pl.ds(0, 2 * hidden)], w_ref.at[i], sems.at[1 + i])
+            pltpu.make_async_copy(part.at[pl.ds(0, 2 * hidden)], w_ref.at[i], sems.at[i])
         )
         wide[i].start()
     tall = []
@@ -141,12 +139,11 @@
             pltpu.make_async_copy(
                 part.at[pl.ds(2 * hidden, hidden)],
                 down_ref.at[pl.ds(i * hidden, hidden)],
-                sems.at[1 + count + i],
+                sems.at[count + i],
             )
         )
         tall[i].start()
     act_ref[: early * hidden] = units_ref[...]
-    x_copy.wait()
     x = x_ref[:, :width]
     route = x_ref[:, width:].astype(F32).T
     each = 3
@@ -178,12 +175,11 @@
     units = pl.pallas_call(
         early_kernel,
         out_shape=jax.ShapeDtypeStruct((early * hidden, rows), BF16),
-        in_specs=[smem] + [whole] * (1 + early),
+        in_specs=[smem, vmem] + [whole] * early,
         out_specs=vmem,
         scratch_shapes=[
-            pltpu.VMEM(x.shape, BF16),
             pltpu.VMEM((early, 2 * hidden, width), BF16),
-            pltpu.SemaphoreType.DMA((early + 1,)),
+            pltpu.SemaphoreType.DMA((early,)),
         ],
         compiler_params=pltpu.CompilerParams(vmem_limit_bytes=30 << 20),
         cost_estimate=pl.CostEstimate(
@@ -195,14 +191,13 @@
     return pl.pallas_call(
         functools.partial(late_kernel, late),
         out_shape=jax.ShapeDtypeStruct((rows, width), BF16),
-        in_specs=[smem, whole, vmem] + [whole] * (early + late),
+        in_specs=[smem, vmem, vmem] + [whole] * (early + late),
         out_specs=vmem,
         scratch_shapes=[
-            pltpu.VMEM(x.shape, BF16),
             pltpu.VMEM((late, 2 * hidden, width), BF16),
             pltpu.VMEM(((early + late) * hidden, rows), BF16),
             pltpu.VMEM(((early + late) * hidden, width), BF16),
-            pltpu.SemaphoreType.DMA((1 + early + 2 * late,)),
+            pltpu.SemaphoreType.DMA((early + 2 * late,)),
         ],
         compiler_params=pltpu.CompilerParams(vmem_limit_bytes=30 << 20),
         cost_estimate=pl.CostEstimate(

time: 203 us -> 204 us (level)
  no operation moved by 1% of the time
where the time goes in v10:
time: 204 us; the launch traced here: 203 us
  blocking collectives  119 us (58%)
  starting transfers between devices  50.2 us (25%)
  Pallas kernels  14.4 us (7%)
  local copies, waits for them, and re-layouts  7.6 us (4%)
  waiting for transfers between devices  5.97 us (3%)
  other arithmetic  5.22 us (3%)
    all_to_all x4, blocking collectives, exchange(): return lax.all_to_all(x, axis, split_axis=0, concat_axis=0, tiled=True)  84.2 us
    all_gather x1, blocking collectives, body(): lax.all_gather(jnp.concatenate([key_proj, value_proj], 1), 'z', axis=0, t...  34.4 us
    all_to_all x4, starting transfers between devices, exchange(): return lax.all_to_all(x, axis, split_axis=0, concat_axis=0, tiled=True)  24.3 us
    ppermute x4, starting transfers between devices, swap(): return lax.ppermute(x, 'pool', [(0, 1), (1, 0)])  15.4 us
    ppermute x3, starting transfers between devices, shift(): return lax.ppermute(x, axis, [(i, (i + count) % size) for i in range(size)])  10.4 us
    pallas_call x1, Pallas kernels, ffn(): pl.pallas_call(functools.partial(late_kernel, late), out_shape=jax.ShapeD...  8.59 us
    all_to_all x4, waiting for transfers between devices, exchange(): return lax.all_to_all(x, axis, split_axis=0, concat_axis=0, tiled=True)  5.81 us
    pallas_call x1, Pallas kernels, ffn(): pl.pallas_call(early_kernel, out_shape=jax.ShapeDtypeStruct((early * hidd...  4.27 us
  transfers between devices with their start and end apart: 11, of which 3 were waited for; matrix products, arithmetic and copies ran while one was open for 4% of the time, Pallas kernels for 3%

profile of v10, /device:TPU:1, one launch (start us, length us, event | category | flops | bytes accessed | tf_op | source)
XLA Modules:
  0.0 202.6 jit_solution(6276021654436007642)
XLA Ops:
  0.0 1.6 fusion.5.refs_0_
  1.7 5.2 %collective-permute-start.1 = (bf16[336,2560]{1,0:T(8,128)(2,1)S(1)}, bf16[336,2560]{1,0:T(8,128)(2,1)}, u32[]{:S(2)}, u32[]{:S(2)}) collective-permute-start(bf16[336,2560]{1,0:T(8,128)(2,1)S(1)} %fusion.5.refs_0_), channel_id=1, source_target_pairs={{0,3},{1,0},{2,1},{3,2},{4,7},{5,4},{6,5},{7,6},{8,11},{9,8},{10,9... | collective-permute-start | bytes 5160968 | tf_op jit(solution)/shard_map/ppermute | solution.py:31
  6.9 1.9 collective-permute-start
  8.8 0.6 broadcast_in_dim.8
  9.4 4.2 %all-to-all-start = ((bf16[4,32,256]{2,1,0:T(8,128)(2,1)}), bf16[4,32,256]{2,1,0:T(8,128)(2,1)}, u32[]{:S(2)}, u32[]{:S(2)}) async-start(bf16[4,32,256]{2,1,0:T(8,128)(2,1)} %broadcast_in_dim.8), calls=%async_computation | async-start | bytes 131072 | tf_op jit(solution)/shard_map/all_to_all | solution.py:39
  13.7 0.7 copy.35
  14.4 34.4 %all_gather.3.kv_ref = bf16[512,512]{1,0:T(8,128)(2,1)S(1)} all-gather(bf16[32,512]{1,0:T(8,128)(2,1)S(1)} %pad_maximum_fusion), channel_id=1, replica_groups=mesh['pool'=2,'y'=4,'z'=16,'tp'=4] {'z'}, dimensions={0}, use_global_device_ids=true | all-gather | bytes 557056 | tf_op jit(solution)/shard_map/all_gather | solution.py:236
  48.8 1.3 reduce-precision_convert_fusion
  50.1 1.5 shard_map.118
  51.6 0.6 copy-done.1
  52.3 4.2 %all-to-all-start.1 = ((bf16[4,32,384]{2,1,0:T(8,128)(2,1)}), bf16[4,32,384]{2,1,0:T(8,128)(2,1)S(1)}, u32[]{:S(2)}, u32[]{:S(2)}) async-start(bf16[4,32,384]{2,1,0:T(8,128)(2,1)} %bitcast.17), calls=%async_computation.1 | async-start | bytes 196608 | tf_op jit(solution)/shard_map/all_to_all | solution.py:39
  56.5 0.7 constant_dynamic-slice_fusion.1
  57.3 0.1 copy.34
  57.4 3.8 %all-to-all-done.1 = bf16[4,32,384]{2,1,0:T(8,128)(2,1)S(1)} async-done(((bf16[4,32,384]{2,1,0:T(8,128)(2,1)}), bf16[4,32,384]{2,1,0:T(8,128)(2,1)S(1)}, u32[]{:S(2)}, u32[]{:S(2)}) %all-to-all-start.1) | async-done | bytes 98336 | tf_op jit(solution)/shard_map/all_to_all | solution.py:39
  61.2 0.2 slice_reduce_fusion.1
  61.4 0.1 fusion.7
  61.5 0.1 divide_convert_fusion.1
  61.6 0.1 divide_convert_fusion
  61.7 0.3 convolution_convert_fusion
  62.0 0.8 reshape.99
  62.8 11.5 %all-to-all-start.2 = ((bf16[8,4,2560]{2,1,0:T(4,128)(2,1)}), bf16[8,4,2560]{2,1,0:T(4,128)(2,1)S(1)}, u32[]{:S(2)}, u32[]{:S(2)}) async-start(bf16[8,4,2560]{2,1,0:T(4,128)(2,1)} %reshape.99), calls=%async_computation.2 | async-start | bytes 327680 | tf_op jit(solution)/shard_map/all_to_all | solution.py:39
  74.3 0.1 fusion.16
  74.3 0.1 slice_reduce_fusion.3
  74.4 3.3 %collective-permute-start.2 = (bf16[336,2560]{1,0:T(8,128)(2,1)}, bf16[336,2560]{1,0:T(8,128)(2,1)}, u32[]{:S(2)}, u32[]{:S(2)}) collective-permute-start(bf16[336,2560]{1,0:T(8,128)(2,1)} %collective-permute-done.refs_1_), channel_id=1, source_target_pairs={{0,1},{1,2},{2,3},{3,0},{4,5},{5,6},{6,7},{7,4},{8,9},{9,10},{10,1... | collective-permute-start | bytes 5160968 | tf_op jit(solution)/shard_map/ppermute | solution.py:31
  77.7 2.0 all-to-all-done.2
  79.8 0.1 convert_reduce_fusion.1
  79.8 0.9 fusion.19
  80.8 0.1 add_convert_fusion.1
  80.9 0.1 broadcast_in_dim.9
  81.0 22.1 %all_to_all.40 = bf16[16,4,2688]{2,1,0:T(4,128)(2,1)S(1)} all-to-all(bf16[16,4,2688]{2,1,0:T(4,128)(2,1)S(1)} %broadcast_in_dim.9), channel_id=1, replica_groups=mesh['pool'=2,'y'=4,'z'=16,'tp'=4] {'z'}, dimensions={0} | all-to-all | bytes 688128 | tf_op jit(solution)/shard_map/all_to_all | solution.py:39
  103.1 0.8 broadcast_in_dim.10
  103.9 2.2 %broadcast_in_dim.11 = bf16[4,64,2688]{2,1,0:T(8,128)(2,1)} broadcast(bf16[64,2688]{1,0:T(8,128)(2,1)} %broadcast_in_dim.10), dimensions={1,2} | broadcast | bytes 1720320 | tf_op jit(solution)/shard_map/broadcast_in_dim | solution.py:22
  106.1 4.4 %all-to-all-start.4 = ((bf16[4,64,2688]{2,1,0:T(8,128)(2,1)}), bf16[4,64,2688]{2,1,0:T(8,128)(2,1)}, u32[]{:S(2)}, u32[]{:S(2)}) async-start(bf16[4,64,2688]{2,1,0:T(8,128)(2,1)} %broadcast_in_dim.11), calls=%async_computation.4 | async-start | bytes 2752512 | tf_op jit(solution)/shard_map/all_to_all | solution.py:39
  110.5 9.2 %collective-permute-start.3 = (bf16[336,2560]{1,0:T(8,128)(2,1)S(1)}, bf16[336,2560]{1,0:T(8,128)(2,1)}, u32[]{:S(2)}, u32[]{:S(2)}) collective-permute-start(bf16[336,2560]{1,0:T(8,128)(2,1)S(1)} %fusion.5.refs_0_), channel_id=1, source_target_pairs={{0,256},{256,0},{1,257},{257,1},{2,258},{258,2},{3,259},{259,3},{4... | collective-permute-start | bytes 5160968 | tf_op jit(solution)/shard_map/ppermute | solution.py:35
  119.7 1.9 collective-permute-start.4
  121.6 2.4 %collective-permute-start.5 = (bf16[336,2560]{1,0:T(8,128)(2,1)}, bf16[336,2560]{1,0:T(8,128)(2,1)}, u32[]{:S(2)}, u32[]{:S(2)}) collective-permute-start(bf16[336,2560]{1,0:T(8,128)(2,1)} %collective-permute-done.1.refs_2_), channel_id=1, source_target_pairs={{0,256},{256,0},{1,257},{257,1},{2,258},{258,2},{3,259},{259,3},{4... | collective-permute-start | bytes 5160968 | tf_op jit(solution)/shard_map/ppermute | solution.py:35
  124.0 1.9 collective-permute-start.6
  126.2 4.3 %shard_map.119.units_ref = bf16[336,256]{1,0:T(8,128)(2,1)S(1)} custom-call(s32[3]{0:T(128)S(1)} %bitcast.18, bf16[256,2688]{1,0:T(8,128)(2,1)} %bitcast.7.x_ref, bf16[336,2560]{1,0:T(8,128)(2,1)S(1)} %fusion.5.refs_0_, bf16[336,2560]{1,0:T(8,128)(2,1)} %collective-permute-done.refs_1_, bf16[336,2560]{1,0:T(8,128)(2,1)} %collective-permute-done.1.refs_2_), custom_call_target="tpu_custom_call" | custom-call | flops 10569646080 | bytes 41287680 | tf_op jit(solution)/shard_map/pallas_call | solution.py:175
  130.5 0.1 collective-permute-done.6.refs_7_
  130.6 8.6 %shard_map.120 = bf16[256,2560]{1,0:T(8,128)(2,1)S(1)} custom-call(s32[5]{0:T(128)S(1)} %slice.36.ids_ref, bf16[256,2688]{1,0:T(8,128)(2,1)} %bitcast.7.x_ref, bf16[336,256]{1,0:T(8,128)(2,1)S(1)} %shard_map.119.units_ref, bf16[336,2560]{1,0:T(8,128)(2,1)S(1)} %fusion.5.refs_0_, bf16[336,2560]{1,0:T(8,128)(2,1)} %collective-permute-done.refs_1_, ...), custom_call_target="tpu_custom_call" | custom-call | flops 4404019200 | bytes 13762560 | tf_op jit(solution)/shard_map/pallas_call | solution.py:191
  139.2 19.9 %all_to_all.41 = bf16[4,64,2560]{2,1,0:T(8,128)(2,1)S(1)} all-to-all(bf16[4,64,2560]{2,1,0:T(8,128)(2,1)S(1)} %bitcast.16), channel_id=1, replica_groups=mesh['pool'=2,'y'=4,'z'=16,'tp'=4] {'y'}, dimensions={0} | all-to-all | bytes 2621440 | tf_op jit(solution)/shard_map/all_to_all | solution.py:39
  159.1 0.2 reduce_sum.111
  159.3 0.1 reshape.102
  159.4 26.7 %all_to_all.42 = bf16[16,4,2560]{2,1,0:T(4,128)(2,1)S(1)} all-to-all(bf16[16,4,2560]{2,1,0:T(4,128)(2,1)S(1)} %reshape.102), channel_id=1, replica_groups=mesh['pool'=2,'y'=4,'z'=16,'tp'=4] {'z'}, dimensions={0} | all-to-all | bytes 655360 | tf_op jit(solution)/shard_map/all_to_all | solution.py:39
  186.1 0.1 convert_reduce_fusion
  186.3 0.1 reshape.103
  186.4 15.6 %all_to_all.43 = bf16[8,4,320]{2,1,0:T(4,128)(2,1)S(1)} all-to-all(bf16[8,4,320]{2,1,0:T(4,128)(2,1)S(1)} %bitcast.22), channel_id=1, replica_groups=mesh['pool'=2,'y'=4,'z'=16,'tp'=4] {'pool','tp'}, dimensions={0} | all-to-all | bytes 40960 | tf_op jit(solution)/shard_map/all_to_all | solution.py:39
  202.0 0.6 reshape.104
  (42 shorter events, 0.4 us)
Async XLA Ops:
  0.0 61.7 %copy-start = (bf16[256,2560]{1,0:T(8,128)(2,1)S(1)}, bf16[256,2560]{1,0:T(8,128)(2,1)}, u32[]{:S(2)}) copy-start(bf16[256,2560]{1,0:T(8,128)(2,1)} %param.16) | copy-start | bytes 3932164
  0.0 8.8 %copy-start.3 = (bf16[32,256]{1,0:T(8,128)(2,1)S(1)}, bf16[32,256]{1,0:T(8,128)(2,1)}, u32[]{:S(2)}) copy-start(bf16[32,256]{1,0:T(8,128)(2,1)} %param.13) | copy-start | bytes 49156
  0.0 13.6 %copy-start.8 = (f32[32,2]{0,1:T(2,128)S(1)}, f32[32,2]{0,1:T(2,128)}, u32[]{:S(2)}) copy-start(f32[32,2]{0,1:T(2,128)} %param.19) | copy-start | bytes 772
  0.0 14.4 %copy-start.4 = (bf16[32,256]{1,0:T(8,128)(2,1)S(1)}, bf16[32,256]{1,0:T(8,128)(2,1)}, u32[]{:S(2)}) copy-start(bf16[32,256]{1,0:T(8,128)(2,1)} %param.15) | copy-start | bytes 49156
  0.0 14.4 %copy-start.5 = (bf16[32,256]{1,0:T(8,128)(2,1)S(1)}, bf16[32,256]{1,0:T(8,128)(2,1)}, u32[]{:S(2)}) copy-start(bf16[32,256]{1,0:T(8,128)(2,1)} %param.14) | copy-start | bytes 49156
  1.7 50.6 %collective-permute-start.1 = (bf16[336,2560]{1,0:T(8,128)(2,1)S(1)}, bf16[336,2560]{1,0:T(8,128)(2,1)}, u32[]{:S(2)}, u32[]{:S(2)}) collective-permute-start(bf16[336,2560]{1,0:T(8,128)(2,1)S(1)} %fusion.5.refs_0_), channel_id=1, source_target_pairs={{0,3},{1,0},{2,1},{3,2},{4,7},{5,4},{6,5},{7,6},{8,11},{9,8},{10,9... | collective-permute-start | bytes 5160968 | tf_op jit(solution)/shard_map/ppermute | solution.py:31
  6.9 45.4 %collective-permute-start = (bf16[336,2560]{1,0:T(8,128)(2,1)S(1)}, bf16[336,2560]{1,0:T(8,128)(2,1)}, u32[]{:S(2)}, u32[]{:S(2)}) collective-permute-start(bf16[336,2560]{1,0:T(8,128)(2,1)S(1)} %fusion.5.refs_0_), channel_id=1, source_target_pairs={{0,1},{1,2},{2,3},{3,0},{4,5},{5,6},{6,7},{7,4},{8,9},{9,10},{10,1... | collective-permute-start | bytes 5160968 | tf_op jit(solution)/shard_map/ppermute | solution.py:31
  9.4 40.7 %all-to-all-start = ((bf16[4,32,256]{2,1,0:T(8,128)(2,1)}), bf16[4,32,256]{2,1,0:T(8,128)(2,1)}, u32[]{:S(2)}, u32[]{:S(2)}) async-start(bf16[4,32,256]{2,1,0:T(8,128)(2,1)} %broadcast_in_dim.8), calls=%async_computation | async-start | bytes 131072 | tf_op jit(solution)/shard_map/all_to_all | solution.py:39
  51.6 0.6 copy-start.1
  52.3 22.0 %copy-start.6 = (bf16[4,2]{1,0:T(4,128)(2,1)S(1)}, bf16[4,2]{1,0:T(4,128)(2,1)}, u32[]{:S(2)}) copy-start(bf16[4,2]{1,0:T(4,128)(2,1)} %get-tuple-element.38) | copy-start | bytes 52
  52.3 22.0 %copy-start.7 = (bf16[4,2]{1,0:T(4,128)(2,1)S(1)}, bf16[4,2]{1,0:T(4,128)(2,1)}, u32[]{:S(2)}) copy-start(bf16[4,2]{1,0:T(4,128)(2,1)} %get-tuple-element.39) | copy-start | bytes 52
  52.3 22.0 %copy-start.2 = (f32[4,2560]{1,0:T(4,128)S(1)}, f32[4,2560]{1,0:T(4,128)}, u32[]{:S(2)}) copy-start(f32[4,2560]{1,0:T(4,128)} %param.17) | copy-start | bytes 122884
  52.3 8.9 %all-to-all-start.1 = ((bf16[4,32,384]{2,1,0:T(8,128)(2,1)}), bf16[4,32,384]{2,1,0:T(8,128)(2,1)S(1)}, u32[]{:S(2)}, u32[]{:S(2)}) async-start(bf16[4,32,384]{2,1,0:T(8,128)(2,1)} %bitcast.17), calls=%async_computation.1 | async-start | bytes 196608 | tf_op jit(solution)/shard_map/all_to_all | solution.py:39
  62.8 17.0 %all-to-all-start.2 = ((bf16[8,4,2560]{2,1,0:T(4,128)(2,1)}), bf16[8,4,2560]{2,1,0:T(4,128)(2,1)S(1)}, u32[]{:S(2)}, u32[]{:S(2)}) async-start(bf16[8,4,2560]{2,1,0:T(4,128)(2,1)} %reshape.99), calls=%async_computation.2 | async-start | bytes 327680 | tf_op jit(solution)/shard_map/all_to_all | solution.py:39
  74.4 49.6 %collective-permute-start.2 = (bf16[336,2560]{1,0:T(8,128)(2,1)}, bf16[336,2560]{1,0:T(8,128)(2,1)}, u32[]{:S(2)}, u32[]{:S(2)}) collective-permute-start(bf16[336,2560]{1,0:T(8,128)(2,1)} %collective-permute-done.refs_1_), channel_id=1, source_target_pairs={{0,1},{1,2},{2,3},{3,0},{4,5},{5,6},{6,7},{7,4},{8,9},{9,10},{10,1... | collective-permute-start | bytes 5160968 | tf_op jit(solution)/shard_map/ppermute | solution.py:31
  106.1 19.9 %copy-start.9 = (s32[4]{0:T(128)S(1)}, s32[4]{0:T(128)}, u32[]{:S(2)}) copy-start(s32[4]{0:T(128)} %constant.47.clone) | copy-start | bytes 52
  106.1 20.1 %all-to-all-start.4 = ((bf16[4,64,2688]{2,1,0:T(8,128)(2,1)}), bf16[4,64,2688]{2,1,0:T(8,128)(2,1)}, u32[]{:S(2)}, u32[]{:S(2)}) async-start(bf16[4,64,2688]{2,1,0:T(8,128)(2,1)} %broadcast_in_dim.11), calls=%async_computation.4 | async-start | bytes 2752512 | tf_op jit(solution)/shard_map/all_to_all | solution.py:39
  110.5 20.0 %collective-permute-start.3 = (bf16[336,2560]{1,0:T(8,128)(2,1)S(1)}, bf16[336,2560]{1,0:T(8,128)(2,1)}, u32[]{:S(2)}, u32[]{:S(2)}) collective-permute-start(bf16[336,2560]{1,0:T(8,128)(2,1)S(1)} %fusion.5.refs_0_), channel_id=1, source_target_pairs={{0,256},{256,0},{1,257},{257,1},{2,258},{258,2},{3,259},{259,3},{4... | collective-permute-start | bytes 5160968 | tf_op jit(solution)/shard_map/ppermute | solution.py:35
  119.7 10.8 %collective-permute-start.4 = (bf16[336,2560]{1,0:T(8,128)(2,1)}, bf16[336,2560]{1,0:T(8,128)(2,1)}, u32[]{:S(2)}, u32[]{:S(2)}) collective-permute-start(bf16[336,2560]{1,0:T(8,128)(2,1)} %collective-permute-done.refs_1_), channel_id=1, source_target_pairs={{0,256},{256,0},{1,257},{257,1},{2,258},{258,2},{3,259},{259,3},{4... | collective-permute-start | bytes 5160968 | tf_op jit(solution)/shard_map/ppermute | solution.py:35
  121.6 8.9 %collective-permute-start.5 = (bf16[336,2560]{1,0:T(8,128)(2,1)}, bf16[336,2560]{1,0:T(8,128)(2,1)}, u32[]{:S(2)}, u32[]{:S(2)}) collective-permute-start(bf16[336,2560]{1,0:T(8,128)(2,1)} %collective-permute-done.1.refs_2_), channel_id=1, source_target_pairs={{0,256},{256,0},{1,257},{257,1},{2,258},{258,2},{3,259},{259,3},{4... | collective-permute-start | bytes 5160968 | tf_op jit(solution)/shard_map/ppermute | solution.py:35
  124.0 6.6 %collective-permute-start.6 = (bf16[336,2560]{1,0:T(8,128)(2,1)}, bf16[336,2560]{1,0:T(8,128)(2,1)}, u32[]{:S(2)}, u32[]{:S(2)}) collective-permute-start(bf16[336,2560]{1,0:T(8,128)(2,1)} %collective-permute-done.2.refs_3_), channel_id=1, source_target_pairs={{0,256},{256,0},{1,257},{257,1},{2,258},{258,2},{3,259},{259,3},{4... | collective-permute-start | bytes 5160968 | tf_op jit(solution)/shard_map/ppermute | solution.py:35

commit v11 on v10

--- a/solution.py
+++ b/solution.py
@@ -146,7 +146,7 @@
     act_ref[: early * hidden] = units_ref[...]
     x = x_ref[:, :width]
     route = x_ref[:, width:].astype(F32).T
-    each = 3
+    each = 5
     for first in range(0, count, each):
         last = min(first + each, count)
         for i in range(first, last):

time: 204 us -> 205 us (level)
  no operation moved by 1% of the time
where the time goes in v11:
time: 205 us; the launch traced here: 204 us
  blocking collectives  119 us (58%)
  starting transfers between devices  50.2 us (24%)
  Pallas kernels  15.8 us (8%)
  local copies, waits for them, and re-layouts  7.6 us (4%)
  waiting for transfers between devices  5.97 us (3%)
  other arithmetic  5.22 us (3%)
    all_to_all x4, blocking collectives, exchange(): return lax.all_to_all(x, axis, split_axis=0, concat_axis=0, tiled=True)  84.2 us
    all_gather x1, blocking collectives, body(): lax.all_gather(jnp.concatenate([key_proj, value_proj], 1), 'z', axis=0, t...  34.4 us
    all_to_all x4, starting transfers between devices, exchange(): return lax.all_to_all(x, axis, split_axis=0, concat_axis=0, tiled=True)  24.3 us
    ppermute x4, starting transfers between devices, swap(): return lax.ppermute(x, 'pool', [(0, 1), (1, 0)])  15.4 us
    ppermute x3, starting transfers between devices, shift(): return lax.ppermute(x, axis, [(i, (i + count) % size) for i in range(size)])  10.4 us
    pallas_call x1, Pallas kernels, ffn(): pl.pallas_call(functools.partial(late_kernel, late), out_shape=jax.ShapeD...  10 us
    all_to_all x4, waiting for transfers between devices, exchange(): return lax.all_to_all(x, axis, split_axis=0, concat_axis=0, tiled=True)  5.81 us
    pallas_call x1, Pallas kernels, ffn(): pl.pallas_call(early_kernel, out_shape=jax.ShapeDtypeStruct((early * hidd...  4.27 us
  transfers between devices with their start and end apart: 11, of which 3 were waited for; matrix products, arithmetic and copies ran while one was open for 4% of the time, Pallas kernels for 3%

profile of v11, /device:TPU:1, one launch (start us, length us, event | category | flops | bytes accessed | tf_op | source)
XLA Modules:
  0.0 204.0 jit_solution(9401202217275096061)
XLA Ops:
  0.0 1.6 fusion.5.refs_0_
  1.7 5.2 %collective-permute-start.1 = (bf16[336,2560]{1,0:T(8,128)(2,1)S(1)}, bf16[336,2560]{1,0:T(8,128)(2,1)}, u32[]{:S(2)}, u32[]{:S(2)}) collective-permute-start(bf16[336,2560]{1,0:T(8,128)(2,1)S(1)} %fusion.5.refs_0_), channel_id=1, source_target_pairs={{0,3},{1,0},{2,1},{3,2},{4,7},{5,4},{6,5},{7,6},{8,11},{9,8},{10,9... | collective-permute-start | bytes 5160968 | tf_op jit(solution)/shard_map/ppermute | solution.py:31
  6.9 1.9 collective-permute-start
  8.8 0.6 broadcast_in_dim.8
  9.4 4.2 %all-to-all-start = ((bf16[4,32,256]{2,1,0:T(8,128)(2,1)}), bf16[4,32,256]{2,1,0:T(8,128)(2,1)}, u32[]{:S(2)}, u32[]{:S(2)}) async-start(bf16[4,32,256]{2,1,0:T(8,128)(2,1)} %broadcast_in_dim.8), calls=%async_computation | async-start | bytes 131072 | tf_op jit(solution)/shard_map/all_to_all | solution.py:39
  13.7 0.7 copy.35
  14.4 34.4 %all_gather.3.kv_ref = bf16[512,512]{1,0:T(8,128)(2,1)S(1)} all-gather(bf16[32,512]{1,0:T(8,128)(2,1)S(1)} %pad_maximum_fusion), channel_id=1, replica_groups=mesh['pool'=2,'y'=4,'z'=16,'tp'=4] {'z'}, dimensions={0}, use_global_device_ids=true | all-gather | bytes 557056 | tf_op jit(solution)/shard_map/all_gather | solution.py:236
  48.8 1.3 reduce-precision_convert_fusion
  50.1 1.5 shard_map.118
  51.6 0.6 copy-done.1
  52.3 4.2 %all-to-all-start.1 = ((bf16[4,32,384]{2,1,0:T(8,128)(2,1)}), bf16[4,32,384]{2,1,0:T(8,128)(2,1)S(1)}, u32[]{:S(2)}, u32[]{:S(2)}) async-start(bf16[4,32,384]{2,1,0:T(8,128)(2,1)} %bitcast.17), calls=%async_computation.1 | async-start | bytes 196608 | tf_op jit(solution)/shard_map/all_to_all | solution.py:39
  56.5 0.7 constant_dynamic-slice_fusion.1
  57.3 0.1 copy.34
  57.4 3.8 %all-to-all-done.1 = bf16[4,32,384]{2,1,0:T(8,128)(2,1)S(1)} async-done(((bf16[4,32,384]{2,1,0:T(8,128)(2,1)}), bf16[4,32,384]{2,1,0:T(8,128)(2,1)S(1)}, u32[]{:S(2)}, u32[]{:S(2)}) %all-to-all-start.1) | async-done | bytes 98336 | tf_op jit(solution)/shard_map/all_to_all | solution.py:39
  61.2 0.2 slice_reduce_fusion.1
  61.4 0.1 fusion.7
  61.5 0.1 divide_convert_fusion.1
  61.6 0.1 divide_convert_fusion
  61.7 0.3 convolution_convert_fusion
  62.0 0.8 reshape.99
  62.8 11.5 %all-to-all-start.2 = ((bf16[8,4,2560]{2,1,0:T(4,128)(2,1)}), bf16[8,4,2560]{2,1,0:T(4,128)(2,1)S(1)}, u32[]{:S(2)}, u32[]{:S(2)}) async-start(bf16[8,4,2560]{2,1,0:T(4,128)(2,1)} %reshape.99), calls=%async_computation.2 | async-start | bytes 327680 | tf_op jit(solution)/shard_map/all_to_all | solution.py:39
  74.3 0.1 fusion.16
  74.3 0.1 slice_reduce_fusion.3
  74.4 3.3 %collective-permute-start.2 = (bf16[336,2560]{1,0:T(8,128)(2,1)}, bf16[336,2560]{1,0:T(8,128)(2,1)}, u32[]{:S(2)}, u32[]{:S(2)}) collective-permute-start(bf16[336,2560]{1,0:T(8,128)(2,1)} %collective-permute-done.refs_1_), channel_id=1, source_target_pairs={{0,1},{1,2},{2,3},{3,0},{4,5},{5,6},{6,7},{7,4},{8,9},{9,10},{10,1... | collective-permute-start | bytes 5160968 | tf_op jit(solution)/shard_map/ppermute | solution.py:31
  77.7 2.0 all-to-all-done.2
  79.8 0.1 convert_reduce_fusion.1
  79.8 0.9 fusion.19
  80.8 0.1 add_convert_fusion.1
  80.9 0.1 broadcast_in_dim.9
  81.0 22.1 %all_to_all.40 = bf16[16,4,2688]{2,1,0:T(4,128)(2,1)S(1)} all-to-all(bf16[16,4,2688]{2,1,0:T(4,128)(2,1)S(1)} %broadcast_in_dim.9), channel_id=1, replica_groups=mesh['pool'=2,'y'=4,'z'=16,'tp'=4] {'z'}, dimensions={0} | all-to-all | bytes 688128 | tf_op jit(solution)/shard_map/all_to_all | solution.py:39
  103.1 0.8 broadcast_in_dim.10
  103.9 2.2 %broadcast_in_dim.11 = bf16[4,64,2688]{2,1,0:T(8,128)(2,1)} broadcast(bf16[64,2688]{1,0:T(8,128)(2,1)} %broadcast_in_dim.10), dimensions={1,2} | broadcast | bytes 1720320 | tf_op jit(solution)/shard_map/broadcast_in_dim | solution.py:22
  106.1 4.4 %all-to-all-start.4 = ((bf16[4,64,2688]{2,1,0:T(8,128)(2,1)}), bf16[4,64,2688]{2,1,0:T(8,128)(2,1)}, u32[]{:S(2)}, u32[]{:S(2)}) async-start(bf16[4,64,2688]{2,1,0:T(8,128)(2,1)} %broadcast_in_dim.11), calls=%async_computation.4 | async-start | bytes 2752512 | tf_op jit(solution)/shard_map/all_to_all | solution.py:39
  110.5 9.2 %collective-permute-start.3 = (bf16[336,2560]{1,0:T(8,128)(2,1)S(1)}, bf16[336,2560]{1,0:T(8,128)(2,1)}, u32[]{:S(2)}, u32[]{:S(2)}) collective-permute-start(bf16[336,2560]{1,0:T(8,128)(2,1)S(1)} %fusion.5.refs_0_), channel_id=1, source_target_pairs={{0,256},{256,0},{1,257},{257,1},{2,258},{258,2},{3,259},{259,3},{4... | collective-permute-start | bytes 5160968 | tf_op jit(solution)/shard_map/ppermute | solution.py:35
  119.7 1.9 collective-permute-start.4
  121.6 2.4 %collective-permute-start.5 = (bf16[336,2560]{1,0:T(8,128)(2,1)}, bf16[336,2560]{1,0:T(8,128)(2,1)}, u32[]{:S(2)}, u32[]{:S(2)}) collective-permute-start(bf16[336,2560]{1,0:T(8,128)(2,1)} %collective-permute-done.1.refs_2_), channel_id=1, source_target_pairs={{0,256},{256,0},{1,257},{257,1},{2,258},{258,2},{3,259},{259,3},{4... | collective-permute-start | bytes 5160968 | tf_op jit(solution)/shard_map/ppermute | solution.py:35
  124.0 1.9 collective-permute-start.6
  126.2 4.3 %shard_map.119.units_ref = bf16[336,256]{1,0:T(8,128)(2,1)S(1)} custom-call(s32[3]{0:T(128)S(1)} %bitcast.18, bf16[256,2688]{1,0:T(8,128)(2,1)} %bitcast.7.x_ref, bf16[336,2560]{1,0:T(8,128)(2,1)S(1)} %fusion.5.refs_0_, bf16[336,2560]{1,0:T(8,128)(2,1)} %collective-permute-done.refs_1_, bf16[336,2560]{1,0:T(8,128)(2,1)} %collective-permute-done.1.refs_2_), custom_call_target="tpu_custom_call" | custom-call | flops 10569646080 | bytes 41287680 | tf_op jit(solution)/shard_map/pallas_call | solution.py:175
  130.5 0.1 collective-permute-done.6.refs_7_
  130.6 10.0 %shard_map.120 = bf16[256,2560]{1,0:T(8,128)(2,1)S(1)} custom-call(s32[5]{0:T(128)S(1)} %slice.36.ids_ref, bf16[256,2688]{1,0:T(8,128)(2,1)} %bitcast.7.x_ref, bf16[336,256]{1,0:T(8,128)(2,1)S(1)} %shard_map.119.units_ref, bf16[336,2560]{1,0:T(8,128)(2,1)S(1)} %fusion.5.refs_0_, bf16[336,2560]{1,0:T(8,128)(2,1)} %collective-permute-done.refs_1_, ...), custom_call_target="tpu_custom_call" | custom-call | flops 4404019200 | bytes 13762560 | tf_op jit(solution)/shard_map/pallas_call | solution.py:191
  140.7 19.9 %all_to_all.41 = bf16[4,64,2560]{2,1,0:T(8,128)(2,1)S(1)} all-to-all(bf16[4,64,2560]{2,1,0:T(8,128)(2,1)S(1)} %bitcast.16), channel_id=1, replica_groups=mesh['pool'=2,'y'=4,'z'=16,'tp'=4] {'y'}, dimensions={0} | all-to-all | bytes 2621440 | tf_op jit(solution)/shard_map/all_to_all | solution.py:39
  160.5 0.2 reduce_sum.111
  160.8 0.1 reshape.102
  160.8 26.7 %all_to_all.42 = bf16[16,4,2560]{2,1,0:T(4,128)(2,1)S(1)} all-to-all(bf16[16,4,2560]{2,1,0:T(4,128)(2,1)S(1)} %reshape.102), channel_id=1, replica_groups=mesh['pool'=2,'y'=4,'z'=16,'tp'=4] {'z'}, dimensions={0} | all-to-all | bytes 655360 | tf_op jit(solution)/shard_map/all_to_all | solution.py:39
  187.5 0.1 convert_reduce_fusion
  187.7 0.1 reshape.103
  187.8 15.6 %all_to_all.43 = bf16[8,4,320]{2,1,0:T(4,128)(2,1)S(1)} all-to-all(bf16[8,4,320]{2,1,0:T(4,128)(2,1)S(1)} %bitcast.22), channel_id=1, replica_groups=mesh['pool'=2,'y'=4,'z'=16,'tp'=4] {'pool','tp'}, dimensions={0} | all-to-all | bytes 40960 | tf_op jit(solution)/shard_map/all_to_all | solution.py:39
  203.4 0.6 reshape.104
  (42 shorter events, 0.4 us)
Async XLA Ops:
  0.0 61.7 %copy-start = (bf16[256,2560]{1,0:T(8,128)(2,1)S(1)}, bf16[256,2560]{1,0:T(8,128)(2,1)}, u32[]{:S(2)}) copy-start(bf16[256,2560]{1,0:T(8,128)(2,1)} %param.16) | copy-start | bytes 3932164
  0.0 8.8 %copy-start.3 = (bf16[32,256]{1,0:T(8,128)(2,1)S(1)}, bf16[32,256]{1,0:T(8,128)(2,1)}, u32[]{:S(2)}) copy-start(bf16[32,256]{1,0:T(8,128)(2,1)} %param.13) | copy-start | bytes 49156
  0.0 13.6 %copy-start.8 = (f32[32,2]{0,1:T(2,128)S(1)}, f32[32,2]{0,1:T(2,128)}, u32[]{:S(2)}) copy-start(f32[32,2]{0,1:T(2,128)} %param.19) | copy-start | bytes 772
  0.0 14.4 %copy-start.4 = (bf16[32,256]{1,0:T(8,128)(2,1)S(1)}, bf16[32,256]{1,0:T(8,128)(2,1)}, u32[]{:S(2)}) copy-start(bf16[32,256]{1,0:T(8,128)(2,1)} %param.15) | copy-start | bytes 49156
  0.0 14.4 %copy-start.5 = (bf16[32,256]{1,0:T(8,128)(2,1)S(1)}, bf16[32,256]{1,0:T(8,128)(2,1)}, u32[]{:S(2)}) copy-start(bf16[32,256]{1,0:T(8,128)(2,1)} %param.14) | copy-start | bytes 49156
  1.7 50.6 %collective-permute-start.1 = (bf16[336,2560]{1,0:T(8,128)(2,1)S(1)}, bf16[336,2560]{1,0:T(8,128)(2,1)}, u32[]{:S(2)}, u32[]{:S(2)}) collective-permute-start(bf16[336,2560]{1,0:T(8,128)(2,1)S(1)} %fusion.5.refs_0_), channel_id=1, source_target_pairs={{0,3},{1,0},{2,1},{3,2},{4,7},{5,4},{6,5},{7,6},{8,11},{9,8},{10,9... | collective-permute-start | bytes 5160968 | tf_op jit(solution)/shard_map/ppermute | solution.py:31
  6.9 45.4 %collective-permute-start = (bf16[336,2560]{1,0:T(8,128)(2,1)S(1)}, bf16[336,2560]{1,0:T(8,128)(2,1)}, u32[]{:S(2)}, u32[]{:S(2)}) collective-permute-start(bf16[336,2560]{1,0:T(8,128)(2,1)S(1)} %fusion.5.refs_0_), channel_id=1, source_target_pairs={{0,1},{1,2},{2,3},{3,0},{4,5},{5,6},{6,7},{7,4},{8,9},{9,10},{10,1... | collective-permute-start | bytes 5160968 | tf_op jit(solution)/shard_map/ppermute | solution.py:31
  9.4 40.7 %all-to-all-start = ((bf16[4,32,256]{2,1,0:T(8,128)(2,1)}), bf16[4,32,256]{2,1,0:T(8,128)(2,1)}, u32[]{:S(2)}, u32[]{:S(2)}) async-start(bf16[4,32,256]{2,1,0:T(8,128)(2,1)} %broadcast_in_dim.8), calls=%async_computation | async-start | bytes 131072 | tf_op jit(solution)/shard_map/all_to_all | solution.py:39
  51.6 0.6 copy-start.1
  52.3 22.0 %copy-start.6 = (bf16[4,2]{1,0:T(4,128)(2,1)S(1)}, bf16[4,2]{1,0:T(4,128)(2,1)}, u32[]{:S(2)}) copy-start(bf16[4,2]{1,0:T(4,128)(2,1)} %get-tuple-element.38) | copy-start | bytes 52
  52.3 22.0 %copy-start.7 = (bf16[4,2]{1,0:T(4,128)(2,1)S(1)}, bf16[4,2]{1,0:T(4,128)(2,1)}, u32[]{:S(2)}) copy-start(bf16[4,2]{1,0:T(4,128)(2,1)} %get-tuple-element.39) | copy-start | bytes 52
  52.3 22.0 %copy-start.2 = (f32[4,2560]{1,0:T(4,128)S(1)}, f32[4,2560]{1,0:T(4,128)}, u32[]{:S(2)}) copy-start(f32[4,2560]{1,0:T(4,128)} %param.17) | copy-start | bytes 122884
  52.3 8.9 %all-to-all-start.1 = ((bf16[4,32,384]{2,1,0:T(8,128)(2,1)}), bf16[4,32,384]{2,1,0:T(8,128)(2,1)S(1)}, u32[]{:S(2)}, u32[]{:S(2)}) async-start(bf16[4,32,384]{2,1,0:T(8,128)(2,1)} %bitcast.17), calls=%async_computation.1 | async-start | bytes 196608 | tf_op jit(solution)/shard_map/all_to_all | solution.py:39
  62.8 17.0 %all-to-all-start.2 = ((bf16[8,4,2560]{2,1,0:T(4,128)(2,1)}), bf16[8,4,2560]{2,1,0:T(4,128)(2,1)S(1)}, u32[]{:S(2)}, u32[]{:S(2)}) async-start(bf16[8,4,2560]{2,1,0:T(4,128)(2,1)} %reshape.99), calls=%async_computation.2 | async-start | bytes 327680 | tf_op jit(solution)/shard_map/all_to_all | solution.py:39
  74.4 49.6 %collective-permute-start.2 = (bf16[336,2560]{1,0:T(8,128)(2,1)}, bf16[336,2560]{1,0:T(8,128)(2,1)}, u32[]{:S(2)}, u32[]{:S(2)}) collective-permute-start(bf16[336,2560]{1,0:T(8,128)(2,1)} %collective-permute-done.refs_1_), channel_id=1, source_target_pairs={{0,1},{1,2},{2,3},{3,0},{4,5},{5,6},{6,7},{7,4},{8,9},{9,10},{10,1... | collective-permute-start | bytes 5160968 | tf_op jit(solution)/shard_map/ppermute | solution.py:31
  106.1 19.9 %copy-start.9 = (s32[4]{0:T(128)S(1)}, s32[4]{0:T(128)}, u32[]{:S(2)}) copy-start(s32[4]{0:T(128)} %constant.47.clone) | copy-start | bytes 52
  106.1 20.1 %all-to-all-start.4 = ((bf16[4,64,2688]{2,1,0:T(8,128)(2,1)}), bf16[4,64,2688]{2,1,0:T(8,128)(2,1)}, u32[]{:S(2)}, u32[]{:S(2)}) async-start(bf16[4,64,2688]{2,1,0:T(8,128)(2,1)} %broadcast_in_dim.11), calls=%async_computation.4 | async-start | bytes 2752512 | tf_op jit(solution)/shard_map/all_to_all | solution.py:39
  110.5 20.0 %collective-permute-start.3 = (bf16[336,2560]{1,0:T(8,128)(2,1)S(1)}, bf16[336,2560]{1,0:T(8,128)(2,1)}, u32[]{:S(2)}, u32[]{:S(2)}) collective-permute-start(bf16[336,2560]{1,0:T(8,128)(2,1)S(1)} %fusion.5.refs_0_), channel_id=1, source_target_pairs={{0,256},{256,0},{1,257},{257,1},{2,258},{258,2},{3,259},{259,3},{4... | collective-permute-start | bytes 5160968 | tf_op jit(solution)/shard_map/ppermute | solution.py:35
  119.7 10.8 %collective-permute-start.4 = (bf16[336,2560]{1,0:T(8,128)(2,1)}, bf16[336,2560]{1,0:T(8,128)(2,1)}, u32[]{:S(2)}, u32[]{:S(2)}) collective-permute-start(bf16[336,2560]{1,0:T(8,128)(2,1)} %collective-permute-done.refs_1_), channel_id=1, source_target_pairs={{0,256},{256,0},{1,257},{257,1},{2,258},{258,2},{3,259},{259,3},{4... | collective-permute-start | bytes 5160968 | tf_op jit(solution)/shard_map/ppermute | solution.py:35
  121.6 8.9 %collective-permute-start.5 = (bf16[336,2560]{1,0:T(8,128)(2,1)}, bf16[336,2560]{1,0:T(8,128)(2,1)}, u32[]{:S(2)}, u32[]{:S(2)}) collective-permute-start(bf16[336,2560]{1,0:T(8,128)(2,1)} %collective-permute-done.1.refs_2_), channel_id=1, source_target_pairs={{0,256},{256,0},{1,257},{257,1},{2,258},{258,2},{3,259},{259,3},{4... | collective-permute-start | bytes 5160968 | tf_op jit(solution)/shard_map/ppermute | solution.py:35
  124.0 6.6 %collective-permute-start.6 = (bf16[336,2560]{1,0:T(8,128)(2,1)}, bf16[336,2560]{1,0:T(8,128)(2,1)}, u32[]{:S(2)}, u32[]{:S(2)}) collective-permute-start(bf16[336,2560]{1,0:T(8,128)(2,1)} %collective-permute-done.2.refs_3_), channel_id=1, source_target_pairs={{0,256},{256,0},{1,257},{257,1},{2,258},{258,2},{3,259},{259,3},{4... | collective-permute-start | bytes 5160968 | tf_op jit(solution)/shard_map/ppermute | solution.py:35
